TPU v7x, 32 devices: a whole 2x2x4 slice. The times are simulated.
32 devices in a mesh: vocab: 8 (over y, x, core), seq: 4 (over z).
Axes of the slice: x: 2, y: 2, z: 4, core: 2. Of those that a mesh axis runs over, the one named last changes fastest.
Arguments:
- hidden_states: bfloat16 [256, 2560], P('seq'), may hold values from -16 to 16
- head_weight: bfloat16 [2560, 75968], P('seq', 'vocab'), may hold values from -3 to 3
- teacher_logits: bfloat16 [4, 64, 75968], P('seq', 'vocab'), may hold values from -20 to 330
Outputs:
- mean_divergence: float32 [], replicated
- hidden_grad: float32 [256, 2560], P('seq', 'vocab')
- head_grad: float32 [2560, 75968], P('seq', 'vocab')
All inputs are finite; a program needn't handle non-finite values.
Results may differ from a plain program's by a relative error of at most 0.003.
Values may be sent and summed in bfloat16 or wider, within the bound.
No kernel may reach another device: no remote copies, remote signals or barrier semaphores. Data moves between devices by JAX's collectives and lax.ppermute only.
A program may use at most 256 MiB of HBM per device.

v0:
```python
import jax
import jax.numpy as jnp
from jax import lax
from jax.sharding import PartitionSpec as P

LOSS_SCALE = 256.0


def body(hidden_states, head_weight, teacher_logits):
    seq_count = lax.axis_size("seq")
    own_tokens = hidden_states.shape[0]
    vocab_cols = head_weight.shape[1]
    total_tokens = own_tokens * seq_count
    local_cols = lax.all_to_all(hidden_states, "seq", split_axis=1, concat_axis=0, tiled=True)
    student = jnp.dot(
        hidden_states,
        lax.all_gather(head_weight, "seq", axis=0, tiled=True),
        preferred_element_type=jnp.float32,
    )
    tiles = lax.all_to_all(teacher_logits, "vocab", split_axis=2, concat_axis=1, tiled=True)
    teacher = tiles.reshape(own_tokens, vocab_cols).astype(jnp.float32)
    student_max, teacher_max = lax.pmax(
        (jnp.max(student, axis=1), jnp.max(teacher, axis=1)), "vocab"
    )
    student_exp = jnp.exp(student - student_max[:, None])
    teacher_exp = jnp.exp(teacher - teacher_max[:, None])
    student_sum, teacher_sum, cross = lax.psum(
        (
            jnp.sum(student_exp, axis=1),
            jnp.sum(teacher_exp, axis=1),
            jnp.sum(teacher_exp * (teacher - student), axis=1),
        ),
        "vocab",
    )
    divergence = (
        cross / teacher_sum
        - teacher_max
        - jnp.log(teacher_sum)
        + student_max
        + jnp.log(student_sum)
    )
    mean_divergence = lax.psum(jnp.sum(divergence), "seq") / total_tokens
    grads = (
        LOSS_SCALE * (student_exp / student_sum[:, None] - teacher_exp / teacher_sum[:, None])
    ).astype(jnp.bfloat16)
    shard_rows = lax.all_gather(grads, "seq", axis=0, tiled=True)
    head_part = lax.dot_general(
        local_cols, shard_rows, (((0,), (0,)), ((), ())), preferred_element_type=jnp.float32
    )
    feature_rows = lax.dot_general(
        shard_rows, head_weight, (((1,), (1,)), ((), ())), preferred_element_type=jnp.float32
    )
    returned = lax.all_to_all(feature_rows, "seq", split_axis=0, concat_axis=1, tiled=True)
    hidden_grad = lax.psum_scatter(returned, "vocab", scatter_dimension=1, tiled=True)
    return (mean_divergence, hidden_grad, head_part)


def solution(mesh):
    in_specs = (P("seq", None), P("seq", "vocab"), P("seq", "vocab", None))
    out_specs = (P(), P("seq", "vocab"), P("seq", "vocab"))
    return jax.shard_map(body, mesh=mesh, in_specs=in_specs, out_specs=out_specs, check_vma=False)
```

profile of v0, /device:TPU:2, one launch (start us, length us, event | category | flops | bytes accessed | tf_op | source)
XLA Modules:
  0.0 1060.3 jit_solution(9472894223824039422)
XLA Ops:
  8.5 57.1 %copy.23 = bf16[1,8,75968]{1,0,2:T(2,128)(2,1)} copy(bf16[1,8,75968]{2,1,0:T(8,128)(2,1)S(1)} %copy-done.2) | data formatting | bytes 2430976 | tf_op args[2]
  66.0 413.1 %reduce.3 = bf16[75968,8]{1,0:T(8,128)(2,1)} reduce(bf16[75968,1,8]{2,1,0:T(2,128)(2,1)} %bitcast.41, bf16[]{:T(256)} %broadcast.7), dimensions={1}, to_apply=%bitcast.32.reduce_sub_computation | reduce | bytes 2430978
  479.1 23.5 %reshape.36 = bf16[8,2,37984]{2,1,0:T(2,128)(2,1)S(1)} reshape(bf16[75968,8]{1,0:T(8,128)(2,1)} %reduce.3) | data formatting | bytes 2430976
  502.6 19.8 %all_to_all.53 = bf16[8,2,37984]{2,1,0:T(2,128)(2,1)S(1)} all-to-all(bf16[8,2,37984]{2,1,0:T(2,128)(2,1)S(1)} %reshape.36), channel_id=1, replica_groups=mesh['vocab'=8,'seq'=4] {'vocab'}, dimensions={0} | all-to-all | bytes 2430976 | tf_op jit(solution)/shard_map/all_to_all | solution.py:20
  522.4 45.4 %reshape.37 = bf16[75968,1,8]{2,1,0:T(2,128)(2,1)} reshape(bf16[8,2,37984]{2,1,0:T(2,128)(2,1)S(1)} %all_to_all.53) | data formatting | bytes 2430976
  567.8 67.7 %copy.24 = bf16[1,8,75968]{2,1,0:T(8,128)(2,1)S(1)} copy(bf16[1,8,75968]{1,0,2:T(2,128)(2,1)} %bitcast.42) | data formatting | bytes 2430976 | tf_op jit(solution)/shard_map/all_to_all | solution.py:20
  636.8 1.8 all_to_all.40
  641.2 177.7 %all-gather.3.cloned.1.call-done = bf16[2560,9496]{0,1:T(8,128)(2,1)} async-done(((bf16[640,9496]{0,1:T(8,128)(2,1)}), bf16[2560,9496]{0,1:T(8,128)(2,1)}) %all-gather.3.cloned.1.call-update) | async-done | bytes 48619536 | tf_op jit(solution)/shard_map/all_gather | solution.py:17
  818.9 21.9 %fusion.4 = (f32[64]{0:T(128)S(1)}, f32[64,9496]{1,0:T(8,128)}) fusion(bf16[64,2560]{1,0:T(8,128)(2,1)S(1)} %copy-done.1, bf16[2560,9496]{0,1:T(8,128)(2,1)} %all-gather.3.cloned.1.call-done), kind=kOutput, calls=%fused_computation.14 | convolution fusion | flops 3112257024 | bytes 51378432 | tf_op jit(solution)/shard_map/dot_general | solution.py:15
  840.8 11.2 %all-reduce.1 = (f32[64]{0:T(128)S(1)}, f32[64]{0:T(128)S(1)}) all-reduce(f32[64]{0:T(128)S(1)} %reshape.31, f32[64]{0:T(128)S(1)} %get-tuple-element.10), channel_id=1, replica_groups=mesh['vocab'=8,'seq'=4] {'vocab'}, use_global_device_ids=true, to_apply=%region_1.0 | all-reduce | flops 128 | bytes 1024 | tf_op jit(solution)/shard_map/pmax | solution.py:22
  852.2 1.9 exponential_reduce_fusion
  854.2 2.7 fusion.2
  856.9 11.8 %all-reduce = (f32[64]{0:T(128)S(1)}, f32[64]{0:T(128)S(1)}, f32[64]{0:T(128)S(1)}) all-reduce(f32[64]{0:T(128)S(1)} %get-tuple-element.4, f32[64]{0:T(128)S(1)} %reduce_sum.40, f32[64]{0:T(128)S(1)} %get-tuple-element.3), channel_id=1, replica_groups=mesh['vocab'=8,'seq'=4] {'vocab'}, use_global_device_ids=true, to_apply=%region_9.0 | all-reduce | flops 192 | bytes 1536 | tf_op jit(solution)/shard_map/psum | solution.py:27
  868.7 3.8 multiply_convert_fusion
  872.5 91.7 %all-gather.5.cloned.1.call-done = bf16[256,9496]{1,0:T(8,128)(2,1)} async-done(((bf16[64,9496]{1,0:T(8,128)(2,1)}), bf16[256,9496]{1,0:T(8,128)(2,1)}) %all-gather.5.cloned.1.call-update) | async-done | bytes 4861968 | tf_op jit(solution)/shard_map/all_gather | solution.py:46
  964.2 10.8 %fusion.5 = f32[256,640]{1,0:T(8,128)} fusion(bf16[256,9496]{1,0:T(8,128)(2,1)} %all-gather.5.cloned.1.call-done, bf16[640,9496]{0,1:T(8,128)(2,1)} %param.4), kind=kOutput, calls=%fused_computation.15 | convolution fusion | flops 3111649280 | bytes 17672192 | tf_op jit(solution)/shard_map/dot_general | solution.py:50
  975.0 3.5 all-to-all-start.1
  979.3 16.9 %all-to-all-done.1 = f32[4,64,640]{2,1,0:T(8,128)S(1)} async-done(((f32[4,64,640]{2,1,0:T(8,128)}), f32[4,64,640]{2,1,0:T(8,128)S(1)}, u32[]{:S(2)}, u32[]{:S(2)}) %all-to-all-start.1) | async-done | bytes 655392 | tf_op jit(solution)/shard_map/all_to_all | solution.py:53
  996.2 3.5 all-to-all-start.2
  1000.3 12.8 %psum.31 = f32[]{:T(128)} all-reduce(f32[]{:T(128)} %add_reduce_fusion), channel_id=1, replica_groups=mesh['vocab'=8,'seq'=4] {'seq'}, use_global_device_ids=true, to_apply=%region_11.0 | all-reduce | flops 1 | bytes 8 | tf_op jit(solution)/shard_map/psum | solution.py:42
  1013.7 1.5 copy.33
  1015.3 15.0 %convolution_bitcast_fusion = f32[640,9496]{0,1:T(8,128)} fusion(bf16[256,9496]{1,0:T(8,128)(2,1)} %all-gather.5.cloned.1.call-done, bf16[256,640]{1,0:T(8,128)(2,1)S(1)} %bitcast.46), kind=kOutput, calls=%fused_computation | convolution fusion | flops 3111649280 | bytes 29499392 | tf_op jit(solution)/shard_map/dot_general | solution.py:47
  1030.3 20.6 %reduce-scatter.4.cloned.1.call-done = f32[320,64]{1,0:T(8,128)} async-done(((f32[2560,64]{1,0:T(8,128)}), f32[320,64]{1,0:T(8,128)}) %reduce-scatter.4.cloned.1.call-update) | async-done | bytes 81936
  1050.9 1.7 copy.32
  (25 shorter events, 7.3 us)
Async XLA Ops:
  7.2 1.3 copy-start.2
  7.2 811.7 %all-gather.3.cloned.1.call-start = ((), (), s32[]{:S(2)}) async-start(), calls=%async_computation.4 | async-start | bytes 60774400 | tf_op jit(solution)/shard_map/all_gather | solution.py:17
  7.9 956.3 %all-gather.5.cloned.1.call-start = ((), (), s32[]{:S(2)}) async-start(), calls=%async_computation.5 | async-start | bytes 6144000 | tf_op jit(solution)/shard_map/all_gather | solution.py:46
  638.6 1.0 copy-start
  638.6 180.3 %copy-start.1 = (bf16[64,2560]{1,0:T(8,128)(2,1)S(1)}, bf16[64,2560]{1,0:T(8,128)(2,1)}, u32[]{:S(2)}) copy-start(bf16[64,2560]{1,0:T(8,128)(2,1)} %param.3) | copy-start | bytes 983044
  975.0 21.1 %all-to-all-start.1 = ((f32[4,64,640]{2,1,0:T(8,128)}), f32[4,64,640]{2,1,0:T(8,128)S(1)}, u32[]{:S(2)}, u32[]{:S(2)}) async-start(f32[4,64,640]{2,1,0:T(8,128)} %bitcast.2), calls=%async_computation.1 | async-start | bytes 1310720 | tf_op jit(solution)/shard_map/all_to_all | solution.py:53
  996.2 19.1 %all-to-all-start.2 = ((bf16[64,4,640]{2,0,1:T(8,128)(2,1)}), bf16[64,4,640]{2,0,1:T(8,128)(2,1)S(1)}, u32[]{:S(2)}, u32[]{:S(2)}) async-start(bf16[64,4,640]{2,0,1:T(8,128)(2,1)} %bitcast.40), calls=%async_computation.2 | async-start | bytes 655360 | tf_op jit(solution)/shard_map/all_to_all | solution.py:14
  999.6 51.3 %reduce-scatter.4.cloned.1.call-start = ((), (), s32[]{:S(2)}) async-start(), calls=%async_computation.6 | async-start | bytes 1474560
Sparse Core Ops, SparseCore 0:
  9.6 809.2 all-gather.2
  872.6 91.5 all-gather.4
  1015.4 35.4 reduce-scatter.3
where the time goes:
time: 1060 us
  other arithmetic  424 us (40%)
  waiting for transfers between devices  308 us (29%)
  local copies, waits for them, and re-layouts  203 us (19%)
  blocking collectives  55.6 us (5%)
  matrix products  47.7 us (4%)
  between operations  15.6 us (1%)
    unnamed x1, other arithmetic  413 us
    all_gather x1, waiting for transfers between devices, body(): lax.all_gather(head_weight, 'seq', axis=0, tiled=True)  178 us
    unnamed x13, local copies, waits for them, and re-layouts  132 us
    all_gather x1, waiting for transfers between devices, body(): shard_rows = lax.all_gather(grads, 'seq', axis=0, tiled=True)  91.7 us
    all_to_all x2, local copies, waits for them, and re-layouts, body(): lax.all_to_all(teacher_logits, 'vocab', split_axis=2, concat_axis=1, tile...  69.5 us
    dot_general x1, matrix products, body(): jnp.dot(hidden_states, lax.all_gather(head_weight, 'seq', axis=0, tiled=T...  21.9 us
    unnamed x4, waiting for transfers between devices  21.3 us
  transfers between devices with their start and end apart: 5, of which 4 were waited for; matrix products, arithmetic and copies ran while one was open for 59% of the time, Pallas kernels for 0%

commit v1 on v0

v1 whole, which is shorter than its diff:
```python
import jax
import jax.numpy as jnp
from jax import lax
from jax.sharding import PartitionSpec as P

LOSS_SCALE = 256.0


def body(hidden_states, head_weight, teacher_logits):
    seq_count = lax.axis_size("seq")
    vocab_count = lax.axis_size("vocab")
    half = seq_count // 2
    last = seq_count - 1
    z = lax.axis_index("seq")
    own_tokens, width = hidden_states.shape
    rows, cols = head_weight.shape
    per_dev = teacher_logits.shape[1]
    chunk = half * per_dev
    chunks = vocab_count
    total_tokens = own_tokens * seq_count

    mine = teacher_logits[0]
    held = [mine] + [
        lax.ppermute(mine, "seq", [(j, 0), (last - j, last)]) for j in range(1, half)
    ]
    held = jnp.concatenate(held, axis=0)
    pieces = jnp.stack([held[:, v * cols:(v + 1) * cols] for v in range(vocab_count)])
    teacher = lax.all_to_all(pieces, "vocab", split_axis=0, concat_axis=0, tiled=True)

    local_cols = lax.all_to_all(hidden_states, "seq", split_axis=1, concat_axis=0, tiled=True)
    by_block = local_cols.reshape(seq_count, vocab_count, per_dev, rows)
    ordered = jnp.stack([by_block[:half], by_block[half:][::-1]])
    ordered = ordered.transpose(0, 2, 1, 3, 4).reshape(total_tokens, rows)
    partial = jnp.dot(ordered, head_weight, preferred_element_type=jnp.float32)
    partial = partial.reshape(2, chunks, chunk, cols)

    def part(side, index):
        index = jnp.clip(index, 0, chunks - 1)
        return lax.dynamic_slice(partial, (side, index, 0, 0), (1, 1, chunk, cols))[0, 0]

    steps = chunks + seq_count - 2
    own_side = (z >= half).astype(jnp.int32)
    down = up = None
    students = []
    for s in range(steps):
        send_down = part(0, s - (last - z))
        send_up = part(1, s - z)
        if down is not None:
            send_down = send_down + down
            send_up = send_up + up
        down = lax.ppermute(
            send_down, "seq",
            [(d, d - 1) for d in range(1, seq_count) if 0 <= s - (last - d) < chunks])
        up = lax.ppermute(
            send_up, "seq", [(d, d + 1) for d in range(last) if 0 <= s - d < chunks])
        index = s - (seq_count - 2)
        if index >= 0:
            students.append(part(own_side, index) + jnp.where(z < half, down, up))

    divergence = jnp.zeros((), jnp.float32)
    grads = []
    for i in range(chunks):
        student = students[i]
        target = teacher[i].astype(jnp.float32)
        student_top = jnp.max(student, axis=1)
        target_top = jnp.max(target, axis=1)
        target_exp = jnp.exp(target - target_top[:, None])
        stats = jnp.stack([
            student_top,
            target_top,
            jnp.sum(jnp.exp(student - student_top[:, None]), axis=1),
            jnp.sum(target_exp, axis=1),
            jnp.sum(target_exp * (target - student), axis=1),
        ])
        stats = lax.all_gather(stats, "vocab", axis=0)
        student_max = jnp.max(stats[:, 0], axis=0)
        teacher_max = jnp.max(stats[:, 1], axis=0)
        student_scale = jnp.exp(stats[:, 0] - student_max)
        teacher_scale = jnp.exp(stats[:, 1] - teacher_max)
        student_sum = jnp.sum(stats[:, 2] * student_scale, axis=0)
        teacher_sum = jnp.sum(stats[:, 3] * teacher_scale, axis=0)
        cross = jnp.sum(stats[:, 4] * teacher_scale, axis=0)
        divergence = divergence + jnp.sum(
            cross / teacher_sum
            - teacher_max
            - jnp.log(teacher_sum)
            + student_max
            + jnp.log(student_sum)
        )
        grads.append((
            LOSS_SCALE * (
                jnp.exp(student - student_max[:, None]) / student_sum[:, None]
                - jnp.exp(target - teacher_max[:, None]) / teacher_sum[:, None]
            )
        ).astype(jnp.bfloat16))
    at_end = (z == 0) | (z == last)
    mean_divergence = lax.psum(jnp.where(at_end, divergence, 0.0), "seq") / total_tokens

    from_low, from_high = [], []
    for s in range(steps):
        send_up = grads[min(s, chunks - 1)]
        send_down = send_up
        if s > 0:
            send_up = jnp.where(z == 0, send_up, from_low[-1])
            send_down = jnp.where(z == last, send_down, from_high[-1])
        from_low.append(lax.ppermute(
            send_up, "seq", [(d, d + 1) for d in range(last) if 0 <= s - d < chunks]))
        from_high.append(lax.ppermute(
            send_down, "seq",
            [(d, d - 1) for d in range(1, seq_count) if 0 <= s - (last - d) < chunks]))
    own = jnp.stack(grads)
    low = lax.dynamic_slice_in_dim(jnp.stack(from_low), jnp.maximum(z - 1, 0), chunks)
    high = lax.dynamic_slice_in_dim(jnp.stack(from_high), jnp.maximum(last - 1 - z, 0), chunks)
    low = jnp.where(z == 0, own, low)
    high = jnp.where(z == last, own, high)
    all_grads = jnp.stack([low, high]).reshape(total_tokens, cols)

    feature = lax.dot_general(
        all_grads, head_weight, (((1,), (1,)), ((), ())), preferred_element_type=jnp.float32
    )
    feature = feature.reshape(2, vocab_count, half, per_dev, rows).transpose(0, 2, 1, 3, 4)
    feature = jnp.concatenate([feature[0], feature[1][::-1]]).reshape(seq_count, own_tokens, rows)
    if vocab_count % seq_count == 0:
        share = vocab_count // seq_count
        out_cols = rows // share
        feature = feature.reshape(seq_count, own_tokens, share, out_cols).transpose(0, 2, 1, 3)
        feature = feature.reshape(vocab_count, own_tokens, out_cols)
        feature = lax.all_to_all(feature, "vocab", split_axis=0, concat_axis=0, tiled=True)
        feature = jnp.sum(feature, axis=0)
        pairs = [
            ((dst * share + b) * seq_count + src, (src * share + b) * seq_count + dst)
            for src in range(seq_count) for dst in range(seq_count) for b in range(share)
        ]
        hidden_grad = lax.ppermute(feature, ("vocab", "seq"), pairs)
    else:
        feature = lax.all_to_all(feature, "seq", split_axis=0, concat_axis=2, tiled=True)
        hidden_grad = lax.psum_scatter(feature[0], "vocab", scatter_dimension=1, tiled=True)
    head_part = lax.dot_general(
        ordered, all_grads, (((0,), (0,)), ((), ())), preferred_element_type=jnp.float32
    )
    return (mean_divergence, hidden_grad, head_part)


def solution(mesh):
    in_specs = (P("seq", None), P("seq", "vocab"), P("seq", "vocab", None))
    out_specs = (P(), P("seq", "vocab"), P("seq", "vocab"))
    return jax.shard_map(body, mesh=mesh, in_specs=in_specs, out_specs=out_specs, check_vma=False)
```

time: 1060 us -> 486 us (0.46)
  other arithmetic: 424 us -> 60.6 us
  local copies, waits for them, and re-layouts: 203 us -> 24.4 us
  waiting for transfers between devices: 308 us -> 175 us
  starting transfers between devices: 7.05 us -> 102 us
  blocking collectives: 55.6 us -> 77.6 us
  matrix products: 47.7 us -> 35.7 us
    unnamed x1 -> x9, other arithmetic: 413 us -> 8.23 us
    all_gather x2 -> x0, waiting for transfers between devices: 269 us -> none  [the longest x1 178 us: body(): lax.all_gather(head_weight, 'seq', axis=0, tiled=True)]
    ppermute x0 -> x42, waiting for transfers between devices: none -> 158 us  [the longest x20 87.7 us: body(): lax.ppermute(send_down, 'seq', [(d, d - 1) for d in range(1, seq_count) i...]
    unnamed x13 -> x55, local copies, waits for them, and re-layouts: 132 us -> 14.4 us
    ppermute x0 -> x42, starting transfers between devices: none -> 87.6 us  [the longest x20 59.5 us: body(): lax.ppermute(send_up, 'seq', [(d, d + 1) for d in range(last) if 0 <= s -...]
    all_to_all x2 -> x0, local copies, waits for them, and re-layouts: 69.5 us -> none  [body(): lax.all_to_all(teacher_logits, 'vocab', split_axis=2, concat_axis=1, tile...]
    all_gather x0 -> x8, blocking collectives: none -> 68.8 us  [body(): stats = lax.all_gather(stats, 'vocab', axis=0)]
    unnamed x4 -> x0, waiting for transfers between devices: 21.3 us -> none
  transfers between devices with their start and end apart: 5 -> 45, of which waited for: 4 -> 28; matrix products, arithmetic and copies ran while one was open for 59% -> 13% of each run, Pallas kernels for 0% -> 0%
where the time goes in v1:
time: 486 us; the launch traced here: 483 us
  waiting for transfers between devices  175 us (36%)
  starting transfers between devices  102 us (21%)
  blocking collectives  77.6 us (16%)
  other arithmetic  60.6 us (12%)
  matrix products  35.7 us (7%)
  local copies, waits for them, and re-layouts  24.4 us (5%)
  between operations  8.33 us (2%)
    ppermute x20, waiting for transfers between devices, body(): lax.ppermute(send_down, 'seq', [(d, d - 1) for d in range(1, seq_count) i...  87.7 us
    all_gather x8, blocking collectives, body(): stats = lax.all_gather(stats, 'vocab', axis=0)  68.8 us
    ppermute x20, starting transfers between devices, body(): lax.ppermute(send_up, 'seq', [(d, d + 1) for d in range(last) if 0 <= s -...  59.5 us
    ppermute x20, waiting for transfers between devices, body(): lax.ppermute(send_up, 'seq', [(d, d + 1) for d in range(last) if 0 <= s -...  58.3 us
    ppermute x20, starting transfers between devices, body(): lax.ppermute(send_down, 'seq', [(d, d - 1) for d in range(1, seq_count) i...  24.3 us
    reduce_max x8, other arithmetic, body(): student_top = jnp.max(student, axis=1)  20.2 us
    dot_general x1, matrix products, body(): lax.dot_general(ordered, all_grads, (((0,), (0,)), ((), ())), preferred_e...  15.1 us
    unnamed x55, local copies, waits for them, and re-layouts  14.4 us
  transfers between devices with their start and end apart: 45, of which 28 were waited for; matrix products, arithmetic and copies ran while one was open for 13% of the time, Pallas kernels for 0%

profile of v1, /device:TPU:2, one launch (start us, length us, event | category | flops | bytes accessed | tf_op | source)
XLA Modules:
  0.0 483.0 jit_solution(338888617207710407)
XLA Ops:
  7.2 10.3 %all-to-all-done = bf16[64,4,640]{2,0,1:T(8,128)(2,1)S(1)} async-done(((bf16[64,4,640]{2,0,1:T(8,128)(2,1)}), bf16[64,4,640]{2,0,1:T(8,128)(2,1)S(1)}, u32[]{:S(2)}, u32[]{:S(2)}) %all-to-all-start) | async-done | bytes 327712 | tf_op jit(solution)/shard_map/all_to_all | solution.py:30
  17.6 13.9 %fusion.2 = f32[2,8,16,9496]{3,2,1,0:T(8,128)} fusion(bf16[640,9496]{0,1:T(8,128)(2,1)} %param.4, bf16[1,2,8,8,640]{4,3,2,1,0:T(8,128)(2,1)S(1)} %reverse_bitcast_fusion, bf16[1,2,8,8,640]{4,3,2,1,0:T(8,128)(2,1)S(1)} %get-tuple-element.121), kind=kOutput, calls=%fused_computation.2 | convolution fusion | flops 3111813120 | bytes 22206464 | tf_op jit(solution)/shard_map/dot_general | solution.py:34
  38.4 9.0 %collective-permute-done.3 = f32[16,9496]{1,0:T(8,128)} collective-permute-done((f32[16,9496]{1,0:T(8,128)}, f32[16,9496]{1,0:T(8,128)}, u32[]{:S(2)}, u32[]{:S(2)}) %collective-permute-start.3) | collective-permute-done | bytes 607776 | tf_op jit(solution)/shard_map/ppermute | solution.py:54
  53.1 11.8 %collective-permute-done.6 = bf16[8,75968]{1,0:T(8,128)(2,1)S(1)} collective-permute-done((bf16[8,75968]{1,0:T(8,128)(2,1)S(1)}, bf16[8,75968]{1,0:T(8,128)(2,1)S(1)}, u32[]{:S(2)}, u32[]{:S(2)}) %collective-permute-start.6) | collective-permute-done | bytes 1215520 | tf_op jit(solution)/shard_map/ppermute | solution.py:24
  77.5 6.9 %collective-permute-done.5 = f32[16,9496]{1,0:T(8,128)S(1)} collective-permute-done((f32[16,9496]{1,0:T(8,128)S(1)}, f32[16,9496]{1,0:T(8,128)S(1)}, u32[]{:S(2)}, u32[]{:S(2)}) %collective-permute-start.5) | collective-permute-done | bytes 607776 | tf_op jit(solution)/shard_map/ppermute | solution.py:54
  84.5 13.5 %collective-permute-done.2 = f32[16,9496]{1,0:T(8,128)S(1)} collective-permute-done((f32[16,9496]{1,0:T(8,128)S(1)}, f32[16,9496]{1,0:T(8,128)S(1)}, u32[]{:S(2)}, u32[]{:S(2)}) %collective-permute-start.2) | collective-permute-done | bytes 607776 | tf_op jit(solution)/shard_map/ppermute | solution.py:51
  127.8 6.5 %collective-permute-done.10 = f32[16,9496]{1,0:T(8,128)} collective-permute-done((f32[16,9496]{1,0:T(8,128)}, f32[16,9496]{1,0:T(8,128)}, u32[]{:S(2)}, u32[]{:S(2)}) %collective-permute-start.10) | collective-permute-done | bytes 607776 | tf_op jit(solution)/shard_map/ppermute | solution.py:54
  196.1 10.7 %collective-permute-done.17 = f32[16,9496]{1,0:T(8,128)S(1)} collective-permute-done((f32[16,9496]{1,0:T(8,128)S(1)}, f32[16,9496]{1,0:T(8,128)S(1)}, u32[]{:S(2)}, u32[]{:S(2)}) %collective-permute-start.17) | collective-permute-done | bytes 607776 | tf_op jit(solution)/shard_map/ppermute | solution.py:51
  211.1 9.0 %all-gather.13 = f32[8,5,16]{2,1,0:T(8,128)S(1)} all-gather(f32[1,5,16]{2,1,0:T(8,128)S(1)} %bitcast.464), channel_id=7, replica_groups=mesh['vocab'=8,'seq'=4] {'vocab'}, dimensions={0}, use_global_device_ids=true | all-gather | bytes 2880 | tf_op jit(solution)/shard_map/all_gather | solution.py:75
  220.2 8.1 %all-gather.12 = f32[8,5,16]{2,1,0:T(8,128)S(1)} all-gather(f32[1,5,16]{2,1,0:T(8,128)S(1)} %bitcast.465), channel_id=6, replica_groups=mesh['vocab'=8,'seq'=4] {'vocab'}, dimensions={0}, use_global_device_ids=true | all-gather | bytes 2880 | tf_op jit(solution)/shard_map/all_gather | solution.py:75
  228.4 9.0 %all-gather.11 = f32[8,5,16]{2,1,0:T(8,128)S(1)} all-gather(f32[1,5,16]{2,1,0:T(8,128)S(1)} %bitcast.466), channel_id=5, replica_groups=mesh['vocab'=8,'seq'=4] {'vocab'}, dimensions={0}, use_global_device_ids=true | all-gather | bytes 2880 | tf_op jit(solution)/shard_map/all_gather | solution.py:75
  237.4 8.3 %all-gather.14 = f32[8,5,16]{2,1,0:T(8,128)S(1)} all-gather(f32[1,5,16]{2,1,0:T(8,128)S(1)} %bitcast.467), channel_id=8, replica_groups=mesh['vocab'=8,'seq'=4] {'vocab'}, dimensions={0}, use_global_device_ids=true | all-gather | bytes 2880 | tf_op jit(solution)/shard_map/all_gather | solution.py:75
  251.4 13.4 %collective-permute-done.19 = f32[16,9496]{1,0:T(8,128)} collective-permute-done((f32[16,9496]{1,0:T(8,128)}, f32[16,9496]{1,0:T(8,128)}, u32[]{:S(2)}, u32[]{:S(2)}) %collective-permute-start.19) | collective-permute-done | bytes 607776 | tf_op jit(solution)/shard_map/ppermute | solution.py:51
  269.0 9.0 %all-gather.10 = f32[8,5,16]{2,1,0:T(8,128)S(1)} all-gather(f32[1,5,16]{2,1,0:T(8,128)S(1)} %bitcast.468), channel_id=4, replica_groups=mesh['vocab'=8,'seq'=4] {'vocab'}, dimensions={0}, use_global_device_ids=true | all-gather | bytes 2880 | tf_op jit(solution)/shard_map/all_gather | solution.py:75
  278.1 8.1 %all-gather.9 = f32[8,5,16]{2,1,0:T(8,128)S(1)} all-gather(f32[1,5,16]{2,1,0:T(8,128)S(1)} %bitcast.469), channel_id=3, replica_groups=mesh['vocab'=8,'seq'=4] {'vocab'}, dimensions={0}, use_global_device_ids=true | all-gather | bytes 2880 | tf_op jit(solution)/shard_map/all_gather | solution.py:75
  286.3 9.0 %all-gather.8 = f32[8,5,16]{2,1,0:T(8,128)S(1)} all-gather(f32[1,5,16]{2,1,0:T(8,128)S(1)} %bitcast.470), channel_id=2, replica_groups=mesh['vocab'=8,'seq'=4] {'vocab'}, dimensions={0}, use_global_device_ids=true | all-gather | bytes 2880 | tf_op jit(solution)/shard_map/all_gather | solution.py:75
  295.4 8.1 %all-gather.15 = f32[8,5,16]{2,1,0:T(8,128)S(1)} all-gather(f32[1,5,16]{2,1,0:T(8,128)S(1)} %bitcast.471), channel_id=9, replica_groups=mesh['vocab'=8,'seq'=4] {'vocab'}, dimensions={0}, use_global_device_ids=true | all-gather | bytes 2880 | tf_op jit(solution)/shard_map/all_gather | solution.py:75
  316.4 8.8 %psum.7 = f32[]{:T(128)} all-reduce(f32[]{:T(128)S(6)} %select_n.182), channel_id=1, replica_groups=mesh['vocab'=8,'seq'=4] {'seq'}, use_global_device_ids=true, to_apply=%region_88.89 | all-reduce | flops 1 | bytes 8 | tf_op jit(solution)/shard_map/psum | solution.py:97
  399.2 11.3 %collective-permute-done.38 = bf16[16,9496]{1,0:T(8,128)(2,1)S(1)} collective-permute-done((bf16[16,9496]{1,0:T(8,128)(2,1)S(1)}, bf16[16,9496]{1,0:T(8,128)(2,1)S(1)}, u32[]{:S(2)}, u32[]{:S(2)}) %collective-permute-start.38) | collective-permute-done | bytes 303904 | tf_op jit(solution)/shard_map/ppermute | solution.py:108
  413.4 6.7 %collective-permute-done.39 = bf16[16,9496]{1,0:T(8,128)(2,1)S(1)} collective-permute-done((bf16[16,9496]{1,0:T(8,128)(2,1)S(1)}, bf16[16,9496]{1,0:T(8,128)(2,1)S(1)}, u32[]{:S(2)}, u32[]{:S(2)}) %collective-permute-start.39) | collective-permute-done | bytes 303904 | tf_op jit(solution)/shard_map/ppermute | solution.py:108
  429.6 7.1 %fusion.12 = (bf16[1,8,16,9496]{3,2,1,0:T(8,128)(2,1)S(1)}, bf16[1,8,2,8,9496]{4,3,2,1,0:T(8,128)(2,1)}, bf16[1,8,2,8,9496]{4,3,2,1,0:T(8,128)(2,1)}, bf16[1,8,16,9496]{3,2,1,0:T(8,128)(2,1)}) fusion(bf16[8,16,9496]{2,1,0:T(8,128)(2,1)} %bitcast_dynamic-update-slice_fusion.20, bf16[10,16,9496]{2,1,0:T(8,128)(2,1)} %copy-done.10, s32[]{:T(128)S(6)} %max.94, ...), kind=kLoop, calls=%fused_computation.50 | loop fusion | flops 2430976 | bytes 17016842 | tf_op jit(solution)/shard_map/stack | solution.py:116
  437.2 6.7 %fusion.7 = f32[2,2,8,8,640]{4,3,1,2,0:T(8,128)S(1)} fusion(bf16[640,9496]{0,1:T(8,128)(2,1)S(1)} %bitcast.427, bf16[1,8,2,8,9496]{4,3,2,1,0:T(8,128)(2,1)} %get-tuple-element.115, bf16[1,8,2,8,9496]{4,3,2,1,0:T(8,128)(2,1)} %get-tuple-element.112), kind=kOutput, calls=%fused_computation.24 | convolution fusion | flops 3114080256 | bytes 17672192 | tf_op jit(solution)/shard_map/dot_general | solution.py:118
  457.0 6.7 %all-to-all-done.2 = f32[8,64,320]{2,1,0:T(8,128)S(1)} async-done(((f32[8,64,320]{2,1,0:T(8,128)}), f32[8,64,320]{2,1,0:T(8,128)S(1)}, u32[]{:S(2)}, u32[]{:S(2)}) %all-to-all-start.2) | async-done | bytes 655392 | tf_op jit(solution)/shard_map/all_to_all | solution.py:128
  466.1 15.1 %fusion.127 = f32[640,9496]{0,1:T(8,128)} fusion(bf16[256,640]{1,0:T(8,128)(2,1)} %bitcast.429, bf16[256,9496]{1,0:T(8,128)(2,1)} %bitcast.425), kind=kOutput, calls=%fused_computation.309 | convolution fusion | flops 3111649280 | bytes 29499392 | tf_op jit(solution)/shard_map/dot_general | solution.py:138
  (249 shorter events, 247.6 us)
Async XLA Ops:
  2.4 15.2 %all-to-all-start = ((bf16[64,4,640]{2,0,1:T(8,128)(2,1)}), bf16[64,4,640]{2,0,1:T(8,128)(2,1)S(1)}, u32[]{:S(2)}, u32[]{:S(2)}) async-start(bf16[64,4,640]{2,0,1:T(8,128)(2,1)} %bitcast.415), calls=%async_computation | async-start | bytes 655360 | tf_op jit(solution)/shard_map/all_to_all | solution.py:30
  33.8 13.5 %collective-permute-start.3 = (f32[16,9496]{1,0:T(8,128)}, f32[16,9496]{1,0:T(8,128)}, u32[]{:S(2)}, u32[]{:S(2)}) collective-permute-start(f32[16,9496]{1,0:T(8,128)} %get-tuple-element.109), channel_id=1, source_target_pairs={{0,1},{4,5},{8,9},{12,13},{16,17},{20,21},{24,25},{28,29}} | collective-permute-start | bytes 1823240 | tf_op jit(solution)/shard_map/ppermute | solution.py:54
  36.3 28.5 %collective-permute-start.6 = (bf16[8,75968]{1,0:T(8,128)(2,1)S(1)}, bf16[8,75968]{1,0:T(8,128)(2,1)S(1)}, u32[]{:S(2)}, u32[]{:S(2)}) collective-permute-start(bf16[8,75968]{1,0:T(8,128)(2,1)S(1)} %bitcast.416), channel_id=1, source_target_pairs={{1,0},{2,3},{5,4},{6,7},{9,8},{10,11},{13,12},{14,15},{17,16},{18,... | collective-permute-start | bytes 3646472 | tf_op jit(solution)/shard_map/ppermute | solution.py:24
  37.7 31.5 %collective-permute-start = (f32[16,9496]{1,0:T(8,128)S(1)}, f32[16,9496]{1,0:T(8,128)S(1)}, u32[]{:S(2)}, u32[]{:S(2)}) collective-permute-start(f32[16,9496]{1,0:T(8,128)S(1)} %get-tuple-element.110), channel_id=1, source_target_pairs={{3,2},{7,6},{11,10},{15,14},{19,18},{23,22},{27,26},{31,30}} | collective-permute-start | bytes 1823240 | tf_op jit(solution)/shard_map/ppermute | solution.py:51
  48.7 20.5 %collective-permute-start.4 = (f32[16,9496]{1,0:T(8,128)S(1)}, f32[16,9496]{1,0:T(8,128)S(1)}, u32[]{:S(2)}, u32[]{:S(2)}) collective-permute-start(f32[16,9496]{1,0:T(8,128)S(1)} %bitcast_add_fusion.21), channel_id=1, source_target_pairs={{0,1},{1,2},{4,5},{5,6},{8,9},{9,10},{12,13},{13,14},{16,17},{17,1... | collective-permute-start | bytes 1823240 | tf_op jit(solution)/shard_map/ppermute | solution.py:54
  72.1 12.3 %collective-permute-start.5 = (f32[16,9496]{1,0:T(8,128)S(1)}, f32[16,9496]{1,0:T(8,128)S(1)}, u32[]{:S(2)}, u32[]{:S(2)}) collective-permute-start(f32[16,9496]{1,0:T(8,128)S(1)} %get-tuple-element.107), channel_id=1, source_target_pairs={{0,1},{1,2},{2,3},{4,5},{5,6},{6,7},{8,9},{9,10},{10,11},{12,13},{... | collective-permute-start | bytes 1823240 | tf_op jit(solution)/shard_map/ppermute | solution.py:54
  75.4 22.6 %collective-permute-start.2 = (f32[16,9496]{1,0:T(8,128)S(1)}, f32[16,9496]{1,0:T(8,128)S(1)}, u32[]{:S(2)}, u32[]{:S(2)}) collective-permute-start(f32[16,9496]{1,0:T(8,128)S(1)} %bitcast_add_fusion.24), channel_id=1, source_target_pairs={{1,0},{2,1},{3,2},{5,4},{6,5},{7,6},{9,8},{10,9},{11,10},{13,12},{... | collective-permute-start | bytes 1823240 | tf_op jit(solution)/shard_map/ppermute | solution.py:51
  100.7 13.9 %collective-permute-start.8 = (f32[16,9496]{1,0:T(8,128)}, f32[16,9496]{1,0:T(8,128)}, u32[]{:S(2)}, u32[]{:S(2)}) collective-permute-start(f32[16,9496]{1,0:T(8,128)} %get-tuple-element.105), channel_id=1, source_target_pairs={{0,1},{1,2},{2,3},{4,5},{5,6},{6,7},{8,9},{9,10},{10,11},{12,13},{... | collective-permute-start | bytes 1823240 | tf_op jit(solution)/shard_map/ppermute | solution.py:54
  105.9 13.4 %collective-permute-start.7 = (f32[16,9496]{1,0:T(8,128)S(1)}, f32[16,9496]{1,0:T(8,128)}, u32[]{:S(2)}, u32[]{:S(2)}) collective-permute-start(f32[16,9496]{1,0:T(8,128)S(1)} %get-tuple-element.106), channel_id=1, source_target_pairs={{1,0},{2,1},{3,2},{5,4},{6,5},{7,6},{9,8},{10,9},{11,10},{13,12},{... | collective-permute-start | bytes 1823240 | tf_op jit(solution)/shard_map/ppermute | solution.py:51
  108.1 55.9 %all-to-all-start.1 = ((bf16[8,16,9496]{2,1,0:T(8,128)(2,1)}), bf16[8,16,9496]{2,1,0:T(8,128)(2,1)S(1)}, u32[]{:S(2)}, u32[]{:S(2)}) async-start(bf16[8,16,9496]{2,1,0:T(8,128)(2,1)} %fusion.97), calls=%async_computation.1 | async-start | bytes 4915200 | tf_op jit(solution)/shard_map/all_to_all | solution.py:28
  122.5 11.7 %collective-permute-start.10 = (f32[16,9496]{1,0:T(8,128)}, f32[16,9496]{1,0:T(8,128)}, u32[]{:S(2)}, u32[]{:S(2)}) collective-permute-start(f32[16,9496]{1,0:T(8,128)} %get-tuple-element.103), channel_id=1, source_target_pairs={{0,1},{1,2},{2,3},{4,5},{5,6},{6,7},{8,9},{9,10},{10,11},{12,13},{... | collective-permute-start | bytes 1823240 | tf_op jit(solution)/shard_map/ppermute | solution.py:54
  126.5 12.5 %collective-permute-start.9 = (f32[16,9496]{1,0:T(8,128)S(1)}, f32[16,9496]{1,0:T(8,128)}, u32[]{:S(2)}, u32[]{:S(2)}) collective-permute-start(f32[16,9496]{1,0:T(8,128)S(1)} %get-tuple-element.104), channel_id=1, source_target_pairs={{1,0},{2,1},{3,2},{5,4},{6,5},{7,6},{9,8},{10,9},{11,10},{13,12},{... | collective-permute-start | bytes 1823240 | tf_op jit(solution)/shard_map/ppermute | solution.py:51
  144.6 12.1 %collective-permute-start.11 = (f32[16,9496]{1,0:T(8,128)S(1)}, f32[16,9496]{1,0:T(8,128)}, u32[]{:S(2)}, u32[]{:S(2)}) collective-permute-start(f32[16,9496]{1,0:T(8,128)S(1)} %get-tuple-element.102), channel_id=1, source_target_pairs={{1,0},{2,1},{3,2},{5,4},{6,5},{7,6},{9,8},{10,9},{11,10},{13,12},{... | collective-permute-start | bytes 1823240 | tf_op jit(solution)/shard_map/ppermute | solution.py:51
  162.7 12.3 %collective-permute-start.13 = (f32[16,9496]{1,0:T(8,128)}, f32[16,9496]{1,0:T(8,128)}, u32[]{:S(2)}, u32[]{:S(2)}) collective-permute-start(f32[16,9496]{1,0:T(8,128)} %get-tuple-element.100), channel_id=1, source_target_pairs={{1,0},{2,1},{3,2},{5,4},{6,5},{7,6},{9,8},{10,9},{11,10},{13,12},{... | collective-permute-start | bytes 1823240 | tf_op jit(solution)/shard_map/ppermute | solution.py:51
  178.7 13.6 %collective-permute-start.15 = (f32[16,9496]{1,0:T(8,128)S(1)}, f32[16,9496]{1,0:T(8,128)S(1)}, u32[]{:S(2)}, u32[]{:S(2)}) collective-permute-start(f32[16,9496]{1,0:T(8,128)S(1)} %get-tuple-element.96), channel_id=1, source_target_pairs={{1,0},{2,1},{3,2},{5,4},{6,5},{7,6},{9,8},{10,9},{11,10},{13,12},{... | collective-permute-start | bytes 1823240 | tf_op jit(solution)/shard_map/ppermute | solution.py:51
  194.8 12.0 %collective-permute-start.17 = (f32[16,9496]{1,0:T(8,128)S(1)}, f32[16,9496]{1,0:T(8,128)S(1)}, u32[]{:S(2)}, u32[]{:S(2)}) collective-permute-start(f32[16,9496]{1,0:T(8,128)S(1)} %get-tuple-element.94), channel_id=1, source_target_pairs={{1,0},{2,1},{5,4},{6,5},{9,8},{10,9},{13,12},{14,13},{17,16},{18,1... | collective-permute-start | bytes 1823240 | tf_op jit(solution)/shard_map/ppermute | solution.py:51
  246.5 18.3 %collective-permute-start.19 = (f32[16,9496]{1,0:T(8,128)}, f32[16,9496]{1,0:T(8,128)}, u32[]{:S(2)}, u32[]{:S(2)}) collective-permute-start(f32[16,9496]{1,0:T(8,128)} %get-tuple-element.98), channel_id=1, source_target_pairs={{1,0},{5,4},{9,8},{13,12},{17,16},{21,20},{25,24},{29,28}} | collective-permute-start | bytes 1823240 | tf_op jit(solution)/shard_map/ppermute | solution.py:51
  306.4 19.5 %collective-permute-start.21 = (bf16[16,9496]{1,0:T(8,128)(2,1)}, bf16[16,9496]{1,0:T(8,128)(2,1)S(1)}, u32[]{:S(2)}, u32[]{:S(2)}) collective-permute-start(bf16[16,9496]{1,0:T(8,128)(2,1)} %get-tuple-element.76), channel_id=1, source_target_pairs={{0,1},{4,5},{8,9},{12,13},{16,17},{20,21},{24,25},{28,29}} | collective-permute-start | bytes 911624 | tf_op jit(solution)/shard_map/ppermute | solution.py:106
  315.0 17.1 %collective-permute-start.31 = (bf16[16,9496]{1,0:T(8,128)(2,1)}, bf16[16,9496]{1,0:T(8,128)(2,1)}, u32[]{:S(2)}, u32[]{:S(2)}) collective-permute-start(bf16[16,9496]{1,0:T(8,128)(2,1)} %get-tuple-element.76), channel_id=1, source_target_pairs={{3,2},{7,6},{11,10},{15,14},{19,18},{23,22},{27,26},{31,30}} | collective-permute-start | bytes 911624 | tf_op jit(solution)/shard_map/ppermute | solution.py:108
  381.5 12.0 %collective-permute-start.37 = (bf16[16,9496]{1,0:T(8,128)(2,1)S(1)}, bf16[16,9496]{1,0:T(8,128)(2,1)S(1)}, u32[]{:S(2)}, u32[]{:S(2)}) collective-permute-start(bf16[16,9496]{1,0:T(8,128)(2,1)S(1)} %broadcast_select_fusion.3), channel_id=1, source_target_pairs={{1,0},{2,1},{3,2},{5,4},{6,5},{7,6},{9,8},{10,9},{11,10},{13,12},{... | collective-permute-start | bytes 911624 | tf_op jit(solution)/shard_map/ppermute | solution.py:108
  397.8 12.7 %collective-permute-start.38 = (bf16[16,9496]{1,0:T(8,128)(2,1)S(1)}, bf16[16,9496]{1,0:T(8,128)(2,1)S(1)}, u32[]{:S(2)}, u32[]{:S(2)}) collective-permute-start(bf16[16,9496]{1,0:T(8,128)(2,1)S(1)} %get-tuple-element.126), channel_id=1, source_target_pairs={{1,0},{2,1},{3,2},{5,4},{6,5},{7,6},{9,8},{10,9},{11,10},{13,12},{... | collective-permute-start | bytes 911624 | tf_op jit(solution)/shard_map/ppermute | solution.py:108
  410.6 11.7 %collective-permute-start.30 = (bf16[16,9496]{1,0:T(8,128)(2,1)S(1)}, bf16[16,9496]{1,0:T(8,128)(2,1)S(1)}, u32[]{:S(2)}, u32[]{:S(2)}) collective-permute-start(bf16[16,9496]{1,0:T(8,128)(2,1)S(1)} %get-tuple-element.123), channel_id=1, source_target_pairs={{2,3},{6,7},{10,11},{14,15},{18,19},{22,23},{26,27},{30,31}} | collective-permute-start | bytes 911624 | tf_op jit(solution)/shard_map/ppermute | solution.py:106
  447.6 16.0 %all-to-all-start.2 = ((f32[8,64,320]{2,1,0:T(8,128)}), f32[8,64,320]{2,1,0:T(8,128)S(1)}, u32[]{:S(2)}, u32[]{:S(2)}) async-start(f32[8,64,320]{2,1,0:T(8,128)} %bitcast.428), calls=%async_computation.2 | async-start | bytes 1572864 | tf_op jit(solution)/shard_map/all_to_all | solution.py:128
  463.7 17.6 %collective-permute-start.41 = (f32[64,320]{1,0:T(8,128)S(1)}, f32[64,320]{1,0:T(8,128)S(1)}, u32[]{:S(2)}, u32[]{:S(2)}) collective-permute-start(f32[64,320]{1,0:T(8,128)S(1)} %reduce_sum.569), channel_id=1, source_target_pairs={{0,0},{4,4},{8,1},{12,5},{16,2},{20,6},{24,3},{28,7},{1,8},{5,12},... | collective-permute-start | bytes 245768 | tf_op jit(solution)/shard_map/ppermute | solution.py:134
  (36 other events, 394.3 us)

commit v2 on v1

v2 whole, which is shorter than its diff:
```python
import jax
import jax.numpy as jnp
from jax import lax
from jax.experimental import pallas as pl
from jax.experimental.pallas import tpu as pltpu
from jax.sharding import PartitionSpec as P

LOSS_SCALE = 256.0
VOCAB_TILE = 1024


def after(value, *others):
    return lax.optimization_barrier((value, *others))[0]


def partial_kernel(hidden_ref, head_ref, *out_refs):
    product = lax.dot_general(
        hidden_ref[...], head_ref[...], (((1,), (1,)), ((), ())),
        preferred_element_type=jnp.float32)
    height = out_refs[0].shape[0]
    for i, out_ref in enumerate(out_refs):
        out_ref[...] = product[i * height:(i + 1) * height]


def partial_students(hidden, head_rows, chunk):
    tokens, rows = hidden.shape
    cols = head_rows.shape[0]
    tile = min(VOCAB_TILE, cols)
    count = tokens // chunk
    return pl.pallas_call(
        partial_kernel,
        grid=(pl.cdiv(cols, tile),),
        in_specs=[
            pl.BlockSpec((tokens, rows), lambda i: (0, 0)),
            pl.BlockSpec((tile, rows), lambda i: (i, 0)),
        ],
        out_specs=[pl.BlockSpec((chunk, tile), lambda i: (0, i))] * count,
        out_shape=[jax.ShapeDtypeStruct((chunk, cols), jnp.float32)] * count,
        compiler_params=pltpu.CompilerParams(vmem_limit_bytes=48 * 1024 * 1024),
        cost_estimate=pl.CostEstimate(
            flops=2 * tokens * rows * cols,
            bytes_accessed=2 * rows * cols + 4 * tokens * cols,
            transcendentals=0),
    )(hidden, head_rows)


def body(hidden_states, head_weight, teacher_logits):
    seq_count = lax.axis_size("seq")
    vocab_count = lax.axis_size("vocab")
    half = seq_count // 2
    last = seq_count - 1
    z = lax.axis_index("seq")
    own_tokens, width = hidden_states.shape
    rows, cols = head_weight.shape
    per_dev = teacher_logits.shape[1]
    chunk = half * per_dev
    chunks = vocab_count
    total_tokens = own_tokens * seq_count
    hops = seq_count - 1
    low_side = z < half

    def hop(value, j):
        return lax.ppermute(value, "seq", [(last - j, last - j - 1), (j, j + 1)])

    blocks = [lax.dynamic_slice_in_dim(hidden_states, z * rows, rows, axis=1)]
    for k in range(1, seq_count):
        piece = lax.dynamic_slice_in_dim(
            hidden_states, ((z + k) % seq_count) * rows, rows, axis=1)
        blocks.append(lax.ppermute(
            piece, "seq", [(d, (d + k) % seq_count) for d in range(seq_count)]))
    blocks = jnp.stack(blocks).reshape(seq_count, vocab_count, per_dev, rows)
    sides = []
    for end in (jnp.where(low_side, 0, last), jnp.where(low_side, last, 0)):
        step = jnp.where(end == 0, 1, -1)
        sides.append(jnp.stack(
            [blocks[(z - (end + step * j)) % seq_count] for j in range(half)], axis=1))
    ordered = jnp.stack(sides).reshape(total_tokens, rows)
    head_rows = head_weight.T
    partial = partial_students(ordered, head_rows, chunk)
    own_part, other_part = partial[:chunks], partial[chunks:]

    mine = teacher_logits[0]
    held = [mine] + [
        lax.ppermute(mine, "seq", [(j, 0), (last - j, last)]) for j in range(1, half)
    ]
    held = jnp.concatenate(held, axis=0)
    pieces = jnp.stack([held[:, v * cols:(v + 1) * cols] for v in range(vocab_count)])
    teacher = lax.all_to_all(pieces, "vocab", split_axis=0, concat_axis=0, tiled=True)

    groups = [[i, i + 1] for i in range(0, chunks - 2, 2)] + [[chunks - 2], [chunks - 1]]
    moving = [None] * chunks
    students = [None] * chunks
    gathered = {}
    grads = {}
    travels = {}
    divergence = jnp.zeros((), jnp.float32)
    tie = []

    def send(i, j):
        value = (other_part if j < half else own_part)[i]
        if j > 0:
            value = value + moving[i]
        if tie:
            value = after(value, *tie)
        tie[:] = [value]
        moving[i] = hop(value, j)

    def local_stats(g):
        student = jnp.concatenate([students[i] for i in groups[g]], axis=0)
        target = jnp.concatenate([teacher[i] for i in groups[g]], axis=0).astype(jnp.float32)
        student_top = jnp.max(student, axis=1)
        target_top = jnp.max(target, axis=1)
        target_exp = jnp.exp(target - target_top[:, None])
        stats = jnp.stack([
            student_top,
            target_top,
            jnp.sum(jnp.exp(student - student_top[:, None]), axis=1),
            jnp.sum(target_exp, axis=1),
            jnp.sum(target_exp * (target - student), axis=1),
        ])
        tie.append(stats)
        stats = jnp.broadcast_to(stats, (vocab_count, *stats.shape))
        gathered[g] = lax.all_to_all(stats, "vocab", split_axis=0, concat_axis=0, tiled=True)

    def finish(g):
        stats = gathered[g]
        student = jnp.concatenate([students[i] for i in groups[g]], axis=0)
        target = jnp.concatenate([teacher[i] for i in groups[g]], axis=0).astype(jnp.float32)
        student_max = jnp.max(stats[:, 0], axis=0)
        teacher_max = jnp.max(stats[:, 1], axis=0)
        student_scale = jnp.exp(stats[:, 0] - student_max)
        teacher_scale = jnp.exp(stats[:, 1] - teacher_max)
        student_sum = jnp.sum(stats[:, 2] * student_scale, axis=0)
        teacher_sum = jnp.sum(stats[:, 3] * teacher_scale, axis=0)
        cross = jnp.sum(stats[:, 4] * teacher_scale, axis=0)
        loss = jnp.sum(
            cross / teacher_sum
            - teacher_max
            - jnp.log(teacher_sum)
            + student_max
            + jnp.log(student_sum)
        )
        grads[g] = (
            LOSS_SCALE * (
                jnp.exp(student - student_max[:, None]) / student_sum[:, None]
                - jnp.exp(target - teacher_max[:, None]) / teacher_sum[:, None]
            )
        ).astype(jnp.bfloat16)
        tie.append(grads[g])
        return loss

    ready = {g: max(members) for g, members in enumerate(groups)}
    send(0, 0)
    send(1, 0)
    for s in range(chunks + hops + 6):
        for j in range(1, hops):
            if 0 <= s - (j - 1) < chunks:
                send(s - (j - 1), j)
        if s + 2 < chunks:
            send(s + 2, 0)
        i = s - (hops - 1)
        if 0 <= i < chunks:
            students[i] = own_part[i] + moving[i]
        for g in range(len(groups)):
            if ready[g] == i:
                local_stats(g)
            if ready[g] == i - 1:
                divergence = divergence + finish(g)
    for g in range(len(groups)):
        travels[g] = [grads[g]]
        for j in range(hops):
            travels[g].append(hop(travels[g][-1], j))

    at_end = (z == 0) | (z == last)
    mean_divergence = lax.psum(jnp.where(at_end, divergence, 0.0), "seq") / total_tokens

    near = jnp.minimum(z, last - z)
    first, second = [], []
    for g in range(len(groups)):
        own, other = travels[g][0], travels[g][hops]
        for j in range(1, half):
            own = jnp.where(near == j, travels[g][j], own)
            other = jnp.where(near == j, travels[g][hops - j], other)
        first.append(own)
        second.append(other)
    all_grads = jnp.concatenate(first + second, axis=0)

    feature = jnp.dot(all_grads, head_rows, preferred_element_type=jnp.float32)
    feature = feature.reshape(2, vocab_count, half, per_dev, rows).transpose(0, 2, 1, 3, 4)
    feature = feature.reshape(2, half, own_tokens, rows)
    low = jnp.where(low_side, feature[0], feature[1])
    high = jnp.where(low_side, feature[1], feature[0])
    feature = jnp.concatenate([low, high[::-1]])
    if vocab_count % seq_count == 0:
        share = vocab_count // seq_count
        out_cols = rows // share
        feature = feature.reshape(seq_count, own_tokens, share, out_cols).transpose(0, 2, 1, 3)
        feature = feature.reshape(vocab_count, own_tokens, out_cols)
        feature = lax.all_to_all(feature, "vocab", split_axis=0, concat_axis=0, tiled=True)
        feature = jnp.sum(feature, axis=0)
        pairs = [
            ((dst * share + b) * seq_count + src, (src * share + b) * seq_count + dst)
            for src in range(seq_count) for dst in range(seq_count) for b in range(share)
        ]
        hidden_grad = lax.ppermute(feature, ("vocab", "seq"), pairs)
    else:
        feature = lax.all_to_all(feature, "seq", split_axis=0, concat_axis=2, tiled=True)
        hidden_grad = lax.psum_scatter(feature[0], "vocab", scatter_dimension=1, tiled=True)
    head_part = lax.dot_general(
        all_grads, ordered, (((0,), (0,)), ((), ())), preferred_element_type=jnp.float32
    ).T
    return (mean_divergence, hidden_grad, head_part)


def solution(mesh):
    in_specs = (P("seq", None), P("seq", "vocab"), P("seq", "vocab", None))
    out_specs = (P(), P("seq", "vocab"), P("seq", "vocab"))
    return jax.shard_map(body, mesh=mesh, in_specs=in_specs, out_specs=out_specs, check_vma=False)
```

time: 486 us -> 411 us (0.85)
  waiting for transfers between devices: 175 us -> 105 us
  blocking collectives: 77.6 us -> 11.2 us
  starting transfers between devices: 102 us -> 156 us
  other arithmetic: 60.6 us -> 78.6 us
  local copies, waits for them, and re-layouts: 24.4 us -> 9.06 us
  Pallas kernels: 0 us -> 15 us
  matrix products: 35.7 us -> 24.4 us
    all_gather x8 -> x0, blocking collectives: 68.8 us -> none  [body(): stats = lax.all_gather(stats, 'vocab', axis=0)]
    ppermute x40 -> x42, waiting for transfers between devices: 146 us -> 102 us  [the longest x39 76.3 us: hop(): return lax.ppermute(value, 'seq', [(last - j, last - j - 1), (j, j + 1)])]
    ppermute x40 -> x42, starting transfers between devices: 83.9 us -> 122 us  [the longest x39 115 us: hop(): return lax.ppermute(value, 'seq', [(last - j, last - j - 1), (j, j + 1)])]
    add x3 -> x22, other arithmetic: 3.88 us -> 28.9 us  [the longest x16 23.1 us: send(): value = value + moving[i]]
    unnamed x9 -> x16, other arithmetic: 8.23 us -> 24.9 us
    reduce_max x33 -> x24, other arithmetic: 21.1 us -> 4.7 us  [the longest x9 2.47 us: local_stats(): target_top = jnp.max(target, axis=1)]
    all_to_all x1 -> x5, starting transfers between devices: 4.87 us -> 21 us  [local_stats(): lax.all_to_all(stats, 'vocab', split_axis=0, concat_axis=0, tiled=True)]
    pallas_call x0 -> x1, Pallas kernels: none -> 15 us  [partial_students(): pl.pallas_call(partial_kernel, grid=(pl.cdiv(cols, tile),), in_specs=[pl....]
  transfers between devices with their start and end apart: 45 -> 51, of which waited for: 28 -> 11; matrix products, arithmetic and copies ran while one was open for 13% -> 23% of each run, Pallas kernels for 0% -> 4%
where the time goes in v2:
time: 411 us; the launch traced here: 406 us
  starting transfers between devices  156 us (38%)
  waiting for transfers between devices  105 us (26%)
  other arithmetic  78.6 us (19%)
  matrix products  24.4 us (6%)
  Pallas kernels  15 us (4%)
  blocking collectives  11.2 us (3%)
  local copies, waits for them, and re-layouts  9.06 us (2%)
  between operations  6.61 us (2%)
    ppermute x39, starting transfers between devices, hop(): return lax.ppermute(value, 'seq', [(last - j, last - j - 1), (j, j + 1)])  115 us
    ppermute x39, waiting for transfers between devices, hop(): return lax.ppermute(value, 'seq', [(last - j, last - j - 1), (j, j + 1)])  76.3 us
    ppermute x3, waiting for transfers between devices, body(): lax.ppermute(piece, 'seq', [(d, (d + k) % seq_count) for d in range(seq_c...  25.6 us
    unnamed x16, other arithmetic  24.9 us
    add x16, other arithmetic, send(): value = value + moving[i]  23.1 us
    all_to_all x5, starting transfers between devices, local_stats(): lax.all_to_all(stats, 'vocab', split_axis=0, concat_axis=0, tiled=True)  21 us
    dot_general x1, matrix products, body(): lax.dot_general(all_grads, ordered, (((0,), (0,)), ((), ())), preferred_e...  15 us
    pallas_call x1, Pallas kernels, partial_students(): pl.pallas_call(partial_kernel, grid=(pl.cdiv(cols, tile),), in_specs=[pl....  15 us
  transfers between devices with their start and end apart: 51, of which 11 were waited for; matrix products, arithmetic and copies ran while one was open for 23% of the time, Pallas kernels for 4%

profile of v2, /device:TPU:2, one launch (start us, length us, event | category | flops | bytes accessed | tf_op | source)
XLA Modules:
  0.0 405.6 jit_solution(14591599917088230292)
XLA Ops:
  10.9 25.6 %collective-permute-done.2 = bf16[64,640]{1,0:T(8,128)(2,1)S(1)} collective-permute-done((bf16[64,640]{1,0:T(8,128)(2,1)S(1)}, bf16[64,640]{1,0:T(8,128)(2,1)S(1)}, u32[]{:S(2)}, u32[]{:S(2)}) %collective-permute-start.2) | collective-permute-done | bytes 81952 | tf_op jit(solution)/shard_map/ppermute | solution.py:69
  36.7 15.0 %shard_map.58 = (f32[16,9496]{1,0:T(8,128)S(1)}, f32[16,9496]{1,0:T(8,128)S(1)}, f32[16,9496]{1,0:T(8,128)S(1)}, f32[16,9496]{1,0:T(8,128)S(1)}, f32[16,9496]{1,...) custom-call(bf16[256,640]{1,0:T(8,128)(2,1)S(1)} %bitcast.166, ...), custom_call_target="tpu_custom_call" | custom-call | flops 3111649280 | bytes 21878784 | tf_op jit(solution)/shard_map/pallas_call | solution.py:30
  70.2 4.3 %all-to-all-start = ((bf16[8,16,9496]{2,1,0:T(8,128)(2,1)}), bf16[8,16,9496]{2,1,0:T(8,128)(2,1)}, u32[]{:S(2)}, u32[]{:S(2)}) async-start(bf16[8,16,9496]{2,1,0:T(8,128)(2,1)} %fusion.58), calls=%async_computation | async-start | bytes 4915200 | tf_op jit(solution)/shard_map/all_to_all | solution.py:88
  83.8 12.7 %collective-permute-start.12 = (f32[16,9496]{1,0:T(8,128)S(1)}, f32[16,9496]{1,0:T(8,128)S(1)}, u32[]{:S(2)}, u32[]{:S(2)}) collective-permute-start(f32[16,9496]{1,0:T(8,128)S(1)} %copy-done.26), channel_id=1, source_target_pairs={{3,2},{0,1},{7,6},{4,5},{11,10},{8,9},{15,14},{12,13},{19,18},{16,... | collective-permute-start | bytes 1823240 | tf_op jit(solution)/shard_map/ppermute | solution.py:63
  98.4 11.1 %collective-permute-start.15 = (f32[16,9496]{1,0:T(8,128)S(1)}, f32[16,9496]{1,0:T(8,128)S(1)}, u32[]{:S(2)}, u32[]{:S(2)}) collective-permute-start(f32[16,9496]{1,0:T(8,128)S(1)} %copy-done.25), channel_id=1, source_target_pairs={{3,2},{0,1},{7,6},{4,5},{11,10},{8,9},{15,14},{12,13},{19,18},{16,... | collective-permute-start | bytes 1823240 | tf_op jit(solution)/shard_map/ppermute | solution.py:63
  113.9 9.1 %collective-permute-start.18 = (f32[16,9496]{1,0:T(8,128)}, f32[16,9496]{1,0:T(8,128)}, u32[]{:S(2)}, u32[]{:S(2)}) collective-permute-start(f32[16,9496]{1,0:T(8,128)} %get-tuple-element.63), channel_id=1, source_target_pairs={{3,2},{0,1},{7,6},{4,5},{11,10},{8,9},{15,14},{12,13},{19,18},{16,... | collective-permute-start | bytes 1823240 | tf_op jit(solution)/shard_map/ppermute | solution.py:63
  130.1 11.6 %collective-permute-done.6 = f32[16,9496]{1,0:T(8,128)} collective-permute-done((f32[16,9496]{1,0:T(8,128)}, f32[16,9496]{1,0:T(8,128)}, u32[]{:S(2)}, u32[]{:S(2)}) %collective-permute-start.6) | collective-permute-done | bytes 607776 | tf_op jit(solution)/shard_map/ppermute | solution.py:63
  145.2 7.5 %collective-permute-done.13 = f32[16,9496]{1,0:T(8,128)} collective-permute-done((f32[16,9496]{1,0:T(8,128)}, f32[16,9496]{1,0:T(8,128)}, u32[]{:S(2)}, u32[]{:S(2)}) %collective-permute-start.13) | collective-permute-done | bytes 607776 | tf_op jit(solution)/shard_map/ppermute | solution.py:63
  161.1 4.2 %all-to-all-start.1 = ((f32[8,1,160]{2,1,0:T(1,128)}), f32[8,1,160]{2,1,0:T(1,128)S(1)}, u32[]{:S(2)}, u32[]{:S(2)}) async-start(f32[8,1,160]{2,1,0:T(1,128)} %reshape.143), calls=%async_computation.1 | async-start | bytes 16384 | tf_op jit(solution)/shard_map/all_to_all | solution.py:123
  168.1 6.2 %collective-permute-start.21 = (f32[16,9496]{1,0:T(8,128)}, f32[16,9496]{1,0:T(8,128)}, u32[]{:S(2)}, u32[]{:S(2)}) collective-permute-start(f32[16,9496]{1,0:T(8,128)} %get-tuple-element.68), channel_id=1, source_target_pairs={{3,2},{0,1},{7,6},{4,5},{11,10},{8,9},{15,14},{12,13},{19,18},{16,... | collective-permute-start | bytes 1823240 | tf_op jit(solution)/shard_map/ppermute | solution.py:63
  180.0 5.0 %collective-permute-done.16 = f32[16,9496]{1,0:T(8,128)} collective-permute-done((f32[16,9496]{1,0:T(8,128)}, f32[16,9496]{1,0:T(8,128)}, u32[]{:S(2)}, u32[]{:S(2)}) %collective-permute-start.16) | collective-permute-done | bytes 607776 | tf_op jit(solution)/shard_map/ppermute | solution.py:63
  187.7 4.2 %all-to-all-start.2 = ((f32[8,1,160]{2,1,0:T(1,128)}), f32[8,1,160]{2,1,0:T(1,128)S(1)}, u32[]{:S(2)}, u32[]{:S(2)}) async-start(f32[8,1,160]{2,1,0:T(1,128)} %reshape.145), calls=%async_computation.2 | async-start | bytes 16384 | tf_op jit(solution)/shard_map/all_to_all | solution.py:123
  197.4 6.2 %collective-permute-start.24 = (f32[16,9496]{1,0:T(8,128)}, f32[16,9496]{1,0:T(8,128)}, u32[]{:S(2)}, u32[]{:S(2)}) collective-permute-start(f32[16,9496]{1,0:T(8,128)} %get-tuple-element.73), channel_id=1, source_target_pairs={{3,2},{0,1},{7,6},{4,5},{11,10},{8,9},{15,14},{12,13},{19,18},{16,... | collective-permute-start | bytes 1823240 | tf_op jit(solution)/shard_map/ppermute | solution.py:63
  212.0 5.4 %collective-permute-start.29 = (bf16[32,9496]{1,0:T(8,128)(2,1)}, bf16[32,9496]{1,0:T(8,128)(2,1)}, u32[]{:S(2)}, u32[]{:S(2)}) collective-permute-start(bf16[32,9496]{1,0:T(8,128)(2,1)} %fusion.25), channel_id=1, source_target_pairs={{3,2},{0,1},{7,6},{4,5},{11,10},{8,9},{15,14},{12,13},{19,18},{16,... | collective-permute-start | bytes 1823240 | tf_op jit(solution)/shard_map/ppermute | solution.py:63
  246.9 12.8 %collective-permute-start.30 = (bf16[32,9496]{1,0:T(8,128)(2,1)}, bf16[32,9496]{1,0:T(8,128)(2,1)S(1)}, u32[]{:S(2)}, u32[]{:S(2)}) collective-permute-start(bf16[32,9496]{1,0:T(8,128)(2,1)} %fusion.24), channel_id=1, source_target_pairs={{3,2},{0,1},{7,6},{4,5},{11,10},{8,9},{15,14},{12,13},{19,18},{16,... | collective-permute-start | bytes 1823240 | tf_op jit(solution)/shard_map/ppermute | solution.py:63
  261.1 24.5 %collective-permute-done.27 = f32[16,9496]{1,0:T(8,128)S(1)} collective-permute-done((f32[16,9496]{1,0:T(8,128)S(1)}, f32[16,9496]{1,0:T(8,128)S(1)}, u32[]{:S(2)}, u32[]{:S(2)}) %collective-permute-start.27) | collective-permute-done | bytes 607776 | tf_op jit(solution)/shard_map/ppermute | solution.py:63
  288.3 4.2 %all-to-all-start.4 = ((f32[8,5,16]{2,1,0:T(8,128)}), f32[8,5,16]{2,1,0:T(8,128)S(1)}, u32[]{:S(2)}, u32[]{:S(2)}) async-start(f32[8,5,16]{2,1,0:T(8,128)} %broadcast_in_dim.13), calls=%async_computation.4 | async-start | bytes 65536 | tf_op jit(solution)/shard_map/all_to_all | solution.py:123
  306.5 7.2 %collective-permute-start.32 = (bf16[16,9496]{1,0:T(8,128)(2,1)S(1)}, bf16[16,9496]{1,0:T(8,128)(2,1)S(1)}, u32[]{:S(2)}, u32[]{:S(2)}) collective-permute-start(bf16[16,9496]{1,0:T(8,128)(2,1)S(1)} %get-tuple-element.114), channel_id=1, source_target_pairs={{3,2},{0,1},{7,6},{4,5},{11,10},{8,9},{15,14},{12,13},{19,18},{16,... | collective-permute-start | bytes 911624 | tf_op jit(solution)/shard_map/ppermute | solution.py:63
  322.0 5.0 %collective-permute-done.31 = bf16[16,9496]{1,0:T(8,128)(2,1)S(1)} collective-permute-done((bf16[16,9496]{1,0:T(8,128)(2,1)S(1)}, bf16[16,9496]{1,0:T(8,128)(2,1)S(1)}, u32[]{:S(2)}, u32[]{:S(2)}) %collective-permute-start.31) | collective-permute-done | bytes 303904 | tf_op jit(solution)/shard_map/ppermute | solution.py:63
  335.9 16.0 %collective-permute-done.40 = bf16[16,9496]{1,0:T(8,128)(2,1)S(1)} collective-permute-done((bf16[16,9496]{1,0:T(8,128)(2,1)S(1)}, bf16[16,9496]{1,0:T(8,128)(2,1)S(1)}, u32[]{:S(2)}, u32[]{:S(2)}) %collective-permute-start.40) | collective-permute-done | bytes 303904 | tf_op jit(solution)/shard_map/ppermute | solution.py:63
  353.6 9.4 %fusion.73 = f32[256,640]{1,0:T(8,128)S(1)} fusion(bf16[256,9496]{1,0:T(8,128)(2,1)} %select_dynamic-update-slice_fusion.6, bf16[640,9496]{0,1:T(8,128)(2,1)} %param.4), kind=kOutput, calls=%fused_computation.187 | convolution fusion | flops 3111649280 | bytes 17672192 | tf_op jit(solution)/shard_map/dot_general | solution.py:188
  364.2 4.3 %all-to-all-start.6 = ((f32[8,64,320]{2,1,0:T(8,128)}), f32[8,64,320]{2,1,0:T(8,128)S(1)}, u32[]{:S(2)}, u32[]{:S(2)}) async-start(f32[8,64,320]{2,1,0:T(8,128)} %bitcast.85), calls=%async_computation.6 | async-start | bytes 1572864 | tf_op jit(solution)/shard_map/all_to_all | solution.py:199
  374.8 11.2 %psum.7 = f32[]{:T(128)} all-reduce(f32[]{:T(128)S(6)} %select_n.158), channel_id=1, replica_groups=mesh['vocab'=8,'seq'=4] {'seq'}, use_global_device_ids=true, to_apply=%region_55.56 | all-reduce | flops 1 | bytes 8 | tf_op jit(solution)/shard_map/psum | solution.py:175
  388.8 15.0 %fusion.74 = f32[640,9496]{0,1:T(8,128)} fusion(bf16[256,640]{1,0:T(8,128)(2,1)S(1)} %bitcast.167, bf16[256,9496]{1,0:T(8,128)(2,1)} %select_dynamic-update-slice_fusion.6), kind=kOutput, calls=%fused_computation.188 | convolution fusion | flops 3111649280 | bytes 29499392 | tf_op jit(solution)/shard_map/dot_general | solution.py:209
  (266 shorter events, 161.3 us)
Async XLA Ops:
  0.6 55.5 %collective-permute-start.10 = (bf16[8,75968]{1,0:T(8,128)(2,1)}, bf16[8,75968]{1,0:T(8,128)(2,1)}, u32[]{:S(2)}, u32[]{:S(2)}) collective-permute-start(bf16[8,75968]{1,0:T(8,128)(2,1)} %bitcast.168), channel_id=1, source_target_pairs={{1,0},{2,3},{5,4},{6,7},{9,8},{10,11},{13,12},{14,15},{17,16},{18,... | collective-permute-start | bytes 3646472 | tf_op jit(solution)/shard_map/ppermute | solution.py:84
  6.7 29.8 %collective-permute-start.2 = (bf16[64,640]{1,0:T(8,128)(2,1)S(1)}, bf16[64,640]{1,0:T(8,128)(2,1)S(1)}, u32[]{:S(2)}, u32[]{:S(2)}) collective-permute-start(bf16[64,640]{1,0:T(8,128)(2,1)S(1)} %get-tuple-element.130), channel_id=1, source_target_pairs={{0,3},{1,0},{2,1},{3,2},{4,7},{5,4},{6,5},{7,6},{8,11},{9,8},{10,9... | collective-permute-start | bytes 245768 | tf_op jit(solution)/shard_map/ppermute | solution.py:69
  6.9 29.6 %collective-permute-start.1 = (bf16[64,640]{1,0:T(8,128)(2,1)S(1)}, bf16[64,640]{1,0:T(8,128)(2,1)S(1)}, u32[]{:S(2)}, u32[]{:S(2)}) collective-permute-start(bf16[64,640]{1,0:T(8,128)(2,1)S(1)} %get-tuple-element.131), channel_id=1, source_target_pairs={{0,2},{1,3},{2,0},{3,1},{4,6},{5,7},{6,4},{7,5},{8,10},{9,11},{10,... | collective-permute-start | bytes 245768 | tf_op jit(solution)/shard_map/ppermute | solution.py:69
  51.7 22.9 %collective-permute-start.3 = (f32[16,9496]{1,0:T(8,128)}, f32[16,9496]{1,0:T(8,128)}, u32[]{:S(2)}, u32[]{:S(2)}) collective-permute-start(f32[16,9496]{1,0:T(8,128)} %get-tuple-element.43), channel_id=1, source_target_pairs={{3,2},{0,1},{7,6},{4,5},{11,10},{8,9},{15,14},{12,13},{19,18},{16,... | collective-permute-start | bytes 1823240 | tf_op jit(solution)/shard_map/ppermute | solution.py:63
  54.0 26.8 %collective-permute-start.5 = (f32[16,9496]{1,0:T(8,128)}, f32[16,9496]{1,0:T(8,128)}, u32[]{:S(2)}, u32[]{:S(2)}) collective-permute-start(f32[16,9496]{1,0:T(8,128)} %get-tuple-element.45), channel_id=1, source_target_pairs={{3,2},{0,1},{7,6},{4,5},{11,10},{8,9},{15,14},{12,13},{19,18},{16,... | collective-permute-start | bytes 1823240 | tf_op jit(solution)/shard_map/ppermute | solution.py:63
  70.2 85.6 %all-to-all-start = ((bf16[8,16,9496]{2,1,0:T(8,128)(2,1)}), bf16[8,16,9496]{2,1,0:T(8,128)(2,1)}, u32[]{:S(2)}, u32[]{:S(2)}) async-start(bf16[8,16,9496]{2,1,0:T(8,128)(2,1)} %fusion.58), calls=%async_computation | async-start | bytes 4915200 | tf_op jit(solution)/shard_map/all_to_all | solution.py:88
  83.8 28.3 %collective-permute-start.12 = (f32[16,9496]{1,0:T(8,128)S(1)}, f32[16,9496]{1,0:T(8,128)S(1)}, u32[]{:S(2)}, u32[]{:S(2)}) collective-permute-start(f32[16,9496]{1,0:T(8,128)S(1)} %copy-done.26), channel_id=1, source_target_pairs={{3,2},{0,1},{7,6},{4,5},{11,10},{8,9},{15,14},{12,13},{19,18},{16,... | collective-permute-start | bytes 1823240 | tf_op jit(solution)/shard_map/ppermute | solution.py:63
  98.4 25.9 %collective-permute-start.15 = (f32[16,9496]{1,0:T(8,128)S(1)}, f32[16,9496]{1,0:T(8,128)S(1)}, u32[]{:S(2)}, u32[]{:S(2)}) collective-permute-start(f32[16,9496]{1,0:T(8,128)S(1)} %copy-done.25), channel_id=1, source_target_pairs={{3,2},{0,1},{7,6},{4,5},{11,10},{8,9},{15,14},{12,13},{19,18},{16,... | collective-permute-start | bytes 1823240 | tf_op jit(solution)/shard_map/ppermute | solution.py:63
  110.8 30.9 %collective-permute-start.6 = (f32[16,9496]{1,0:T(8,128)}, f32[16,9496]{1,0:T(8,128)}, u32[]{:S(2)}, u32[]{:S(2)}) collective-permute-start(f32[16,9496]{1,0:T(8,128)} %add.198), channel_id=1, source_target_pairs={{1,0},{2,3},{5,4},{6,7},{9,8},{10,11},{13,12},{14,15},{17,16},{18,... | collective-permute-start | bytes 1823240 | tf_op jit(solution)/shard_map/ppermute | solution.py:63
  113.9 29.1 %collective-permute-start.18 = (f32[16,9496]{1,0:T(8,128)}, f32[16,9496]{1,0:T(8,128)}, u32[]{:S(2)}, u32[]{:S(2)}) collective-permute-start(f32[16,9496]{1,0:T(8,128)} %get-tuple-element.63), channel_id=1, source_target_pairs={{3,2},{0,1},{7,6},{4,5},{11,10},{8,9},{15,14},{12,13},{19,18},{16,... | collective-permute-start | bytes 1823240 | tf_op jit(solution)/shard_map/ppermute | solution.py:63
  123.0 29.7 %collective-permute-start.13 = (f32[16,9496]{1,0:T(8,128)}, f32[16,9496]{1,0:T(8,128)}, u32[]{:S(2)}, u32[]{:S(2)}) collective-permute-start(f32[16,9496]{1,0:T(8,128)} %add.206), channel_id=1, source_target_pairs={{1,0},{2,3},{5,4},{6,7},{9,8},{10,11},{13,12},{14,15},{17,16},{18,... | collective-permute-start | bytes 1823240 | tf_op jit(solution)/shard_map/ppermute | solution.py:63
  125.2 28.7 %collective-permute-start.14 = (f32[16,9496]{1,0:T(8,128)}, f32[16,9496]{1,0:T(8,128)}, u32[]{:S(2)}, u32[]{:S(2)}) collective-permute-start(f32[16,9496]{1,0:T(8,128)} %add.207), channel_id=1, source_target_pairs={{2,1},{1,2},{6,5},{5,6},{10,9},{9,10},{14,13},{13,14},{18,17},{17,... | collective-permute-start | bytes 1823240 | tf_op jit(solution)/shard_map/ppermute | solution.py:63
  165.3 28.8 %collective-permute-start.17 = (f32[16,9496]{1,0:T(8,128)}, f32[16,9496]{1,0:T(8,128)}, u32[]{:S(2)}, u32[]{:S(2)}) collective-permute-start(f32[16,9496]{1,0:T(8,128)} %add.210), channel_id=1, source_target_pairs={{2,1},{1,2},{6,5},{5,6},{10,9},{9,10},{14,13},{13,14},{18,17},{17,... | collective-permute-start | bytes 1823240 | tf_op jit(solution)/shard_map/ppermute | solution.py:63
  168.1 35.5 %collective-permute-start.21 = (f32[16,9496]{1,0:T(8,128)}, f32[16,9496]{1,0:T(8,128)}, u32[]{:S(2)}, u32[]{:S(2)}) collective-permute-start(f32[16,9496]{1,0:T(8,128)} %get-tuple-element.68), channel_id=1, source_target_pairs={{3,2},{0,1},{7,6},{4,5},{11,10},{8,9},{15,14},{12,13},{19,18},{16,... | collective-permute-start | bytes 1823240 | tf_op jit(solution)/shard_map/ppermute | solution.py:63
  178.3 29.7 %collective-permute-start.20 = (f32[16,9496]{1,0:T(8,128)}, f32[16,9496]{1,0:T(8,128)}, u32[]{:S(2)}, u32[]{:S(2)}) collective-permute-start(f32[16,9496]{1,0:T(8,128)} %add.216), channel_id=1, source_target_pairs={{2,1},{1,2},{6,5},{5,6},{10,9},{9,10},{14,13},{13,14},{18,17},{17,... | collective-permute-start | bytes 1823240 | tf_op jit(solution)/shard_map/ppermute | solution.py:63
  196.2 28.6 %collective-permute-start.19 = (f32[16,9496]{1,0:T(8,128)}, f32[16,9496]{1,0:T(8,128)}, u32[]{:S(2)}, u32[]{:S(2)}) collective-permute-start(f32[16,9496]{1,0:T(8,128)} %add.215), channel_id=1, source_target_pairs={{1,0},{2,3},{5,4},{6,7},{9,8},{10,11},{13,12},{14,15},{17,16},{18,... | collective-permute-start | bytes 1823240 | tf_op jit(solution)/shard_map/ppermute | solution.py:63
  197.4 23.6 %collective-permute-start.24 = (f32[16,9496]{1,0:T(8,128)}, f32[16,9496]{1,0:T(8,128)}, u32[]{:S(2)}, u32[]{:S(2)}) collective-permute-start(f32[16,9496]{1,0:T(8,128)} %get-tuple-element.73), channel_id=1, source_target_pairs={{3,2},{0,1},{7,6},{4,5},{11,10},{8,9},{15,14},{12,13},{19,18},{16,... | collective-permute-start | bytes 1823240 | tf_op jit(solution)/shard_map/ppermute | solution.py:63
  205.6 30.5 %collective-permute-start.23 = (f32[16,9496]{1,0:T(8,128)}, f32[16,9496]{1,0:T(8,128)}, u32[]{:S(2)}, u32[]{:S(2)}) collective-permute-start(f32[16,9496]{1,0:T(8,128)} %add.219), channel_id=1, source_target_pairs={{2,1},{1,2},{6,5},{5,6},{10,9},{9,10},{14,13},{13,14},{18,17},{17,... | collective-permute-start | bytes 1823240 | tf_op jit(solution)/shard_map/ppermute | solution.py:63
  212.0 28.8 %collective-permute-start.29 = (bf16[32,9496]{1,0:T(8,128)(2,1)}, bf16[32,9496]{1,0:T(8,128)(2,1)}, u32[]{:S(2)}, u32[]{:S(2)}) collective-permute-start(bf16[32,9496]{1,0:T(8,128)(2,1)} %fusion.25), channel_id=1, source_target_pairs={{3,2},{0,1},{7,6},{4,5},{11,10},{8,9},{15,14},{12,13},{19,18},{16,... | collective-permute-start | bytes 1823240 | tf_op jit(solution)/shard_map/ppermute | solution.py:63
  239.4 89.9 %collective-permute-start.34 = (bf16[32,9496]{1,0:T(8,128)(2,1)}, bf16[32,9496]{1,0:T(8,128)(2,1)}, u32[]{:S(2)}, u32[]{:S(2)}) collective-permute-start(bf16[32,9496]{1,0:T(8,128)(2,1)} %collective-permute-done.33), channel_id=1, source_target_pairs={{1,0},{2,3},{5,4},{6,7},{9,8},{10,11},{13,12},{14,15},{17,16},{18,... | collective-permute-start | bytes 1823240 | tf_op jit(solution)/shard_map/ppermute | solution.py:63
  240.7 53.8 %collective-permute-start.35 = (bf16[32,9496]{1,0:T(8,128)(2,1)}, bf16[32,9496]{1,0:T(8,128)(2,1)}, u32[]{:S(2)}, u32[]{:S(2)}) collective-permute-start(bf16[32,9496]{1,0:T(8,128)(2,1)} %collective-permute-done.29), channel_id=1, source_target_pairs={{2,1},{1,2},{6,5},{5,6},{10,9},{9,10},{14,13},{13,14},{18,17},{17,... | collective-permute-start | bytes 1823240 | tf_op jit(solution)/shard_map/ppermute | solution.py:63
  244.3 41.3 %collective-permute-start.27 = (f32[16,9496]{1,0:T(8,128)S(1)}, f32[16,9496]{1,0:T(8,128)S(1)}, u32[]{:S(2)}, u32[]{:S(2)}) collective-permute-start(f32[16,9496]{1,0:T(8,128)S(1)} %add.230), channel_id=1, source_target_pairs={{1,0},{2,3},{5,4},{6,7},{9,8},{10,11},{13,12},{14,15},{17,16},{18,... | collective-permute-start | bytes 1823240 | tf_op jit(solution)/shard_map/ppermute | solution.py:63
  246.9 48.9 %collective-permute-start.30 = (bf16[32,9496]{1,0:T(8,128)(2,1)}, bf16[32,9496]{1,0:T(8,128)(2,1)S(1)}, u32[]{:S(2)}, u32[]{:S(2)}) collective-permute-start(bf16[32,9496]{1,0:T(8,128)(2,1)} %fusion.24), channel_id=1, source_target_pairs={{3,2},{0,1},{7,6},{4,5},{11,10},{8,9},{15,14},{12,13},{19,18},{16,... | collective-permute-start | bytes 1823240 | tf_op jit(solution)/shard_map/ppermute | solution.py:63
  294.5 36.9 %collective-permute-start.36 = (bf16[32,9496]{1,0:T(8,128)(2,1)}, bf16[32,9496]{1,0:T(8,128)(2,1)S(1)}, u32[]{:S(2)}, u32[]{:S(2)}) collective-permute-start(bf16[32,9496]{1,0:T(8,128)(2,1)} %collective-permute-done.35), channel_id=1, source_target_pairs={{1,0},{2,3},{5,4},{6,7},{9,8},{10,11},{13,12},{14,15},{17,16},{18,... | collective-permute-start | bytes 1823240 | tf_op jit(solution)/shard_map/ppermute | solution.py:63
  (57 other events, 584.2 us)

commit v3 on v2

--- a/solution.py
+++ b/solution.py
@@ -76,38 +76,51 @@
             [blocks[(z - (end + step * j)) % seq_count] for j in range(half)], axis=1))
     ordered = jnp.stack(sides).reshape(total_tokens, rows)
     head_rows = head_weight.T
-    partial = partial_students(ordered, head_rows, chunk)
-    own_part, other_part = partial[:chunks], partial[chunks:]
-
-    mine = teacher_logits[0]
+    half_tokens = total_tokens // 2
+
+    mine, ordered = lax.optimization_barrier((teacher_logits[0], ordered))
     held = [mine] + [
         lax.ppermute(mine, "seq", [(j, 0), (last - j, last)]) for j in range(1, half)
     ]
     held = jnp.concatenate(held, axis=0)
-    pieces = jnp.stack([held[:, v * cols:(v + 1) * cols] for v in range(vocab_count)])
-    teacher = lax.all_to_all(pieces, "vocab", split_axis=0, concat_axis=0, tiled=True)
 
     groups = [[i, i + 1] for i in range(0, chunks - 2, 2)] + [[chunks - 2], [chunks - 1]]
     moving = [None] * chunks
     students = [None] * chunks
+    targets = []
     gathered = {}
-    grads = {}
     travels = {}
-    divergence = jnp.zeros((), jnp.float32)
+    losses = []
     tie = []
 
+    def tied(value):
+        value = after(value, *tie) if tie else value
+        tie[:] = [value]
+        return value
+
     def send(i, j):
-        value = (other_part if j < half else own_part)[i]
-        if j > 0:
-            value = value + moving[i]
-        if tie:
-            value = after(value, *tie)
-        tie[:] = [value]
+        part = (other_part if j < half else own_part)[i]
+        if j == 0:
+            value = tied(part)
+        else:
+            value = part + tied(moving[i])
+            tie[:] = [value]
         moving[i] = hop(value, j)
 
+    def exchange_teacher():
+        rows_held = tied(held)
+        pieces = jnp.stack([rows_held[:, v * cols:(v + 1) * cols] for v in range(vocab_count)])
+        tie[:] = [pieces]
+        targets.extend(
+            lax.all_to_all(pieces, "vocab", split_axis=0, concat_axis=0, tiled=True))
+
+    def group_rows(g):
+        student = jnp.concatenate([students[i] for i in groups[g]], axis=0)
+        target = jnp.concatenate([targets[i] for i in groups[g]], axis=0)
+        return student, target.astype(jnp.float32)
+
     def local_stats(g):
-        student = jnp.concatenate([students[i] for i in groups[g]], axis=0)
-        target = jnp.concatenate([teacher[i] for i in groups[g]], axis=0).astype(jnp.float32)
+        student, target = group_rows(g)
         student_top = jnp.max(student, axis=1)
         target_top = jnp.max(target, axis=1)
         target_exp = jnp.exp(target - target_top[:, None])
@@ -118,14 +131,13 @@
             jnp.sum(target_exp, axis=1),
             jnp.sum(target_exp * (target - student), axis=1),
         ])
-        tie.append(stats)
+        tie[:] = [stats]
         stats = jnp.broadcast_to(stats, (vocab_count, *stats.shape))
         gathered[g] = lax.all_to_all(stats, "vocab", split_axis=0, concat_axis=0, tiled=True)
 
     def finish(g):
-        stats = gathered[g]
-        student = jnp.concatenate([students[i] for i in groups[g]], axis=0)
-        target = jnp.concatenate([teacher[i] for i in groups[g]], axis=0).astype(jnp.float32)
+        stats = tied(gathered[g])
+        student, target = group_rows(g)
         student_max = jnp.max(stats[:, 0], axis=0)
         teacher_max = jnp.max(stats[:, 1], axis=0)
         student_scale = jnp.exp(stats[:, 0] - student_max)
@@ -133,46 +145,69 @@
         student_sum = jnp.sum(stats[:, 2] * student_scale, axis=0)
         teacher_sum = jnp.sum(stats[:, 3] * teacher_scale, axis=0)
         cross = jnp.sum(stats[:, 4] * teacher_scale, axis=0)
-        loss = jnp.sum(
-            cross / teacher_sum
-            - teacher_max
-            - jnp.log(teacher_sum)
-            + student_max
-            + jnp.log(student_sum)
-        )
-        grads[g] = (
+        losses.append(jnp.stack([cross, teacher_sum, teacher_max, student_max, student_sum]))
+        grad = (
             LOSS_SCALE * (
                 jnp.exp(student - student_max[:, None]) / student_sum[:, None]
                 - jnp.exp(target - teacher_max[:, None]) / teacher_sum[:, None]
             )
         ).astype(jnp.bfloat16)
-        tie.append(grads[g])
-        return loss
-
-    ready = {g: max(members) for g, members in enumerate(groups)}
-    send(0, 0)
-    send(1, 0)
-    for s in range(chunks + hops + 6):
-        for j in range(1, hops):
-            if 0 <= s - (j - 1) < chunks:
-                send(s - (j - 1), j)
-        if s + 2 < chunks:
-            send(s + 2, 0)
-        i = s - (hops - 1)
-        if 0 <= i < chunks:
-            students[i] = own_part[i] + moving[i]
-        for g in range(len(groups)):
-            if ready[g] == i:
-                local_stats(g)
-            if ready[g] == i - 1:
-                divergence = divergence + finish(g)
-    for g in range(len(groups)):
-        travels[g] = [grads[g]]
+        tie[:] = [grad]
+        travels[g] = [grad]
+
+    def send_grad(g, j):
+        value = travels[g][j] if j == 0 else tied(travels[g][j])
+        travels[g].append(hop(value, j))
+
+    lag = 2
+    sums_end = chunks - 1 + lag * (hops - 1)
+    slots = {}
+
+    def plan(slot, order, call, *args):
+        slots.setdefault(slot, []).append((order, len(slots[slot]) if slot in slots else 0, call, args))
+
+    for i in range(chunks):
         for j in range(hops):
-            travels[g].append(hop(travels[g][-1], j))
-
+            plan(i + lag * j, j, send, i, j)
+    plan(1, 50, exchange_teacher)
+    for g, members in enumerate(groups):
+        arrived = max(members) + lag * hops
+        plan(arrived, 20, local_stats, g)
+        slot = arrived + 1
+        plan(slot, 30, finish, g)
+        for j in range(hops):
+            plan(slot, 40 + j, send_grad, g, j)
+            slot += lag if slot < sums_end else 1
+
+    def sum_up(i):
+        students[i] = own_part[i] + tied(moving[i])
+        tie[:] = [students[i]]
+
+    for i in range(chunks):
+        plan(i + lag * hops, 10, sum_up, i)
+
+    partial = partial_students(ordered[half_tokens:], head_rows, chunk)
+    other_part = list(partial)
+    own_part = None
+    for slot in sorted(slots):
+        for _, _, call, args in sorted(slots[slot], key=lambda e: e[:2]):
+            call(*args)
+        if own_part is None:
+            own_part = list(partial_students(tied(ordered[:half_tokens]), head_rows, chunk))
+            tie[:] = [own_part[0]]
+
+    cross, teacher_sum, teacher_max, student_max, student_sum = jnp.concatenate(losses, axis=1)
+    divergence = jnp.sum(
+        cross / teacher_sum
+        - teacher_max
+        - jnp.log(teacher_sum)
+        + student_max
+        + jnp.log(student_sum)
+    )
     at_end = (z == 0) | (z == last)
-    mean_divergence = lax.psum(jnp.where(at_end, divergence, 0.0), "seq") / total_tokens
+    divergence = tied(jnp.where(at_end, divergence, 0.0))
+    mean_divergence = lax.psum(divergence, "seq") / total_tokens
+    tie[:] = [mean_divergence]
 
     near = jnp.minimum(z, last - z)
     first, second = [], []
@@ -183,9 +218,19 @@
             other = jnp.where(near == j, travels[g][hops - j], other)
         first.append(own)
         second.append(other)
-    all_grads = jnp.concatenate(first + second, axis=0)
-
-    feature = jnp.dot(all_grads, head_rows, preferred_element_type=jnp.float32)
+    early = len(groups) - 2
+    early_rows = sum(len(members) for members in groups[:early]) * chunk
+    early_grads = jnp.concatenate(first[:early] + second[:early], axis=0)
+    late_grads = jnp.concatenate(first[early:] + second[early:], axis=0)
+    feature_early = jnp.dot(early_grads, head_rows, preferred_element_type=jnp.float32)
+    late_grads = tied(late_grads)
+    feature_late = jnp.dot(late_grads, head_rows, preferred_element_type=jnp.float32)
+    feature = jnp.concatenate(
+        [feature_early.reshape(2, -1, rows), feature_late.reshape(2, -1, rows)], axis=1)
+    both = ordered.reshape(2, half_tokens, rows)
+    matching = jnp.concatenate([
+        both[:, :early_rows].reshape(-1, rows), both[:, early_rows:].reshape(-1, rows)])
+    all_grads = jnp.concatenate([early_grads, late_grads])
     feature = feature.reshape(2, vocab_count, half, per_dev, rows).transpose(0, 2, 1, 3, 4)
     feature = feature.reshape(2, half, own_tokens, rows)
     low = jnp.where(low_side, feature[0], feature[1])
@@ -207,7 +252,7 @@
         feature = lax.all_to_all(feature, "seq", split_axis=0, concat_axis=2, tiled=True)
         hidden_grad = lax.psum_scatter(feature[0], "vocab", scatter_dimension=1, tiled=True)
     head_part = lax.dot_general(
-        all_grads, ordered, (((0,), (0,)), ((), ())), preferred_element_type=jnp.float32
+        all_grads, matching, (((0,), (0,)), ((), ())), preferred_element_type=jnp.float32
     ).T
     return (mean_divergence, hidden_grad, head_part)
 

time: 411 us -> 383 us (0.932)
  waiting for transfers between devices: 105 us -> 76.3 us
  Pallas kernels: 15 us -> 27 us
  local copies, waits for them, and re-layouts: 9.06 us -> 20.1 us
  starting transfers between devices: 156 us -> 146 us
  other arithmetic: 78.6 us -> 70.8 us
    ppermute x39, waiting for transfers between devices: 76.3 us -> 55.3 us  [hop(): return lax.ppermute(value, 'seq', [(last - j, last - j - 1), (j, j + 1)])]
    ppermute x3, waiting for transfers between devices: 25.6 us -> 6.69 us  [body(): lax.ppermute(piece, 'seq', [(d, (d + k) % seq_count) for d in range(seq_c...]
    unnamed x16 -> x7, other arithmetic: 24.9 us -> 11.2 us
    pallas_call x1 -> x2, Pallas kernels: 15 us -> 27 us  [partial_students(): pl.pallas_call(partial_kernel, grid=(pl.cdiv(cols, tile),), in_specs=[pl....]
    all_to_all x1, waiting for transfers between devices: 0.01 us -> 9.99 us  [body(): lax.all_to_all(feature, 'vocab', split_axis=0, concat_axis=0, tiled=True)]
    ppermute x39, starting transfers between devices: 115 us -> 106 us  [hop(): return lax.ppermute(value, 'seq', [(last - j, last - j - 1), (j, j + 1)])]
    unnamed x67 -> x97, local copies, waits for them, and re-layouts: 5.91 us -> 13.9 us
    add x22, other arithmetic: 28.9 us -> 33.1 us  [the longest x16 25.3 us: send(): value = part + tied(moving[i])]
  transfers between devices with their start and end apart: 51 -> 51, of which waited for: 11 -> 14; matrix products, arithmetic and copies ran while one was open for 23% -> 25% of each run, Pallas kernels for 4% -> 7%
where the time goes in v3:
time: 383 us; the launch traced here: 380 us
  starting transfers between devices  146 us (38%)
  waiting for transfers between devices  76.3 us (20%)
  other arithmetic  70.8 us (18%)
  Pallas kernels  27 us (7%)
  matrix products  24.9 us (7%)
  local copies, waits for them, and re-layouts  20.1 us (5%)
  blocking collectives  11 us (3%)
  between operations  4.18 us (1%)
    ppermute x39, starting transfers between devices, hop(): return lax.ppermute(value, 'seq', [(last - j, last - j - 1), (j, j + 1)])  106 us
    ppermute x39, waiting for transfers between devices, hop(): return lax.ppermute(value, 'seq', [(last - j, last - j - 1), (j, j + 1)])  55.3 us
    pallas_call x2, Pallas kernels, partial_students(): pl.pallas_call(partial_kernel, grid=(pl.cdiv(cols, tile),), in_specs=[pl....  27 us
    add x16, other arithmetic, send(): value = part + tied(moving[i])  25.3 us
    all_to_all x5, starting transfers between devices, local_stats(): lax.all_to_all(stats, 'vocab', split_axis=0, concat_axis=0, tiled=True)  21.6 us
    dot_general x1, matrix products, body(): lax.dot_general(all_grads, matching, (((0,), (0,)), ((), ())), preferred_...  15 us
    unnamed x97, local copies, waits for them, and re-layouts  13.9 us
    unnamed x7, other arithmetic  11.2 us
  transfers between devices with their start and end apart: 51, of which 14 were waited for; matrix products, arithmetic and copies ran while one was open for 25% of the time, Pallas kernels for 7%

profile of v3, /device:TPU:2, one launch (start us, length us, event | category | flops | bytes accessed | tf_op | source)
XLA Modules:
  0.0 380.2 jit_solution(17590551373393628774)
XLA Ops:
  15.7 13.0 %shard_map.58 = (f32[16,9496]{1,0:T(8,128)S(1)}, f32[16,9496]{1,0:T(8,128)S(1)}, f32[16,9496]{1,0:T(8,128)S(1)}, f32[16,9496]{1,0:T(8,128)S(1)}, f32[16,9496]{1,...) custom-call(bf16[128,640]{1,0:T(8,128)(2,1)S(1)} %get-tuple-element.205.hidden_ref, ...), custom_call_target="tpu_custom_call" | custom-call | flops 1555824640 | bytes 17016832 | tf_op jit(solution)/shard_map/pallas_call | solution.py:30
  28.7 14.0 %shard_map.59 = (f32[16,9496]{1,0:T(8,128)S(1)}, f32[16,9496]{1,0:T(8,128)S(1)}, f32[16,9496]{1,0:T(8,128)S(1)}, f32[16,9496]{1,0:T(8,128)S(1)}, f32[16,9496]{1,...) custom-call(bf16[128,640]{1,0:T(8,128)(2,1)S(1)} %get-tuple-element.73.hidden_ref, ...), custom_call_target="tpu_custom_call" | custom-call | flops 1555824640 | bytes 17016832 | tf_op jit(solution)/shard_map/pallas_call | solution.py:30
  51.7 5.1 %all-to-all-start = ((bf16[8,16,9496]{2,1,0:T(8,128)(2,1)}), bf16[8,16,9496]{2,1,0:T(8,128)(2,1)}, u32[]{:S(2)}, u32[]{:S(2)}) async-start(bf16[8,16,9496]{2,1,0:T(8,128)(2,1)} %bitcast_dynamic-update-slice_fusion), calls=%async_computation | async-start | bytes 4915200 | tf_op jit(solution)/shard_map/all_to_all | solution.py:115
  63.2 11.8 %collective-permute-done.3 = f32[16,9496]{1,0:T(8,128)S(1)} collective-permute-done((f32[16,9496]{1,0:T(8,128)}, f32[16,9496]{1,0:T(8,128)S(1)}, u32[]{:S(2)}, u32[]{:S(2)}) %collective-permute-start.3) | collective-permute-done | bytes 607776 | tf_op jit(solution)/shard_map/ppermute | solution.py:63
  77.0 6.5 %collective-permute-start.12 = (f32[16,9496]{1,0:T(8,128)S(1)}, f32[16,9496]{1,0:T(8,128)S(1)}, u32[]{:S(2)}, u32[]{:S(2)}) collective-permute-start(f32[16,9496]{1,0:T(8,128)S(1)} %copy-done.12), channel_id=1, source_target_pairs={{3,2},{0,1},{7,6},{4,5},{11,10},{8,9},{15,14},{12,13},{19,18},{16,... | collective-permute-start | bytes 1823240 | tf_op jit(solution)/shard_map/ppermute | solution.py:63
  83.5 4.6 %collective-permute-done.7 = f32[16,9496]{1,0:T(8,128)S(1)} collective-permute-done((f32[16,9496]{1,0:T(8,128)}, f32[16,9496]{1,0:T(8,128)S(1)}, u32[]{:S(2)}, u32[]{:S(2)}) %collective-permute-start.7) | collective-permute-done | bytes 607776 | tf_op jit(solution)/shard_map/ppermute | solution.py:63
  89.1 6.5 %collective-permute-start.10 = (f32[16,9496]{1,0:T(8,128)S(1)}, f32[16,9496]{1,0:T(8,128)S(1)}, u32[]{:S(2)}, u32[]{:S(2)}) collective-permute-start(f32[16,9496]{1,0:T(8,128)S(1)} %copy-done.10), channel_id=1, source_target_pairs={{3,2},{0,1},{7,6},{4,5},{11,10},{8,9},{15,14},{12,13},{19,18},{16,... | collective-permute-start | bytes 1823240 | tf_op jit(solution)/shard_map/ppermute | solution.py:63
  95.6 5.7 %collective-permute-done.6 = f32[16,9496]{1,0:T(8,128)S(1)} collective-permute-done((f32[16,9496]{1,0:T(8,128)}, f32[16,9496]{1,0:T(8,128)S(1)}, u32[]{:S(2)}, u32[]{:S(2)}) %collective-permute-start.6) | collective-permute-done | bytes 607776 | tf_op jit(solution)/shard_map/ppermute | solution.py:63
  105.9 8.4 %collective-permute-done.12 = f32[16,9496]{1,0:T(8,128)S(1)} collective-permute-done((f32[16,9496]{1,0:T(8,128)S(1)}, f32[16,9496]{1,0:T(8,128)S(1)}, u32[]{:S(2)}, u32[]{:S(2)}) %collective-permute-start.12) | collective-permute-done | bytes 607776 | tf_op jit(solution)/shard_map/ppermute | solution.py:63
  114.4 5.2 %collective-permute-start.15 = (f32[16,9496]{1,0:T(8,128)}, f32[16,9496]{1,0:T(8,128)}, u32[]{:S(2)}, u32[]{:S(2)}) collective-permute-start(f32[16,9496]{1,0:T(8,128)} %get-tuple-element.93), channel_id=1, source_target_pairs={{3,2},{0,1},{7,6},{4,5},{11,10},{8,9},{15,14},{12,13},{19,18},{16,... | collective-permute-start | bytes 1823240 | tf_op jit(solution)/shard_map/ppermute | solution.py:63
  123.0 4.6 %collective-permute-done.10 = f32[16,9496]{1,0:T(8,128)S(1)} collective-permute-done((f32[16,9496]{1,0:T(8,128)S(1)}, f32[16,9496]{1,0:T(8,128)S(1)}, u32[]{:S(2)}, u32[]{:S(2)}) %collective-permute-start.10) | collective-permute-done | bytes 607776 | tf_op jit(solution)/shard_map/ppermute | solution.py:63
  136.2 7.6 %collective-permute-start.18 = (f32[16,9496]{1,0:T(8,128)}, f32[16,9496]{1,0:T(8,128)}, u32[]{:S(2)}, u32[]{:S(2)}) collective-permute-start(f32[16,9496]{1,0:T(8,128)} %get-tuple-element.96), channel_id=1, source_target_pairs={{3,2},{0,1},{7,6},{4,5},{11,10},{8,9},{15,14},{12,13},{19,18},{16,... | collective-permute-start | bytes 1823240 | tf_op jit(solution)/shard_map/ppermute | solution.py:63
  166.6 8.5 %collective-permute-start.21 = (f32[16,9496]{1,0:T(8,128)S(1)}, f32[16,9496]{1,0:T(8,128)}, u32[]{:S(2)}, u32[]{:S(2)}) collective-permute-start(f32[16,9496]{1,0:T(8,128)S(1)} %copy-done.8), channel_id=1, source_target_pairs={{3,2},{0,1},{7,6},{4,5},{11,10},{8,9},{15,14},{12,13},{19,18},{16,... | collective-permute-start | bytes 1823240 | tf_op jit(solution)/shard_map/ppermute | solution.py:63
  202.0 8.5 %collective-permute-start.26 = (bf16[32,9496]{1,0:T(8,128)(2,1)}, bf16[32,9496]{1,0:T(8,128)(2,1)}, u32[]{:S(2)}, u32[]{:S(2)}) collective-permute-start(bf16[32,9496]{1,0:T(8,128)(2,1)} %fusion.26), channel_id=1, source_target_pairs={{3,2},{0,1},{7,6},{4,5},{11,10},{8,9},{15,14},{12,13},{19,18},{16,... | collective-permute-start | bytes 1823240 | tf_op jit(solution)/shard_map/ppermute | solution.py:63
  217.5 6.1 %collective-permute-start.30 = (bf16[32,9496]{1,0:T(8,128)(2,1)}, bf16[32,9496]{1,0:T(8,128)(2,1)}, u32[]{:S(2)}, u32[]{:S(2)}) collective-permute-start(bf16[32,9496]{1,0:T(8,128)(2,1)} %fusion.25), channel_id=1, source_target_pairs={{3,2},{0,1},{7,6},{4,5},{11,10},{8,9},{15,14},{12,13},{19,18},{16,... | collective-permute-start | bytes 1823240 | tf_op jit(solution)/shard_map/ppermute | solution.py:63
  244.6 6.7 %collective-permute-start.32 = (bf16[32,9496]{1,0:T(8,128)(2,1)}, bf16[32,9496]{1,0:T(8,128)(2,1)S(1)}, u32[]{:S(2)}, u32[]{:S(2)}) collective-permute-start(bf16[32,9496]{1,0:T(8,128)(2,1)} %fusion.24), channel_id=1, source_target_pairs={{3,2},{0,1},{7,6},{4,5},{11,10},{8,9},{15,14},{12,13},{19,18},{16,... | collective-permute-start | bytes 1823240 | tf_op jit(solution)/shard_map/ppermute | solution.py:63
  252.0 4.7 %all-to-all-start.4 = ((f32[8,5,16]{2,1,0:T(8,128)}), f32[8,5,16]{2,1,0:T(8,128)S(1)}, u32[]{:S(2)}, u32[]{:S(2)}) async-start(f32[8,5,16]{2,1,0:T(8,128)} %broadcast_in_dim.26), calls=%async_computation.4 | async-start | bytes 65536 | tf_op jit(solution)/shard_map/all_to_all | solution.py:136
  278.2 7.2 %collective-permute-start.33 = (bf16[16,9496]{1,0:T(8,128)(2,1)S(1)}, bf16[16,9496]{1,0:T(8,128)(2,1)S(1)}, u32[]{:S(2)}, u32[]{:S(2)}) collective-permute-start(bf16[16,9496]{1,0:T(8,128)(2,1)S(1)} %fusion.44), channel_id=1, source_target_pairs={{3,2},{0,1},{7,6},{4,5},{11,10},{8,9},{15,14},{12,13},{19,18},{16,... | collective-permute-start | bytes 911624 | tf_op jit(solution)/shard_map/ppermute | solution.py:63
  302.9 16.1 %collective-permute-done.41 = bf16[16,9496]{1,0:T(8,128)(2,1)S(1)} collective-permute-done((bf16[16,9496]{1,0:T(8,128)(2,1)S(1)}, bf16[16,9496]{1,0:T(8,128)(2,1)S(1)}, u32[]{:S(2)}, u32[]{:S(2)}) %collective-permute-start.41) | collective-permute-done | bytes 303904 | tf_op jit(solution)/shard_map/ppermute | solution.py:63
  319.0 11.0 %psum.7 = f32[]{:T(128)} all-reduce(f32[]{:T(128)S(6)} %select_n.158), channel_id=1, replica_groups=mesh['vocab'=8,'seq'=4] {'seq'}, use_global_device_ids=true, to_apply=%region_51.52 | all-reduce | flops 1 | bytes 8 | tf_op jit(solution)/shard_map/psum | solution.py:209
  331.0 6.7 %fusion.116 = f32[64,640]{1,0:T(8,128)S(1)} fusion(bf16[64,9496]{1,0:T(8,128)(2,1)S(1)} %pad_maximum_fusion.4, bf16[640,9496]{0,1:T(8,128)(2,1)} %param.4), kind=kOutput, calls=%fused_computation.229 | convolution fusion | flops 777912320 | bytes 13534208 | tf_op jit(solution)/shard_map/dot_general | solution.py:227
  344.7 4.3 %all-to-all-start.6 = ((f32[8,64,320]{2,1,0:T(8,128)}), f32[8,64,320]{2,1,0:T(8,128)S(1)}, u32[]{:S(2)}, u32[]{:S(2)}) async-start(f32[8,64,320]{2,1,0:T(8,128)} %bitcast.113), calls=%async_computation.6 | async-start | bytes 1572864 | tf_op jit(solution)/shard_map/all_to_all | solution.py:244
  350.0 10.0 %all-to-all-done.6 = f32[8,64,320]{2,1,0:T(8,128)S(1)} async-done(((f32[8,64,320]{2,1,0:T(8,128)}), f32[8,64,320]{2,1,0:T(8,128)S(1)}, u32[]{:S(2)}, u32[]{:S(2)}) %all-to-all-start.6) | async-done | bytes 655392 | tf_op jit(solution)/shard_map/all_to_all | solution.py:244
  363.5 15.0 %fusion.50 = f32[640,9496]{0,1:T(8,128)} fusion(bf16[256,9496]{1,0:T(8,128)(2,1)} %constant_dynamic-update-slice_fusion, bf16[64,640]{1,0:T(8,128)(2,1)S(1)} %bitcast.285, bf16[192,640]{1,0:T(8,128)(2,1)S(1)} %bitcast.282), kind=kOutput, calls=%fused_computation.90 | convolution fusion | flops 3112304640 | bytes 29499392 | tf_op jit(solution)/shard_map/dot_general | solution.py:254
  (300 shorter events, 178.2 us)
Async XLA Ops:
  14.4 30.2 %collective-permute-start.4 = (bf16[8,75968]{1,0:T(8,128)(2,1)S(1)}, bf16[8,75968]{1,0:T(8,128)(2,1)S(1)}, u32[]{:S(2)}, u32[]{:S(2)}) collective-permute-start(bf16[8,75968]{1,0:T(8,128)(2,1)S(1)} %bitcast.280), channel_id=1, source_target_pairs={{1,0},{2,3},{5,4},{6,7},{9,8},{10,11},{13,12},{14,15},{17,16},{18,... | collective-permute-start | bytes 3646472 | tf_op jit(solution)/shard_map/ppermute | solution.py:83
  51.7 103.7 %all-to-all-start = ((bf16[8,16,9496]{2,1,0:T(8,128)(2,1)}), bf16[8,16,9496]{2,1,0:T(8,128)(2,1)}, u32[]{:S(2)}, u32[]{:S(2)}) async-start(bf16[8,16,9496]{2,1,0:T(8,128)(2,1)} %bitcast_dynamic-update-slice_fusion), calls=%async_computation | async-start | bytes 4915200 | tf_op jit(solution)/shard_map/all_to_all | solution.py:115
  61.8 39.5 %collective-permute-start.6 = (f32[16,9496]{1,0:T(8,128)}, f32[16,9496]{1,0:T(8,128)S(1)}, u32[]{:S(2)}, u32[]{:S(2)}) collective-permute-start(f32[16,9496]{1,0:T(8,128)} %copy-done.13), channel_id=1, source_target_pairs={{3,2},{0,1},{7,6},{4,5},{11,10},{8,9},{15,14},{12,13},{19,18},{16,... | collective-permute-start | bytes 1823240 | tf_op jit(solution)/shard_map/ppermute | solution.py:63
  77.0 37.4 %collective-permute-start.12 = (f32[16,9496]{1,0:T(8,128)S(1)}, f32[16,9496]{1,0:T(8,128)S(1)}, u32[]{:S(2)}, u32[]{:S(2)}) collective-permute-start(f32[16,9496]{1,0:T(8,128)S(1)} %copy-done.12), channel_id=1, source_target_pairs={{3,2},{0,1},{7,6},{4,5},{11,10},{8,9},{15,14},{12,13},{19,18},{16,... | collective-permute-start | bytes 1823240 | tf_op jit(solution)/shard_map/ppermute | solution.py:63
  88.2 32.3 %collective-permute-start.11 = (f32[16,9496]{1,0:T(8,128)S(1)}, f32[16,9496]{1,0:T(8,128)S(1)}, u32[]{:S(2)}, u32[]{:S(2)}) collective-permute-start(f32[16,9496]{1,0:T(8,128)S(1)} %add.165), channel_id=1, source_target_pairs={{2,1},{1,2},{6,5},{5,6},{10,9},{9,10},{14,13},{13,14},{18,17},{17,... | collective-permute-start | bytes 1823240 | tf_op jit(solution)/shard_map/ppermute | solution.py:63
  89.1 38.5 %collective-permute-start.10 = (f32[16,9496]{1,0:T(8,128)S(1)}, f32[16,9496]{1,0:T(8,128)S(1)}, u32[]{:S(2)}, u32[]{:S(2)}) collective-permute-start(f32[16,9496]{1,0:T(8,128)S(1)} %copy-done.10), channel_id=1, source_target_pairs={{3,2},{0,1},{7,6},{4,5},{11,10},{8,9},{15,14},{12,13},{19,18},{16,... | collective-permute-start | bytes 1823240 | tf_op jit(solution)/shard_map/ppermute | solution.py:63
  102.2 30.3 %collective-permute-start.9 = (f32[16,9496]{1,0:T(8,128)}, f32[16,9496]{1,0:T(8,128)}, u32[]{:S(2)}, u32[]{:S(2)}) collective-permute-start(f32[16,9496]{1,0:T(8,128)} %add.166), channel_id=1, source_target_pairs={{2,1},{1,2},{6,5},{5,6},{10,9},{9,10},{14,13},{13,14},{18,17},{17,... | collective-permute-start | bytes 1823240 | tf_op jit(solution)/shard_map/ppermute | solution.py:63
  104.6 31.6 %collective-permute-start.8 = (f32[16,9496]{1,0:T(8,128)}, f32[16,9496]{1,0:T(8,128)}, u32[]{:S(2)}, u32[]{:S(2)}) collective-permute-start(f32[16,9496]{1,0:T(8,128)} %add.167), channel_id=1, source_target_pairs={{1,0},{2,3},{5,4},{6,7},{9,8},{10,11},{13,12},{14,15},{17,16},{18,... | collective-permute-start | bytes 1823240 | tf_op jit(solution)/shard_map/ppermute | solution.py:63
  114.4 30.6 %collective-permute-start.15 = (f32[16,9496]{1,0:T(8,128)}, f32[16,9496]{1,0:T(8,128)}, u32[]{:S(2)}, u32[]{:S(2)}) collective-permute-start(f32[16,9496]{1,0:T(8,128)} %get-tuple-element.93), channel_id=1, source_target_pairs={{3,2},{0,1},{7,6},{4,5},{11,10},{8,9},{15,14},{12,13},{19,18},{16,... | collective-permute-start | bytes 1823240 | tf_op jit(solution)/shard_map/ppermute | solution.py:63
  120.5 27.9 %collective-permute-start.14 = (f32[16,9496]{1,0:T(8,128)}, f32[16,9496]{1,0:T(8,128)}, u32[]{:S(2)}, u32[]{:S(2)}) collective-permute-start(f32[16,9496]{1,0:T(8,128)} %add.168), channel_id=1, source_target_pairs={{2,1},{1,2},{6,5},{5,6},{10,9},{9,10},{14,13},{13,14},{18,17},{17,... | collective-permute-start | bytes 1823240 | tf_op jit(solution)/shard_map/ppermute | solution.py:63
  132.6 44.7 %collective-permute-start.17 = (f32[16,9496]{1,0:T(8,128)}, f32[16,9496]{1,0:T(8,128)}, u32[]{:S(2)}, u32[]{:S(2)}) collective-permute-start(f32[16,9496]{1,0:T(8,128)} %add.170), channel_id=1, source_target_pairs={{2,1},{1,2},{6,5},{5,6},{10,9},{9,10},{14,13},{13,14},{18,17},{17,... | collective-permute-start | bytes 1823240 | tf_op jit(solution)/shard_map/ppermute | solution.py:63
  136.2 30.4 %collective-permute-start.18 = (f32[16,9496]{1,0:T(8,128)}, f32[16,9496]{1,0:T(8,128)}, u32[]{:S(2)}, u32[]{:S(2)}) collective-permute-start(f32[16,9496]{1,0:T(8,128)} %get-tuple-element.96), channel_id=1, source_target_pairs={{3,2},{0,1},{7,6},{4,5},{11,10},{8,9},{15,14},{12,13},{19,18},{16,... | collective-permute-start | bytes 1823240 | tf_op jit(solution)/shard_map/ppermute | solution.py:63
  145.0 35.8 %collective-permute-start.16 = (f32[16,9496]{1,0:T(8,128)}, f32[16,9496]{1,0:T(8,128)}, u32[]{:S(2)}, u32[]{:S(2)}) collective-permute-start(f32[16,9496]{1,0:T(8,128)} %add.171), channel_id=1, source_target_pairs={{1,0},{2,3},{5,4},{6,7},{9,8},{10,11},{13,12},{14,15},{17,16},{18,... | collective-permute-start | bytes 1823240 | tf_op jit(solution)/shard_map/ppermute | solution.py:63
  148.4 41.7 %collective-permute-start.20 = (f32[16,9496]{1,0:T(8,128)}, f32[16,9496]{1,0:T(8,128)}, u32[]{:S(2)}, u32[]{:S(2)}) collective-permute-start(f32[16,9496]{1,0:T(8,128)} %add.173), channel_id=1, source_target_pairs={{2,1},{1,2},{6,5},{5,6},{10,9},{9,10},{14,13},{13,14},{18,17},{17,... | collective-permute-start | bytes 1823240 | tf_op jit(solution)/shard_map/ppermute | solution.py:63
  151.9 40.2 %collective-permute-start.19 = (f32[16,9496]{1,0:T(8,128)}, f32[16,9496]{1,0:T(8,128)}, u32[]{:S(2)}, u32[]{:S(2)}) collective-permute-start(f32[16,9496]{1,0:T(8,128)} %add.174), channel_id=1, source_target_pairs={{1,0},{2,3},{5,4},{6,7},{9,8},{10,11},{13,12},{14,15},{17,16},{18,... | collective-permute-start | bytes 1823240 | tf_op jit(solution)/shard_map/ppermute | solution.py:63
  177.3 34.0 %collective-permute-start.23 = (f32[16,9496]{1,0:T(8,128)}, f32[16,9496]{1,0:T(8,128)}, u32[]{:S(2)}, u32[]{:S(2)}) collective-permute-start(f32[16,9496]{1,0:T(8,128)} %add.176), channel_id=1, source_target_pairs={{2,1},{1,2},{6,5},{5,6},{10,9},{9,10},{14,13},{13,14},{18,17},{17,... | collective-permute-start | bytes 1823240 | tf_op jit(solution)/shard_map/ppermute | solution.py:63
  180.8 32.5 %collective-permute-start.22 = (f32[16,9496]{1,0:T(8,128)}, f32[16,9496]{1,0:T(8,128)}, u32[]{:S(2)}, u32[]{:S(2)}) collective-permute-start(f32[16,9496]{1,0:T(8,128)} %add.177), channel_id=1, source_target_pairs={{1,0},{2,3},{5,4},{6,7},{9,8},{10,11},{13,12},{14,15},{17,16},{18,... | collective-permute-start | bytes 1823240 | tf_op jit(solution)/shard_map/ppermute | solution.py:63
  199.2 29.3 %collective-permute-start.24 = (f32[16,9496]{1,0:T(8,128)}, f32[16,9496]{1,0:T(8,128)}, u32[]{:S(2)}, u32[]{:S(2)}) collective-permute-start(f32[16,9496]{1,0:T(8,128)} %add.180), channel_id=1, source_target_pairs={{1,0},{2,3},{5,4},{6,7},{9,8},{10,11},{13,12},{14,15},{17,16},{18,... | collective-permute-start | bytes 1823240 | tf_op jit(solution)/shard_map/ppermute | solution.py:63
  217.5 33.8 %collective-permute-start.30 = (bf16[32,9496]{1,0:T(8,128)(2,1)}, bf16[32,9496]{1,0:T(8,128)(2,1)}, u32[]{:S(2)}, u32[]{:S(2)}) collective-permute-start(bf16[32,9496]{1,0:T(8,128)(2,1)} %fusion.25), channel_id=1, source_target_pairs={{3,2},{0,1},{7,6},{4,5},{11,10},{8,9},{15,14},{12,13},{19,18},{16,... | collective-permute-start | bytes 1823240 | tf_op jit(solution)/shard_map/ppermute | solution.py:63
  223.7 33.8 %collective-permute-start.29 = (bf16[32,9496]{1,0:T(8,128)(2,1)}, bf16[32,9496]{1,0:T(8,128)(2,1)}, u32[]{:S(2)}, u32[]{:S(2)}) collective-permute-start(bf16[32,9496]{1,0:T(8,128)(2,1)} %collective-permute-done.26), channel_id=1, source_target_pairs={{2,1},{1,2},{6,5},{5,6},{10,9},{9,10},{14,13},{13,14},{18,17},{17,... | collective-permute-start | bytes 1823240 | tf_op jit(solution)/shard_map/ppermute | solution.py:63
  227.2 30.4 %collective-permute-start.28 = (f32[16,9496]{1,0:T(8,128)}, f32[16,9496]{1,0:T(8,128)}, u32[]{:S(2)}, u32[]{:S(2)}) collective-permute-start(f32[16,9496]{1,0:T(8,128)} %add.184), channel_id=1, source_target_pairs={{1,0},{2,3},{5,4},{6,7},{9,8},{10,11},{13,12},{14,15},{17,16},{18,... | collective-permute-start | bytes 1823240 | tf_op jit(solution)/shard_map/ppermute | solution.py:63
  244.6 29.0 %collective-permute-start.32 = (bf16[32,9496]{1,0:T(8,128)(2,1)}, bf16[32,9496]{1,0:T(8,128)(2,1)S(1)}, u32[]{:S(2)}, u32[]{:S(2)}) collective-permute-start(bf16[32,9496]{1,0:T(8,128)(2,1)} %fusion.24), channel_id=1, source_target_pairs={{3,2},{0,1},{7,6},{4,5},{11,10},{8,9},{15,14},{12,13},{19,18},{16,... | collective-permute-start | bytes 1823240 | tf_op jit(solution)/shard_map/ppermute | solution.py:63
  292.1 45.6 %collective-permute-start.40 = (bf16[32,9496]{1,0:T(8,128)(2,1)}, bf16[32,9496]{1,0:T(8,128)(2,1)S(1)}, u32[]{:S(2)}, u32[]{:S(2)}) collective-permute-start(bf16[32,9496]{1,0:T(8,128)(2,1)} %collective-permute-done.34), channel_id=1, source_target_pairs={{1,0},{2,3},{5,4},{6,7},{9,8},{10,11},{13,12},{14,15},{17,16},{18,... | collective-permute-start | bytes 1823240 | tf_op jit(solution)/shard_map/ppermute | solution.py:63
  301.6 29.1 %collective-permute-start.42 = (bf16[16,9496]{1,0:T(8,128)(2,1)S(1)}, bf16[16,9496]{1,0:T(8,128)(2,1)S(1)}, u32[]{:S(2)}, u32[]{:S(2)}) collective-permute-start(bf16[16,9496]{1,0:T(8,128)(2,1)S(1)} %collective-permute-done.36), channel_id=1, source_target_pairs={{1,0},{2,3},{5,4},{6,7},{9,8},{10,11},{13,12},{14,15},{17,16},{18,... | collective-permute-start | bytes 911624 | tf_op jit(solution)/shard_map/ppermute | solution.py:63
  (70 other events, 796.4 us)

commit v4 on v3

--- a/solution.py
+++ b/solution.py
@@ -14,9 +14,7 @@
 
 
 def partial_kernel(hidden_ref, head_ref, *out_refs):
-    product = lax.dot_general(
-        hidden_ref[...], head_ref[...], (((1,), (1,)), ((), ())),
-        preferred_element_type=jnp.float32)
+    product = jnp.dot(head_ref[...], hidden_ref[...], preferred_element_type=jnp.float32).T
     height = out_refs[0].shape[0]
     for i, out_ref in enumerate(out_refs):
         out_ref[...] = product[i * height:(i + 1) * height]
@@ -31,7 +29,7 @@
         partial_kernel,
         grid=(pl.cdiv(cols, tile),),
         in_specs=[
-            pl.BlockSpec((tokens, rows), lambda i: (0, 0)),
+            pl.BlockSpec((rows, tokens), lambda i: (0, 0)),
             pl.BlockSpec((tile, rows), lambda i: (i, 0)),
         ],
         out_specs=[pl.BlockSpec((chunk, tile), lambda i: (0, i))] * count,
@@ -41,7 +39,7 @@
             flops=2 * tokens * rows * cols,
             bytes_accessed=2 * rows * cols + 4 * tokens * cols,
             transcendentals=0),
-    )(hidden, head_rows)
+    )(hidden.T, head_rows)
 
 
 def body(hidden_states, head_weight, teacher_logits):
@@ -84,7 +82,9 @@
     ]
     held = jnp.concatenate(held, axis=0)
 
-    groups = [[i, i + 1] for i in range(0, chunks - 2, 2)] + [[chunks - 2], [chunks - 1]]
+    groups = [list(range(i, min(i + 3, chunks - 2))) for i in range(0, chunks - 2, 3)]
+    groups.append([chunks - 2, chunks - 1])
+    loads = [[members] for members in groups[:-1]] + [[[i] for i in groups[-1]]]
     moving = [None] * chunks
     students = [None] * chunks
     targets = []
@@ -114,13 +114,13 @@
         targets.extend(
             lax.all_to_all(pieces, "vocab", split_axis=0, concat_axis=0, tiled=True))
 
-    def group_rows(g):
-        student = jnp.concatenate([students[i] for i in groups[g]], axis=0)
-        target = jnp.concatenate([targets[i] for i in groups[g]], axis=0)
+    def rows_of(members):
+        student = jnp.concatenate([students[i] for i in members], axis=0)
+        target = jnp.concatenate([targets[i] for i in members], axis=0)
         return student, target.astype(jnp.float32)
 
     def local_stats(g):
-        student, target = group_rows(g)
+        student, target = rows_of(groups[g])
         student_top = jnp.max(student, axis=1)
         target_top = jnp.max(target, axis=1)
         target_exp = jnp.exp(target - target_top[:, None])
@@ -137,7 +137,6 @@
 
     def finish(g):
         stats = tied(gathered[g])
-        student, target = group_rows(g)
         student_max = jnp.max(stats[:, 0], axis=0)
         teacher_max = jnp.max(stats[:, 1], axis=0)
         student_scale = jnp.exp(stats[:, 0] - student_max)
@@ -146,91 +145,109 @@
         teacher_sum = jnp.sum(stats[:, 3] * teacher_scale, axis=0)
         cross = jnp.sum(stats[:, 4] * teacher_scale, axis=0)
         losses.append(jnp.stack([cross, teacher_sum, teacher_max, student_max, student_sum]))
-        grad = (
-            LOSS_SCALE * (
-                jnp.exp(student - student_max[:, None]) / student_sum[:, None]
-                - jnp.exp(target - teacher_max[:, None]) / teacher_sum[:, None]
-            )
-        ).astype(jnp.bfloat16)
-        tie[:] = [grad]
-        travels[g] = [grad]
-
-    def send_grad(g, j):
-        value = travels[g][j] if j == 0 else tied(travels[g][j])
-        travels[g].append(hop(value, j))
-
-    lag = 2
-    sums_end = chunks - 1 + lag * (hops - 1)
-    slots = {}
-
-    def plan(slot, order, call, *args):
-        slots.setdefault(slot, []).append((order, len(slots[slot]) if slot in slots else 0, call, args))
-
-    for i in range(chunks):
-        for j in range(hops):
-            plan(i + lag * j, j, send, i, j)
-    plan(1, 50, exchange_teacher)
-    for g, members in enumerate(groups):
-        arrived = max(members) + lag * hops
-        plan(arrived, 20, local_stats, g)
-        slot = arrived + 1
-        plan(slot, 30, finish, g)
-        for j in range(hops):
-            plan(slot, 40 + j, send_grad, g, j)
-            slot += lag if slot < sums_end else 1
+        start = 0
+        for p, members in enumerate(loads[g]):
+            student, target = rows_of(members)
+            at = slice(start, start + len(members) * chunk)
+            start = at.stop
+            grad = (
+                LOSS_SCALE * (
+                    jnp.exp(student - student_max[at, None]) / student_sum[at, None]
+                    - jnp.exp(target - teacher_max[at, None]) / teacher_sum[at, None]
+                )
+            ).astype(jnp.bfloat16)
+            tie[:] = [grad]
+            travels[g, p] = [grad]
+
+    def send_grad(g, p, j):
+        value = travels[g, p][j] if j == 0 else tied(travels[g, p][j])
+        travels[g, p].append(hop(value, j))
 
     def sum_up(i):
         students[i] = own_part[i] + tied(moving[i])
         tie[:] = [students[i]]
 
+    def loss():
+        cross, teacher_sum, teacher_max, student_max, student_sum = tied(
+            jnp.concatenate(losses, axis=1))
+        divergence = jnp.sum(
+            cross / teacher_sum
+            - teacher_max
+            - jnp.log(teacher_sum)
+            + student_max
+            + jnp.log(student_sum)
+        )
+        at_end = (z == 0) | (z == last)
+        total = lax.psum(jnp.where(at_end, divergence, 0.0), "seq")
+        tie[:] = [total]
+        return total / total_tokens
+
+    near = jnp.minimum(z, last - z)
+
+    def arrived(keys):
+        first, second = [], []
+        for key in keys:
+            own, other = travels[key][0], travels[key][hops]
+            for j in range(1, half):
+                own = jnp.where(near == j, travels[key][j], own)
+                other = jnp.where(near == j, travels[key][hops - j], other)
+            first.append(own)
+            second.append(other)
+        return jnp.concatenate(first + second, axis=0)
+
+    slots = {}
+
+    def plan(slot, order, call, *args):
+        slots.setdefault(slot, []).append((order, len(slots.get(slot, ())), call, args))
+
     for i in range(chunks):
-        plan(i + lag * hops, 10, sum_up, i)
-
-    partial = partial_students(ordered[half_tokens:], head_rows, chunk)
-    other_part = list(partial)
+        plan(i - 1, 5, send, i, 0)
+        for j in range(1, hops):
+            plan(i + j, j, send, i, j)
+        plan(i + hops, 4, sum_up, i)
+    plan(1, 50, exchange_teacher)
+    keys = []
+    for g, members in enumerate(groups):
+        slot = max(members) + hops
+        plan(slot, 20, local_stats, g)
+        slot += 1
+        plan(slot, 30, finish, g)
+        for p in range(len(loads[g])):
+            keys.append((g, p))
+            at = slot
+            for j in range(hops):
+                plan(at, 40 + j, send_grad, g, p, j)
+                at += 2 if at < chunks + hops else 1
+
+    other_part = list(partial_students(ordered[half_tokens:], head_rows, chunk))
     own_part = None
+    final = max(slots)
+    early_keys = [key for key in keys if key[0] < len(groups) - 1]
+    late_keys = [key for key in keys if key[0] == len(groups) - 1]
     for slot in sorted(slots):
+        if slot == final:
+            mean_divergence = loss()
         for _, _, call, args in sorted(slots[slot], key=lambda e: e[:2]):
             call(*args)
         if own_part is None:
             own_part = list(partial_students(tied(ordered[:half_tokens]), head_rows, chunk))
             tie[:] = [own_part[0]]
 
-    cross, teacher_sum, teacher_max, student_max, student_sum = jnp.concatenate(losses, axis=1)
-    divergence = jnp.sum(
-        cross / teacher_sum
-        - teacher_max
-        - jnp.log(teacher_sum)
-        + student_max
-        + jnp.log(student_sum)
-    )
-    at_end = (z == 0) | (z == last)
-    divergence = tied(jnp.where(at_end, divergence, 0.0))
-    mean_divergence = lax.psum(divergence, "seq") / total_tokens
-    tie[:] = [mean_divergence]
-
-    near = jnp.minimum(z, last - z)
-    first, second = [], []
-    for g in range(len(groups)):
-        own, other = travels[g][0], travels[g][hops]
-        for j in range(1, half):
-            own = jnp.where(near == j, travels[g][j], own)
-            other = jnp.where(near == j, travels[g][hops - j], other)
-        first.append(own)
-        second.append(other)
-    early = len(groups) - 2
-    early_rows = sum(len(members) for members in groups[:early]) * chunk
-    early_grads = jnp.concatenate(first[:early] + second[:early], axis=0)
-    late_grads = jnp.concatenate(first[early:] + second[early:], axis=0)
+    early_grads = tied(arrived(early_keys))
     feature_early = jnp.dot(early_grads, head_rows, preferred_element_type=jnp.float32)
-    late_grads = tied(late_grads)
+    tie[:] = [feature_early]
+    late_grads = tied(arrived(late_keys))
     feature_late = jnp.dot(late_grads, head_rows, preferred_element_type=jnp.float32)
+    early_rows = early_grads.shape[0] // 2
     feature = jnp.concatenate(
         [feature_early.reshape(2, -1, rows), feature_late.reshape(2, -1, rows)], axis=1)
     both = ordered.reshape(2, half_tokens, rows)
     matching = jnp.concatenate([
         both[:, :early_rows].reshape(-1, rows), both[:, early_rows:].reshape(-1, rows)])
     all_grads = jnp.concatenate([early_grads, late_grads])
+    head_part = lax.dot_general(
+        all_grads, matching, (((0,), (0,)), ((), ())), preferred_element_type=jnp.float32
+    ).T
     feature = feature.reshape(2, vocab_count, half, per_dev, rows).transpose(0, 2, 1, 3, 4)
     feature = feature.reshape(2, half, own_tokens, rows)
     low = jnp.where(low_side, feature[0], feature[1])
@@ -242,6 +259,7 @@
         feature = feature.reshape(seq_count, own_tokens, share, out_cols).transpose(0, 2, 1, 3)
         feature = feature.reshape(vocab_count, own_tokens, out_cols)
         feature = lax.all_to_all(feature, "vocab", split_axis=0, concat_axis=0, tiled=True)
+        feature, head_part = lax.optimization_barrier((feature, head_part))
         feature = jnp.sum(feature, axis=0)
         pairs = [
             ((dst * share + b) * seq_count + src, (src * share + b) * seq_count + dst)
@@ -251,9 +269,6 @@
     else:
         feature = lax.all_to_all(feature, "seq", split_axis=0, concat_axis=2, tiled=True)
         hidden_grad = lax.psum_scatter(feature[0], "vocab", scatter_dimension=1, tiled=True)
-    head_part = lax.dot_general(
-        all_grads, matching, (((0,), (0,)), ((), ())), preferred_element_type=jnp.float32
-    ).T
     return (mean_divergence, hidden_grad, head_part)
 
 

time: 383 us -> 372 us (0.971)
  starting transfers between devices: 146 us -> 115 us
  waiting for transfers between devices: 76.3 us -> 105 us
  other arithmetic: 70.8 us -> 50.2 us
  blocking collectives: 11 us -> 24 us
    ppermute x39 -> x36, waiting for transfers between devices: 55.3 us -> 91 us  [hop(): return lax.ppermute(value, 'seq', [(last - j, last - j - 1), (j, j + 1)])]
    ppermute x39 -> x36, starting transfers between devices: 106 us -> 84.2 us  [hop(): return lax.ppermute(value, 'seq', [(last - j, last - j - 1), (j, j + 1)])]
    psum x1, blocking collectives: 11 us -> 24 us  [loss(): total = lax.psum(jnp.where(at_end, divergence, 0.0), 'seq')]
    unnamed x7 -> x1, other arithmetic: 11.2 us -> 0.01 us
    all_to_all x1, waiting for transfers between devices: 9.99 us -> 0.01 us  [body(): lax.all_to_all(feature, 'vocab', split_axis=0, concat_axis=0, tiled=True)]
    ppermute x1, waiting for transfers between devices: 0.01 us -> 9.28 us  [body(): hidden_grad = lax.ppermute(feature, ('vocab', 'seq'), pairs)]
    all_to_all x5 -> x3, starting transfers between devices: 21.6 us -> 12.6 us  [local_stats(): lax.all_to_all(stats, 'vocab', split_axis=0, concat_axis=0, tiled=True)]
    add x16, other arithmetic: 25.3 us -> 18.5 us  [send(): value = part + tied(moving[i])]
  transfers between devices with their start and end apart: 51 -> 46, of which waited for: 14 -> 19; matrix products, arithmetic and copies ran while one was open for 25% -> 19% of each run, Pallas kernels for 7% -> 7%
where the time goes in v4:
time: 372 us; the launch traced here: 370 us
  starting transfers between devices  115 us (31%)
  waiting for transfers between devices  105 us (28%)
  other arithmetic  50.2 us (13%)
  Pallas kernels  26.7 us (7%)
  matrix products  24.6 us (7%)
  blocking collectives  24 us (6%)
  local copies, waits for them, and re-layouts  20.3 us (5%)
  between operations  4.2 us (1%)
    ppermute x36, waiting for transfers between devices, hop(): return lax.ppermute(value, 'seq', [(last - j, last - j - 1), (j, j + 1)])  91 us
    ppermute x36, starting transfers between devices, hop(): return lax.ppermute(value, 'seq', [(last - j, last - j - 1), (j, j + 1)])  84.2 us
    pallas_call x2, Pallas kernels, partial_students(): pl.pallas_call(partial_kernel, grid=(pl.cdiv(cols, tile),), in_specs=[pl....  26.7 us
    psum x1, blocking collectives, loss(): total = lax.psum(jnp.where(at_end, divergence, 0.0), 'seq')  24 us
    add x16, other arithmetic, send(): value = part + tied(moving[i])  18.5 us
    dot_general x1, matrix products, body(): lax.dot_general(all_grads, matching, (((0,), (0,)), ((), ())), preferred_...  14.7 us
    all_to_all x3, starting transfers between devices, local_stats(): lax.all_to_all(stats, 'vocab', split_axis=0, concat_axis=0, tiled=True)  12.6 us
    unnamed x89, local copies, waits for them, and re-layouts  11.4 us
  transfers between devices with their start and end apart: 46, of which 19 were waited for; matrix products, arithmetic and copies ran while one was open for 19% of the time, Pallas kernels for 7%

profile of v4, /device:TPU:2, one launch (start us, length us, event | category | flops | bytes accessed | tf_op | source)
XLA Modules:
  0.0 369.7 jit_solution(409921424720504536)
XLA Ops:
  13.4 13.4 %shard_map.58 = (f32[16,9496]{1,0:T(8,128)S(1)}, f32[16,9496]{1,0:T(8,128)S(1)}, f32[16,9496]{1,0:T(8,128)S(1)}, f32[16,9496]{1,0:T(8,128)S(1)}, f32[16,9496]{1,...) custom-call(bf16[640,128]{1,0:T(8,128)(2,1)S(1)} %get-tuple-element.173.hidden_ref, ...), custom_call_target="tpu_custom_call" | custom-call | flops 1555824640 | bytes 17016832 | tf_op jit(solution)/shard_map/pallas_call | solution.py:28
  26.8 5.6 %collective-permute-start.3 = (f32[16,9496]{1,0:T(8,128)S(1)}, f32[16,9496]{1,0:T(8,128)S(1)}, u32[]{:S(2)}, u32[]{:S(2)}) collective-permute-start(f32[16,9496]{1,0:T(8,128)S(1)} %get-tuple-element.71), channel_id=1, source_target_pairs={{3,2},{0,1},{7,6},{4,5},{11,10},{8,9},{15,14},{12,13},{19,18},{16,... | collective-permute-start | bytes 1823240 | tf_op jit(solution)/shard_map/ppermute | solution.py:61
  32.5 13.3 %shard_map.59 = (f32[16,9496]{1,0:T(8,128)S(1)}, f32[16,9496]{1,0:T(8,128)S(1)}, f32[16,9496]{1,0:T(8,128)S(1)}, f32[16,9496]{1,0:T(8,128)S(1)}, f32[16,9496]{1,...) custom-call(bf16[640,128]{1,0:T(8,128)(2,1)S(1)} %bitcast.183, ...), custom_call_target="tpu_custom_call" | custom-call | flops 1555824640 | bytes 17016832 | tf_op jit(solution)/shard_map/pallas_call | solution.py:28
  55.6 4.8 %all-to-all-start = ((bf16[8,16,9496]{2,1,0:T(8,128)(2,1)}), bf16[8,16,9496]{2,1,0:T(8,128)(2,1)}, u32[]{:S(2)}, u32[]{:S(2)}) async-start(bf16[8,16,9496]{2,1,0:T(8,128)(2,1)} %bitcast_dynamic-update-slice_fusion), calls=%async_computation | async-start | bytes 4915200 | tf_op jit(solution)/shard_map/all_to_all | solution.py:115
  68.9 9.7 %collective-permute-done.5 = f32[16,9496]{1,0:T(8,128)S(1)} collective-permute-done((f32[16,9496]{1,0:T(8,128)}, f32[16,9496]{1,0:T(8,128)S(1)}, u32[]{:S(2)}, u32[]{:S(2)}) %collective-permute-start.5) | collective-permute-done | bytes 607776 | tf_op jit(solution)/shard_map/ppermute | solution.py:61
  81.9 7.1 %collective-permute-start.12 = (f32[16,9496]{1,0:T(8,128)S(1)}, f32[16,9496]{1,0:T(8,128)S(1)}, u32[]{:S(2)}, u32[]{:S(2)}) collective-permute-start(f32[16,9496]{1,0:T(8,128)S(1)} %copy-done.11), channel_id=1, source_target_pairs={{3,2},{0,1},{7,6},{4,5},{11,10},{8,9},{15,14},{12,13},{19,18},{16,... | collective-permute-start | bytes 1823240 | tf_op jit(solution)/shard_map/ppermute | solution.py:61
  94.0 6.2 %collective-permute-done.7 = f32[16,9496]{1,0:T(8,128)S(1)} collective-permute-done((f32[16,9496]{1,0:T(8,128)S(1)}, f32[16,9496]{1,0:T(8,128)S(1)}, u32[]{:S(2)}, u32[]{:S(2)}) %collective-permute-start.7) | collective-permute-done | bytes 607776 | tf_op jit(solution)/shard_map/ppermute | solution.py:61
  107.0 5.6 %collective-permute-done.10 = f32[16,9496]{1,0:T(8,128)S(1)} collective-permute-done((f32[16,9496]{1,0:T(8,128)S(1)}, f32[16,9496]{1,0:T(8,128)S(1)}, u32[]{:S(2)}, u32[]{:S(2)}) %collective-permute-start.10) | collective-permute-done | bytes 607776 | tf_op jit(solution)/shard_map/ppermute | solution.py:61
  112.7 4.5 %collective-permute-start.18 = (f32[16,9496]{1,0:T(8,128)}, f32[16,9496]{1,0:T(8,128)}, u32[]{:S(2)}, u32[]{:S(2)}) collective-permute-start(f32[16,9496]{1,0:T(8,128)} %get-tuple-element.97), channel_id=1, source_target_pairs={{3,2},{0,1},{7,6},{4,5},{11,10},{8,9},{15,14},{12,13},{19,18},{16,... | collective-permute-start | bytes 1823240 | tf_op jit(solution)/shard_map/ppermute | solution.py:61
  131.9 4.2 %all-to-all-start.1 = ((f32[8,1,240]{2,1,0:T(1,128)}), f32[8,1,240]{2,1,0:T(1,128)S(1)}, u32[]{:S(2)}, u32[]{:S(2)}) async-start(f32[8,1,240]{2,1,0:T(1,128)} %reshape.128), calls=%async_computation.1 | async-start | bytes 16384 | tf_op jit(solution)/shard_map/all_to_all | solution.py:136
  136.2 5.0 %collective-permute-start.21 = (f32[16,9496]{1,0:T(8,128)}, f32[16,9496]{1,0:T(8,128)}, u32[]{:S(2)}, u32[]{:S(2)}) collective-permute-start(f32[16,9496]{1,0:T(8,128)} %copy-done.6), channel_id=1, source_target_pairs={{3,2},{0,1},{7,6},{4,5},{11,10},{8,9},{15,14},{12,13},{19,18},{16,... | collective-permute-start | bytes 1823240 | tf_op jit(solution)/shard_map/ppermute | solution.py:61
  150.0 6.2 %collective-permute-start.24 = (f32[16,9496]{1,0:T(8,128)}, f32[16,9496]{1,0:T(8,128)}, u32[]{:S(2)}, u32[]{:S(2)}) collective-permute-start(f32[16,9496]{1,0:T(8,128)} %get-tuple-element.106), channel_id=1, source_target_pairs={{3,2},{0,1},{7,6},{4,5},{11,10},{8,9},{15,14},{12,13},{19,18},{16,... | collective-permute-start | bytes 1823240 | tf_op jit(solution)/shard_map/ppermute | solution.py:61
  170.6 6.3 %collective-permute-start.27 = (bf16[48,9496]{1,0:T(8,128)(2,1)}, bf16[48,9496]{1,0:T(8,128)(2,1)}, u32[]{:S(2)}, u32[]{:S(2)}) collective-permute-start(bf16[48,9496]{1,0:T(8,128)(2,1)} %fusion.21), channel_id=1, source_target_pairs={{3,2},{0,1},{7,6},{4,5},{11,10},{8,9},{15,14},{12,13},{19,18},{16,... | collective-permute-start | bytes 2734856 | tf_op jit(solution)/shard_map/ppermute | solution.py:61
  207.1 11.3 %collective-permute-done.28 = f32[16,9496]{1,0:T(8,128)} collective-permute-done((f32[16,9496]{1,0:T(8,128)}, f32[16,9496]{1,0:T(8,128)}, u32[]{:S(2)}, u32[]{:S(2)}) %collective-permute-start.28) | collective-permute-done | bytes 607776 | tf_op jit(solution)/shard_map/ppermute | solution.py:61
  233.1 5.5 %collective-permute-start.33 = (bf16[16,9496]{1,0:T(8,128)(2,1)S(1)}, bf16[16,9496]{1,0:T(8,128)(2,1)S(1)}, u32[]{:S(2)}, u32[]{:S(2)}) collective-permute-start(bf16[16,9496]{1,0:T(8,128)(2,1)S(1)} %get-tuple-element.161), channel_id=1, source_target_pairs={{3,2},{0,1},{7,6},{4,5},{11,10},{8,9},{15,14},{12,13},{19,18},{16,... | collective-permute-start | bytes 911624 | tf_op jit(solution)/shard_map/ppermute | solution.py:61
  240.0 9.2 %collective-permute-done.30 = bf16[48,9496]{1,0:T(8,128)(2,1)} collective-permute-done((bf16[48,9496]{1,0:T(8,128)(2,1)}, bf16[48,9496]{1,0:T(8,128)(2,1)}, u32[]{:S(2)}, u32[]{:S(2)}) %collective-permute-start.30) | collective-permute-done | bytes 911648 | tf_op jit(solution)/shard_map/ppermute | solution.py:61
  256.3 5.3 %collective-permute-done.32 = bf16[16,9496]{1,0:T(8,128)(2,1)S(1)} collective-permute-done((bf16[16,9496]{1,0:T(8,128)(2,1)S(1)}, bf16[16,9496]{1,0:T(8,128)(2,1)S(1)}, u32[]{:S(2)}, u32[]{:S(2)}) %collective-permute-start.32) | collective-permute-done | bytes 303904 | tf_op jit(solution)/shard_map/ppermute | solution.py:61
  263.6 24.0 %psum.7 = f32[]{:T(128)} all-reduce(f32[]{:T(128)S(6)} %select_n.150), channel_id=1, replica_groups=mesh['vocab'=8,'seq'=4] {'seq'}, use_global_device_ids=true, to_apply=%region_31.32 | all-reduce | flops 1 | bytes 8 | tf_op jit(solution)/shard_map/psum | solution.py:181
  292.9 6.9 %collective-permute-done.38 = bf16[16,9496]{1,0:T(8,128)(2,1)S(1)} collective-permute-done((bf16[16,9496]{1,0:T(8,128)(2,1)S(1)}, bf16[16,9496]{1,0:T(8,128)(2,1)S(1)}, u32[]{:S(2)}, u32[]{:S(2)}) %collective-permute-start.38) | collective-permute-done | bytes 303904 | tf_op jit(solution)/shard_map/ppermute | solution.py:61
  299.8 22.7 %collective-permute-done.39 = bf16[16,9496]{1,0:T(8,128)(2,1)S(1)} collective-permute-done((bf16[16,9496]{1,0:T(8,128)(2,1)S(1)}, bf16[16,9496]{1,0:T(8,128)(2,1)S(1)}, u32[]{:S(2)}, u32[]{:S(2)}) %collective-permute-start.39) | collective-permute-done | bytes 303904 | tf_op jit(solution)/shard_map/ppermute | solution.py:61
  324.6 7.9 %fusion.66 = f32[192,640]{1,0:T(8,128)S(1)} fusion(bf16[192,9496]{1,0:T(8,128)(2,1)S(1)} %pad_maximum_fusion, bf16[640,9496]{0,1:T(8,128)(2,1)} %param.4), kind=kOutput, calls=%fused_computation.156 | convolution fusion | flops 2333736960 | bytes 16292864 | tf_op jit(solution)/shard_map/dot_general | solution.py:237
  336.6 4.8 %all-to-all-start.4 = ((f32[8,64,320]{2,1,0:T(8,128)}), f32[8,64,320]{2,1,0:T(8,128)S(1)}, u32[]{:S(2)}, u32[]{:S(2)}) async-start(f32[8,64,320]{2,1,0:T(8,128)} %bitcast.83), calls=%async_computation.4 | async-start | bytes 1572864 | tf_op jit(solution)/shard_map/all_to_all | solution.py:261
  341.4 14.7 %fusion = f32[640,9496]{0,1:T(8,128)} fusion(bf16[64,9496]{1,0:T(8,128)(2,1)S(1)} %pad_maximum_fusion.5, bf16[192,9496]{1,0:T(8,128)(2,1)} %copy-done.15, bf16[64,640]{1,0:T(8,128)(2,1)S(1)} %bitcast.198, bf16[192,640]{1,0:T(8,128)(2,1)S(1)} %bitcast.195), kind=kOutput, calls=%fused_computation | convolution fusion | flops 3122028544 | bytes 29499392 | tf_op jit(solution)/shard_map/dot_general | solution.py:248
  358.7 9.3 %collective-permute-done.40 = f32[64,320]{1,0:T(8,128)S(1)} collective-permute-done((f32[64,320]{1,0:T(8,128)S(1)}, f32[64,320]{1,0:T(8,128)S(1)}, u32[]{:S(2)}, u32[]{:S(2)}) %collective-permute-start.40) | collective-permute-done | bytes 81952 | tf_op jit(solution)/shard_map/ppermute | solution.py:268
  (268 shorter events, 152.1 us)
Async XLA Ops:
  11.9 35.0 %collective-permute-start.6 = (bf16[8,75968]{1,0:T(8,128)(2,1)}, bf16[8,75968]{1,0:T(8,128)(2,1)}, u32[]{:S(2)}, u32[]{:S(2)}) collective-permute-start(bf16[8,75968]{1,0:T(8,128)(2,1)} %bitcast), channel_id=1, source_target_pairs={{1,0},{2,3},{5,4},{6,7},{9,8},{10,11},{13,12},{14,15},{17,16},{18,... | collective-permute-start | bytes 3646472 | tf_op jit(solution)/shard_map/ppermute | solution.py:81
  55.6 71.5 %all-to-all-start = ((bf16[8,16,9496]{2,1,0:T(8,128)(2,1)}), bf16[8,16,9496]{2,1,0:T(8,128)(2,1)}, u32[]{:S(2)}, u32[]{:S(2)}) async-start(bf16[8,16,9496]{2,1,0:T(8,128)(2,1)} %bitcast_dynamic-update-slice_fusion), calls=%async_computation | async-start | bytes 4915200 | tf_op jit(solution)/shard_map/all_to_all | solution.py:115
  64.8 26.9 %collective-permute-start.9 = (f32[16,9496]{1,0:T(8,128)}, f32[16,9496]{1,0:T(8,128)S(1)}, u32[]{:S(2)}, u32[]{:S(2)}) collective-permute-start(f32[16,9496]{1,0:T(8,128)} %copy-done.12), channel_id=1, source_target_pairs={{3,2},{0,1},{7,6},{4,5},{11,10},{8,9},{15,14},{12,13},{19,18},{16,... | collective-permute-start | bytes 1823240 | tf_op jit(solution)/shard_map/ppermute | solution.py:61
  81.9 22.8 %collective-permute-start.12 = (f32[16,9496]{1,0:T(8,128)S(1)}, f32[16,9496]{1,0:T(8,128)S(1)}, u32[]{:S(2)}, u32[]{:S(2)}) collective-permute-start(f32[16,9496]{1,0:T(8,128)S(1)} %copy-done.11), channel_id=1, source_target_pairs={{3,2},{0,1},{7,6},{4,5},{11,10},{8,9},{15,14},{12,13},{19,18},{16,... | collective-permute-start | bytes 1823240 | tf_op jit(solution)/shard_map/ppermute | solution.py:61
  105.7 20.2 %collective-permute-start.13 = (f32[16,9496]{1,0:T(8,128)S(1)}, f32[16,9496]{1,0:T(8,128)S(1)}, u32[]{:S(2)}, u32[]{:S(2)}) collective-permute-start(f32[16,9496]{1,0:T(8,128)S(1)} %add.171), channel_id=1, source_target_pairs={{1,0},{2,3},{5,4},{6,7},{9,8},{10,11},{13,12},{14,15},{17,16},{18,... | collective-permute-start | bytes 1823240 | tf_op jit(solution)/shard_map/ppermute | solution.py:61
  112.7 28.5 %collective-permute-start.18 = (f32[16,9496]{1,0:T(8,128)}, f32[16,9496]{1,0:T(8,128)}, u32[]{:S(2)}, u32[]{:S(2)}) collective-permute-start(f32[16,9496]{1,0:T(8,128)} %get-tuple-element.97), channel_id=1, source_target_pairs={{3,2},{0,1},{7,6},{4,5},{11,10},{8,9},{15,14},{12,13},{19,18},{16,... | collective-permute-start | bytes 1823240 | tf_op jit(solution)/shard_map/ppermute | solution.py:61
  118.8 26.0 %collective-permute-start.17 = (f32[16,9496]{1,0:T(8,128)}, f32[16,9496]{1,0:T(8,128)}, u32[]{:S(2)}, u32[]{:S(2)}) collective-permute-start(f32[16,9496]{1,0:T(8,128)} %add.173), channel_id=1, source_target_pairs={{2,1},{1,2},{6,5},{5,6},{10,9},{9,10},{14,13},{13,14},{18,17},{17,... | collective-permute-start | bytes 1823240 | tf_op jit(solution)/shard_map/ppermute | solution.py:61
  121.2 26.8 %collective-permute-start.16 = (f32[16,9496]{1,0:T(8,128)}, f32[16,9496]{1,0:T(8,128)}, u32[]{:S(2)}, u32[]{:S(2)}) collective-permute-start(f32[16,9496]{1,0:T(8,128)} %add.174), channel_id=1, source_target_pairs={{1,0},{2,3},{5,4},{6,7},{9,8},{10,11},{13,12},{14,15},{17,16},{18,... | collective-permute-start | bytes 1823240 | tf_op jit(solution)/shard_map/ppermute | solution.py:61
  131.9 24.3 %all-to-all-start.1 = ((f32[8,1,240]{2,1,0:T(1,128)}), f32[8,1,240]{2,1,0:T(1,128)S(1)}, u32[]{:S(2)}, u32[]{:S(2)}) async-start(f32[8,1,240]{2,1,0:T(1,128)} %reshape.128), calls=%async_computation.1 | async-start | bytes 16384 | tf_op jit(solution)/shard_map/all_to_all | solution.py:136
  136.2 24.9 %collective-permute-start.21 = (f32[16,9496]{1,0:T(8,128)}, f32[16,9496]{1,0:T(8,128)}, u32[]{:S(2)}, u32[]{:S(2)}) collective-permute-start(f32[16,9496]{1,0:T(8,128)} %copy-done.6), channel_id=1, source_target_pairs={{3,2},{0,1},{7,6},{4,5},{11,10},{8,9},{15,14},{12,13},{19,18},{16,... | collective-permute-start | bytes 1823240 | tf_op jit(solution)/shard_map/ppermute | solution.py:61
  143.3 21.4 %collective-permute-start.20 = (f32[16,9496]{1,0:T(8,128)}, f32[16,9496]{1,0:T(8,128)}, u32[]{:S(2)}, u32[]{:S(2)}) collective-permute-start(f32[16,9496]{1,0:T(8,128)} %add.176), channel_id=1, source_target_pairs={{2,1},{1,2},{6,5},{5,6},{10,9},{9,10},{14,13},{13,14},{18,17},{17,... | collective-permute-start | bytes 1823240 | tf_op jit(solution)/shard_map/ppermute | solution.py:61
  146.8 31.6 %collective-permute-start.19 = (f32[16,9496]{1,0:T(8,128)}, f32[16,9496]{1,0:T(8,128)}, u32[]{:S(2)}, u32[]{:S(2)}) collective-permute-start(f32[16,9496]{1,0:T(8,128)} %add.177), channel_id=1, source_target_pairs={{1,0},{2,3},{5,4},{6,7},{9,8},{10,11},{13,12},{14,15},{17,16},{18,... | collective-permute-start | bytes 1823240 | tf_op jit(solution)/shard_map/ppermute | solution.py:61
  150.0 29.5 %collective-permute-start.24 = (f32[16,9496]{1,0:T(8,128)}, f32[16,9496]{1,0:T(8,128)}, u32[]{:S(2)}, u32[]{:S(2)}) collective-permute-start(f32[16,9496]{1,0:T(8,128)} %get-tuple-element.106), channel_id=1, source_target_pairs={{3,2},{0,1},{7,6},{4,5},{11,10},{8,9},{15,14},{12,13},{19,18},{16,... | collective-permute-start | bytes 1823240 | tf_op jit(solution)/shard_map/ppermute | solution.py:61
  163.1 20.2 %collective-permute-start.23 = (f32[16,9496]{1,0:T(8,128)}, f32[16,9496]{1,0:T(8,128)}, u32[]{:S(2)}, u32[]{:S(2)}) collective-permute-start(f32[16,9496]{1,0:T(8,128)} %add.179), channel_id=1, source_target_pairs={{2,1},{1,2},{6,5},{5,6},{10,9},{9,10},{14,13},{13,14},{18,17},{17,... | collective-permute-start | bytes 1823240 | tf_op jit(solution)/shard_map/ppermute | solution.py:61
  170.6 24.5 %collective-permute-start.27 = (bf16[48,9496]{1,0:T(8,128)(2,1)}, bf16[48,9496]{1,0:T(8,128)(2,1)}, u32[]{:S(2)}, u32[]{:S(2)}) collective-permute-start(bf16[48,9496]{1,0:T(8,128)(2,1)} %fusion.21), channel_id=1, source_target_pairs={{3,2},{0,1},{7,6},{4,5},{11,10},{8,9},{15,14},{12,13},{19,18},{16,... | collective-permute-start | bytes 2734856 | tf_op jit(solution)/shard_map/ppermute | solution.py:61
  195.1 34.7 %collective-permute-start.29 = (bf16[48,9496]{1,0:T(8,128)(2,1)}, bf16[48,9496]{1,0:T(8,128)(2,1)}, u32[]{:S(2)}, u32[]{:S(2)}) collective-permute-start(bf16[48,9496]{1,0:T(8,128)(2,1)} %collective-permute-done.27), channel_id=1, source_target_pairs={{2,1},{1,2},{6,5},{5,6},{10,9},{9,10},{14,13},{13,14},{18,17},{17,... | collective-permute-start | bytes 2734856 | tf_op jit(solution)/shard_map/ppermute | solution.py:61
  226.6 22.5 %collective-permute-start.30 = (bf16[48,9496]{1,0:T(8,128)(2,1)}, bf16[48,9496]{1,0:T(8,128)(2,1)}, u32[]{:S(2)}, u32[]{:S(2)}) collective-permute-start(bf16[48,9496]{1,0:T(8,128)(2,1)} %fusion.20), channel_id=1, source_target_pairs={{3,2},{0,1},{7,6},{4,5},{11,10},{8,9},{15,14},{12,13},{19,18},{16,... | collective-permute-start | bytes 2734856 | tf_op jit(solution)/shard_map/ppermute | solution.py:61
  229.8 59.1 %collective-permute-start.34 = (bf16[48,9496]{1,0:T(8,128)(2,1)}, bf16[48,9496]{1,0:T(8,128)(2,1)}, u32[]{:S(2)}, u32[]{:S(2)}) collective-permute-start(bf16[48,9496]{1,0:T(8,128)(2,1)} %collective-permute-done.29), channel_id=1, source_target_pairs={{1,0},{2,3},{5,4},{6,7},{9,8},{10,11},{13,12},{14,15},{17,16},{18,... | collective-permute-start | bytes 2734856 | tf_op jit(solution)/shard_map/ppermute | solution.py:61
  233.1 22.6 %collective-permute-start.33 = (bf16[16,9496]{1,0:T(8,128)(2,1)S(1)}, bf16[16,9496]{1,0:T(8,128)(2,1)S(1)}, u32[]{:S(2)}, u32[]{:S(2)}) collective-permute-start(bf16[16,9496]{1,0:T(8,128)(2,1)S(1)} %get-tuple-element.161), channel_id=1, source_target_pairs={{3,2},{0,1},{7,6},{4,5},{11,10},{8,9},{15,14},{12,13},{19,18},{16,... | collective-permute-start | bytes 911624 | tf_op jit(solution)/shard_map/ppermute | solution.py:61
  238.6 23.0 %collective-permute-start.32 = (bf16[16,9496]{1,0:T(8,128)(2,1)S(1)}, bf16[16,9496]{1,0:T(8,128)(2,1)S(1)}, u32[]{:S(2)}, u32[]{:S(2)}) collective-permute-start(bf16[16,9496]{1,0:T(8,128)(2,1)S(1)} %get-tuple-element.162), channel_id=1, source_target_pairs={{3,2},{0,1},{7,6},{4,5},{11,10},{8,9},{15,14},{12,13},{19,18},{16,... | collective-permute-start | bytes 911624 | tf_op jit(solution)/shard_map/ppermute | solution.py:61
  255.7 32.0 %collective-permute-start.37 = (bf16[16,9496]{1,0:T(8,128)(2,1)S(1)}, bf16[16,9496]{1,0:T(8,128)(2,1)S(1)}, u32[]{:S(2)}, u32[]{:S(2)}) collective-permute-start(bf16[16,9496]{1,0:T(8,128)(2,1)S(1)} %collective-permute-done.33), channel_id=1, source_target_pairs={{2,1},{1,2},{6,5},{5,6},{10,9},{9,10},{14,13},{13,14},{18,17},{17,... | collective-permute-start | bytes 911624 | tf_op jit(solution)/shard_map/ppermute | solution.py:61
  261.6 29.9 %collective-permute-start.36 = (bf16[16,9496]{1,0:T(8,128)(2,1)S(1)}, bf16[16,9496]{1,0:T(8,128)(2,1)S(1)}, u32[]{:S(2)}, u32[]{:S(2)}) collective-permute-start(bf16[16,9496]{1,0:T(8,128)(2,1)S(1)} %collective-permute-done.32), channel_id=1, source_target_pairs={{2,1},{1,2},{6,5},{5,6},{10,9},{9,10},{14,13},{13,14},{18,17},{17,... | collective-permute-start | bytes 911624 | tf_op jit(solution)/shard_map/ppermute | solution.py:61
  290.2 32.5 %collective-permute-start.35 = (bf16[48,9496]{1,0:T(8,128)(2,1)}, bf16[48,9496]{1,0:T(8,128)(2,1)S(1)}, u32[]{:S(2)}, u32[]{:S(2)}) collective-permute-start(bf16[48,9496]{1,0:T(8,128)(2,1)} %collective-permute-done.31), channel_id=1, source_target_pairs={{1,0},{2,3},{5,4},{6,7},{9,8},{10,11},{13,12},{14,15},{17,16},{18,... | collective-permute-start | bytes 2734856 | tf_op jit(solution)/shard_map/ppermute | solution.py:61
  291.6 30.9 %collective-permute-start.39 = (bf16[16,9496]{1,0:T(8,128)(2,1)S(1)}, bf16[16,9496]{1,0:T(8,128)(2,1)S(1)}, u32[]{:S(2)}, u32[]{:S(2)}) collective-permute-start(bf16[16,9496]{1,0:T(8,128)(2,1)S(1)} %collective-permute-done.36), channel_id=1, source_target_pairs={{1,0},{2,3},{5,4},{6,7},{9,8},{10,11},{13,12},{14,15},{17,16},{18,... | collective-permute-start | bytes 911624 | tf_op jit(solution)/shard_map/ppermute | solution.py:61
  (61 other events, 712.5 us)

commit v5 on v4

v5 whole, which is shorter than its diff:
```python
import jax
import jax.numpy as jnp
from jax import lax
from jax.experimental import pallas as pl
from jax.experimental.pallas import tpu as pltpu
from jax.sharding import PartitionSpec as P

LOSS_SCALE = 256.0
VOCAB_TILE = 1024


def after(value, *others):
    return lax.optimization_barrier((value, *others))[0]


def partial_kernel(hidden_ref, head_ref, *out_refs):
    product = lax.dot_general(
        hidden_ref[...], head_ref[...], (((1,), (1,)), ((), ())),
        preferred_element_type=jnp.float32)
    height = out_refs[0].shape[0]
    for i, out_ref in enumerate(out_refs):
        out_ref[...] = product[i * height:(i + 1) * height]


def partial_students(hidden, head_rows, chunk):
    tokens, rows = hidden.shape
    cols = head_rows.shape[0]
    tile = min(VOCAB_TILE, cols)
    count = tokens // chunk
    return pl.pallas_call(
        partial_kernel,
        grid=(pl.cdiv(cols, tile),),
        in_specs=[
            pl.BlockSpec((tokens, rows), lambda i: (0, 0)),
            pl.BlockSpec((tile, rows), lambda i: (i, 0)),
        ],
        out_specs=[pl.BlockSpec((chunk, tile), lambda i: (0, i))] * count,
        out_shape=[jax.ShapeDtypeStruct((chunk, cols), jnp.float32)] * count,
        compiler_params=pltpu.CompilerParams(vmem_limit_bytes=16 * 1024 * 1024),
        cost_estimate=pl.CostEstimate(
            flops=2 * tokens * rows * cols,
            bytes_accessed=2 * rows * cols + 4 * tokens * cols,
            transcendentals=0),
    )(hidden, head_rows)


def body(hidden_states, head_weight, teacher_logits):
    seq_count = lax.axis_size("seq")
    vocab_count = lax.axis_size("vocab")
    half = seq_count // 2
    last = seq_count - 1
    z = lax.axis_index("seq")
    own_tokens, width = hidden_states.shape
    rows, cols = head_weight.shape
    per_dev = teacher_logits.shape[1]
    chunk = half * per_dev
    chunks = vocab_count
    total_tokens = own_tokens * seq_count
    hops = seq_count - 1
    low_side = z < half

    def hop(value, j):
        return lax.ppermute(value, "seq", [(last - j, last - j - 1), (j, j + 1)])

    strips = [
        lax.dynamic_slice_in_dim(hidden_states, ((z + k) % seq_count) * rows, rows, axis=1)
        for k in range(seq_count)
    ]
    blocks = [strips[0]] + [
        lax.ppermute(strips[k], "seq", [(d, (d + k) % seq_count) for d in range(seq_count)])
        for k in range(1, seq_count)
    ]
    blocks = jnp.stack(blocks).reshape(seq_count, vocab_count, per_dev, rows)
    sides = []
    for end in (jnp.where(low_side, 0, last), jnp.where(low_side, last, 0)):
        step = jnp.where(end == 0, 1, -1)
        sides.append(jnp.stack(
            [blocks[(z - (end + step * j)) % seq_count] for j in range(half)], axis=1))
    ordered = jnp.stack(sides).reshape(total_tokens, rows)
    head_rows = head_weight.T
    half_tokens = total_tokens // 2

    mine, ordered = lax.optimization_barrier((teacher_logits[0], ordered))
    held = [mine] + [
        lax.ppermute(mine, "seq", [(j, 0), (last - j, last)]) for j in range(1, half)
    ]

    middle = chunks // 2
    groups = [list(range(middle)), list(range(middle, chunks))]
    loads = [[[i, i + 1] for i in range(0, middle - 1, 2)] + [[middle - 1]] * (middle % 2),
             [[middle, middle + 1]] + [[i] for i in range(middle + 2, chunks)]]
    moving = [None] * chunks
    students = [None] * chunks
    targets = []
    pieces = []
    locals_ = [None] * chunks
    exchanged = {}
    travels = {}
    settled_loss = []
    tie = []

    def tied(value):
        value = after(value, *tie) if tie else value
        tie[:] = [value]
        return value

    def send(i, j):
        part = (other_part if j < half else own_part)[i]
        if j == 0:
            value = tied(part)
        else:
            value = part + tied(moving[i])
            tie[:] = [value]
        moving[i] = hop(value, j)

    def cut_teacher():
        rows_held = tied(jnp.concatenate(held, axis=0))
        pieces.append(jnp.stack(
            [rows_held[:, v * cols:(v + 1) * cols] for v in range(vocab_count)]))
        tie[:] = pieces

    def exchange_teacher():
        targets.extend(
            lax.all_to_all(tied(pieces[0]), "vocab", split_axis=0, concat_axis=0, tiled=True))

    def hold_teacher():
        held[:] = lax.optimization_barrier((*held, *tie))[:half]
        tie[:] = [held[-1]]

    def local_stats(i):
        student = tied(students[i])
        target = targets[i].astype(jnp.float32)
        student_top = jnp.max(student, axis=1)
        target_top = jnp.max(target, axis=1)
        target_exp = jnp.exp(target - target_top[:, None])
        locals_[i] = jnp.stack([
            student_top,
            target_top,
            jnp.sum(jnp.exp(student - student_top[:, None]), axis=1),
            jnp.sum(target_exp, axis=1),
            jnp.sum(target_exp * (target - student), axis=1),
        ])
        tie[:] = [locals_[i]]

    def exchange_stats(g):
        stats = jnp.concatenate([locals_[i] for i in groups[g]], axis=1)
        tie[:] = [stats]
        stats = jnp.broadcast_to(stats, (vocab_count, *stats.shape))
        stats = lax.all_to_all(stats, "vocab", split_axis=0, concat_axis=0, tiled=True)
        exchanged[g] = stats

    def merge_stats(g):
        stats = tied(exchanged[g])
        student_max = jnp.max(stats[:, 0], axis=0)
        teacher_max = jnp.max(stats[:, 1], axis=0)
        student_scale = jnp.exp(stats[:, 0] - student_max)
        teacher_scale = jnp.exp(stats[:, 1] - teacher_max)
        student_sum = jnp.sum(stats[:, 2] * student_scale, axis=0)
        teacher_sum = jnp.sum(stats[:, 3] * teacher_scale, axis=0)
        cross = jnp.sum(stats[:, 4] * teacher_scale, axis=0)
        exchanged[g] = lax.optimization_barrier(
            (student_max, student_sum, teacher_max, teacher_sum, cross))
        tie[:] = [exchanged[g][0]]

    def form_grads(g, p):
        student_max, student_sum, teacher_max, teacher_sum, _ = exchanged[g]
        grads = []
        for i in loads[g][p]:
            first = (i - groups[g][0]) * chunk
            at = slice(first, first + chunk)
            student = tied(students[i])
            target = targets[i].astype(jnp.float32)
            grads.append((
                LOSS_SCALE * (
                    jnp.exp(student - student_max[at, None]) / student_sum[at, None]
                    - jnp.exp(target - teacher_max[at, None]) / teacher_sum[at, None]
                )
            ).astype(jnp.bfloat16))
        grad = jnp.concatenate(grads, axis=0)
        tie[:] = [grad]
        travels[g, p] = [grad]

    def send_grad(g, p, j):
        value = travels[g, p][j] if j == 0 else tied(travels[g, p][j])
        travels[g, p].append(hop(value, j))

    def sum_up(i):
        students[i] = own_part[i] + tied(moving[i])
        tie[:] = [students[i]]

    def loss():
        student_max, student_sum, teacher_max, teacher_sum, cross = (
            jnp.concatenate(both) for both in zip(*exchanged.values()))
        divergence = jnp.sum(
            cross / teacher_sum
            - teacher_max
            - jnp.log(teacher_sum)
            + student_max
            + jnp.log(student_sum)
        )
        travels["loss"] = [tied(divergence.reshape(1, 1))]

    def send_loss(j):
        value = travels["loss"][j] if j == 0 else tied(travels["loss"][j])
        travels["loss"].append(hop(value, j))

    near = jnp.minimum(z, last - z)

    def settle(key):
        own, other = travels[key][0], travels[key][hops]
        for j in range(1, half):
            own = jnp.where(near == j, travels[key][j], own)
            other = jnp.where(near == j, travels[key][hops - j], other)
        return own, other

    def settled(keys):
        pairs = [settle(key) for key in keys]
        return jnp.concatenate([p[0] for p in pairs] + [p[1] for p in pairs], axis=0)

    features = []

    def settle_loss():
        travels["loss"][hops] = tied(travels["loss"][hops])
        settled_loss.append(sum(settle("loss"))[0, 0] / total_tokens)
        tie[:] = [settled_loss[0]]

    def early_feature():
        grads = tied(settled(early_keys))
        features.append((grads, jnp.dot(grads, head_rows, preferred_element_type=jnp.float32)))
        tie[:] = [features[0][1]]

    slots = {}

    def plan(slot, order, call, *args):
        slots.setdefault(slot, []).append((order, len(slots.get(slot, ())), call, args))

    for i in range(chunks):
        plan(i - 1, 5, send, i, 0)
        for j in range(1, hops):
            plan(i + j, j, send, i, j)
        plan(i + hops, 4, sum_up, i)
    end = chunks + hops - 1
    plan(2, 0, hold_teacher)
    plan(3, 15, cut_teacher)
    plan(4, 15, exchange_teacher)
    stats_slot = middle + hops
    for i in range(chunks):
        wait = min(6 + i // 2, stats_slot) if i < middle else i + hops + (i == middle)
        plan(max(i + hops, wait), 15, local_stats, i)
    early_keys, late_keys = [], []
    for g, slot in enumerate((stats_slot, end)):
        plan(slot, 18, exchange_stats, g)
        plan(slot + 1, 20, merge_stats, g)
        for p in range(len(loads[g])):
            (late_keys if g else early_keys).append((g, p))
            first = slot + 1 + (0 if g else p)
            plan(first, 40 + 2 * p, form_grads, g, p)
            plan(first, 41 + 2 * p, send_grad, g, p, 0)
            for j in range(1, hops):
                if g == 0:
                    plan(first + j, 30 - j if first + j <= end else 90 - j, send_grad, g, p, j)
                else:
                    plan(first + j + (p + 1) // 2, 120 + 10 * j + p, send_grad, g, p, j)
    plan(end + 1, 60, loss)
    for j in range(hops):
        plan(end + 1 + j + (j > 0), 1510, send_loss, j)
    final = max(slots)
    plan(final, 1600, early_feature)
    plan(final, 1700, settle_loss)

    first_part = jnp.dot(
        ordered[half_tokens:half_tokens + chunk], head_weight, preferred_element_type=jnp.float32)
    other_part = [first_part]
    own_part = None
    for slot in sorted(slots):
        for _, _, call, args in sorted(slots[slot], key=lambda e: e[:2]):
            call(*args)
        if own_part is None:
            remaining = tied(jnp.concatenate(
                [ordered[half_tokens + chunk:], ordered[:half_tokens]]))
            parts = partial_students(remaining, head_rows, chunk)
            other_part.extend(parts[:chunks - 1])
            own_part = parts[chunks - 1:]
            tie[:] = [own_part[0]]

    mean_divergence = settled_loss[0]
    early_grads, feature_early = features[0]
    for key in late_keys:
        travels[key][hops] = tied(travels[key][hops])
    late_grads = settled(late_keys)
    feature_late = jnp.dot(late_grads, head_rows, preferred_element_type=jnp.float32)
    early_rows = early_grads.shape[0] // 2
    feature = jnp.concatenate(
        [feature_early.reshape(2, -1, rows), feature_late.reshape(2, -1, rows)], axis=1)
    both = ordered.reshape(2, half_tokens, rows)
    matching = jnp.concatenate([
        both[:, :early_rows].reshape(-1, rows), both[:, early_rows:].reshape(-1, rows)])
    all_grads = jnp.concatenate([early_grads, late_grads])
    head_part = lax.dot_general(
        all_grads, matching, (((0,), (0,)), ((), ())), preferred_element_type=jnp.float32
    ).T
    feature = feature.reshape(2, vocab_count, half, per_dev, rows).transpose(0, 2, 1, 3, 4)
    feature = feature.reshape(2, half, own_tokens, rows)
    low = jnp.where(low_side, feature[0], feature[1])
    high = jnp.where(low_side, feature[1], feature[0])
    feature = jnp.concatenate([low, high[::-1]])
    if vocab_count % seq_count == 0:
        share = vocab_count // seq_count
        out_cols = rows // share
        feature = feature.reshape(seq_count, own_tokens, share, out_cols).transpose(0, 2, 1, 3)
        feature = feature.reshape(vocab_count, own_tokens, out_cols)
        feature = lax.all_to_all(feature, "vocab", split_axis=0, concat_axis=0, tiled=True)
        feature, head_part = lax.optimization_barrier((feature, head_part))
        feature = jnp.sum(feature, axis=0)
        pairs = [
            ((dst * share + b) * seq_count + src, (src * share + b) * seq_count + dst)
            for src in range(seq_count) for dst in range(seq_count) for b in range(share)
        ]
        hidden_grad = lax.ppermute(feature, ("vocab", "seq"), pairs)
    else:
        feature = lax.all_to_all(feature, "seq", split_axis=0, concat_axis=2, tiled=True)
        hidden_grad = lax.psum_scatter(feature[0], "vocab", scatter_dimension=1, tiled=True)
    return (mean_divergence, hidden_grad, head_part)


def solution(mesh):
    in_specs = (P("seq", None), P("seq", "vocab"), P("seq", "vocab", None))
    out_specs = (P(), P("seq", "vocab"), P("seq", "vocab"))
    return jax.shard_map(body, mesh=mesh, in_specs=in_specs, out_specs=out_specs, check_vma=False)
```

time: 372 us -> 359 us (0.965)
  blocking collectives: 24 us -> 0 us
  other arithmetic: 50.2 us -> 67.7 us
  Pallas kernels: 26.7 us -> 15.1 us
  local copies, waits for them, and re-layouts: 20.3 us -> 9.08 us
  starting transfers between devices: 115 us -> 121 us
  waiting for transfers between devices: 105 us -> 110 us
    psum x1 -> x0, blocking collectives: 24 us -> none  [loss(): total = lax.psum(jnp.where(at_end, divergence, 0.0), 'seq')]
    pallas_call x2 -> x1, Pallas kernels: 26.7 us -> 15.1 us  [partial_students(): pl.pallas_call(partial_kernel, grid=(pl.cdiv(cols, tile),), in_specs=[pl....]
    ppermute x36 -> x42, starting transfers between devices: 84.2 us -> 95.1 us  [hop(): return lax.ppermute(value, 'seq', [(last - j, last - j - 1), (j, j + 1)])]
    reduce_sum x3 -> x8, other arithmetic: 2.58 us -> 11.8 us  [local_stats(): jnp.sum(target_exp * (target - student), axis=1)]
    unnamed x89 -> x61, local copies, waits for them, and re-layouts: 11.4 us -> 5.49 us
    reduce_max x3 -> x8, other arithmetic: 0.57 us -> 5.9 us  [local_stats(): student_top = jnp.max(student, axis=1)]
    add x8, other arithmetic: 6.76 us -> 11.1 us  [sum_up(): students[i] = own_part[i] + tied(moving[i])]
    all_to_all x4 -> x3, starting transfers between devices: 17.4 us -> 13.2 us  [the longest x2 8.42 us: exchange_stats(): lax.all_to_all(stats, 'vocab', split_axis=0, concat_axis=0, tiled=True)]
  transfers between devices with their start and end apart: 46 -> 51, of which waited for: 19 -> 17; matrix products, arithmetic and copies ran while one was open for 19% -> 26% of each run, Pallas kernels for 7% -> 4%
where the time goes in v5:
time: 359 us; the launch traced here: 357 us
  starting transfers between devices  121 us (34%)
  waiting for transfers between devices  110 us (31%)
  other arithmetic  67.7 us (19%)
  matrix products  27.6 us (8%)
  Pallas kernels  15.1 us (4%)
  local copies, waits for them, and re-layouts  9.08 us (3%)
  between operations  5.33 us (1%)
    ppermute x42, starting transfers between devices, hop(): return lax.ppermute(value, 'seq', [(last - j, last - j - 1), (j, j + 1)])  95.1 us
    ppermute x42, waiting for transfers between devices, hop(): return lax.ppermute(value, 'seq', [(last - j, last - j - 1), (j, j + 1)])  91.6 us
    add x16, other arithmetic, send(): value = part + tied(moving[i])  19.4 us
    pallas_call x1, Pallas kernels, partial_students(): pl.pallas_call(partial_kernel, grid=(pl.cdiv(cols, tile),), in_specs=[pl....  15.1 us
    dot_general x1, matrix products, body(): lax.dot_general(all_grads, matching, (((0,), (0,)), ((), ())), preferred_...  15 us
    reduce_sum x8, other arithmetic, local_stats(): jnp.sum(target_exp * (target - student), axis=1)  11.8 us
    add x8, other arithmetic, sum_up(): students[i] = own_part[i] + tied(moving[i])  11.1 us
    ppermute x1, waiting for transfers between devices, body(): hidden_grad = lax.ppermute(feature, ('vocab', 'seq'), pairs)  9.93 us
  transfers between devices with their start and end apart: 51, of which 17 were waited for; matrix products, arithmetic and copies ran while one was open for 26% of the time, Pallas kernels for 4%

profile of v5, /device:TPU:2, one launch (start us, length us, event | category | flops | bytes accessed | tf_op | source)
XLA Modules:
  0.0 356.6 jit_solution(6778981459067187354)
XLA Ops:
  14.9 8.4 %fusion.90 = f32[16,9496]{1,0:T(8,128)S(1)} fusion(bf16[640,9496]{0,1:T(8,128)(2,1)} %param.4, bf16[256,640]{1,0:T(8,128)(2,1)S(1)} %bitcast.201), kind=kOutput, calls=%fused_computation.172 | convolution fusion | flops 194478080 | bytes 12783104 | tf_op jit(solution)/shard_map/dot_general | solution.py:271
  27.4 15.1 %shard_map.58 = (f32[16,9496]{1,0:T(8,128)S(1)}, f32[16,9496]{1,0:T(8,128)S(1)}, f32[16,9496]{1,0:T(8,128)S(1)}, f32[16,9496]{1,0:T(8,128)S(1)}, f32[16,9496]{1,...) custom-call(bf16[240,640]{1,0:T(8,128)(2,1)S(1)} %pad_maximum_fusion, ...), custom_call_target="tpu_custom_call" | custom-call | flops 2917171200 | bytes 21271040 | tf_op jit(solution)/shard_map/pallas_call | solution.py:30
  48.1 10.0 %collective-permute-done.5 = f32[16,9496]{1,0:T(8,128)S(1)} collective-permute-done((f32[16,9496]{1,0:T(8,128)S(1)}, f32[16,9496]{1,0:T(8,128)S(1)}, u32[]{:S(2)}, u32[]{:S(2)}) %collective-permute-start.5) | collective-permute-done | bytes 607776 | tf_op jit(solution)/shard_map/ppermute | solution.py:63
  60.3 6.6 %collective-permute-start.10 = (f32[16,9496]{1,0:T(8,128)S(1)}, f32[16,9496]{1,0:T(8,128)S(1)}, u32[]{:S(2)}, u32[]{:S(2)}) collective-permute-start(f32[16,9496]{1,0:T(8,128)S(1)} %get-tuple-element.118), channel_id=1, source_target_pairs={{3,2},{0,1},{7,6},{4,5},{11,10},{8,9},{15,14},{12,13},{19,18},{16,... | collective-permute-start | bytes 1823240 | tf_op jit(solution)/shard_map/ppermute | solution.py:63
  66.9 4.3 %collective-permute-done.9 = f32[16,9496]{1,0:T(8,128)S(1)} collective-permute-done((f32[16,9496]{1,0:T(8,128)S(1)}, f32[16,9496]{1,0:T(8,128)S(1)}, u32[]{:S(2)}, u32[]{:S(2)}) %collective-permute-start.9) | collective-permute-done | bytes 607776 | tf_op jit(solution)/shard_map/ppermute | solution.py:63
  84.6 6.3 %collective-permute-done.13 = f32[16,9496]{1,0:T(8,128)S(1)} collective-permute-done((f32[16,9496]{1,0:T(8,128)S(1)}, f32[16,9496]{1,0:T(8,128)S(1)}, u32[]{:S(2)}, u32[]{:S(2)}) %collective-permute-start.13) | collective-permute-done | bytes 607776 | tf_op jit(solution)/shard_map/ppermute | solution.py:63
  91.8 4.8 %all-to-all-start = ((bf16[8,16,9496]{2,1,0:T(8,128)(2,1)}), bf16[8,16,9496]{2,1,0:T(8,128)(2,1)}, u32[]{:S(2)}, u32[]{:S(2)}) async-start(bf16[8,16,9496]{2,1,0:T(8,128)(2,1)} %copy-done.12), calls=%async_computation | async-start | bytes 4915200 | tf_op jit(solution)/shard_map/all_to_all | solution.py:124
  100.1 6.2 %collective-permute-start.17 = (f32[16,9496]{1,0:T(8,128)}, f32[16,9496]{1,0:T(8,128)}, u32[]{:S(2)}, u32[]{:S(2)}) collective-permute-start(f32[16,9496]{1,0:T(8,128)} %copy-done.1), channel_id=1, source_target_pairs={{3,2},{0,1},{7,6},{4,5},{11,10},{8,9},{15,14},{12,13},{19,18},{16,... | collective-permute-start | bytes 1823240 | tf_op jit(solution)/shard_map/ppermute | solution.py:63
  106.2 6.3 %collective-permute-done.12 = f32[16,9496]{1,0:T(8,128)S(1)} collective-permute-done((f32[16,9496]{1,0:T(8,128)}, f32[16,9496]{1,0:T(8,128)S(1)}, u32[]{:S(2)}, u32[]{:S(2)}) %collective-permute-start.12) | collective-permute-done | bytes 607776 | tf_op jit(solution)/shard_map/ppermute | solution.py:63
  121.2 7.0 %collective-permute-start.21 = (f32[16,9496]{1,0:T(8,128)}, f32[16,9496]{1,0:T(8,128)}, u32[]{:S(2)}, u32[]{:S(2)}) collective-permute-start(f32[16,9496]{1,0:T(8,128)} %get-tuple-element.140), channel_id=1, source_target_pairs={{3,2},{0,1},{7,6},{4,5},{11,10},{8,9},{15,14},{12,13},{19,18},{16,... | collective-permute-start | bytes 1823240 | tf_op jit(solution)/shard_map/ppermute | solution.py:63
  136.9 6.4 %collective-permute-start.24 = (f32[16,9496]{1,0:T(8,128)}, f32[16,9496]{1,0:T(8,128)}, u32[]{:S(2)}, u32[]{:S(2)}) collective-permute-start(f32[16,9496]{1,0:T(8,128)} %get-tuple-element.144), channel_id=1, source_target_pairs={{3,2},{0,1},{7,6},{4,5},{11,10},{8,9},{15,14},{12,13},{19,18},{16,... | collective-permute-start | bytes 1823240 | tf_op jit(solution)/shard_map/ppermute | solution.py:63
  164.4 4.2 %all-to-all-start.1 = ((f32[8,1,320]{2,1,0:T(1,128)}), f32[8,1,320]{2,1,0:T(1,128)S(1)}, u32[]{:S(2)}, u32[]{:S(2)}) async-start(f32[8,1,320]{2,1,0:T(1,128)} %reshape.236), calls=%async_computation.1 | async-start | bytes 24576 | tf_op jit(solution)/shard_map/all_to_all | solution.py:149
  187.6 8.1 %collective-permute-start.28 = (bf16[32,9496]{1,0:T(8,128)(2,1)}, bf16[32,9496]{1,0:T(8,128)(2,1)}, u32[]{:S(2)}, u32[]{:S(2)}) collective-permute-start(bf16[32,9496]{1,0:T(8,128)(2,1)} %pad_maximum_fusion.4), channel_id=1, source_target_pairs={{3,2},{0,1},{7,6},{4,5},{11,10},{8,9},{15,14},{12,13},{19,18},{16,... | collective-permute-start | bytes 1823240 | tf_op jit(solution)/shard_map/ppermute | solution.py:63
  199.1 5.8 %collective-permute-done.25 = f32[16,9496]{1,0:T(8,128)S(1)} collective-permute-done((f32[16,9496]{1,0:T(8,128)}, f32[16,9496]{1,0:T(8,128)S(1)}, u32[]{:S(2)}, u32[]{:S(2)}) %collective-permute-start.25) | collective-permute-done | bytes 607776 | tf_op jit(solution)/shard_map/ppermute | solution.py:63
  213.1 6.5 %collective-permute-start.29 = (bf16[32,9496]{1,0:T(8,128)(2,1)}, bf16[32,9496]{1,0:T(8,128)(2,1)}, u32[]{:S(2)}, u32[]{:S(2)}) collective-permute-start(bf16[32,9496]{1,0:T(8,128)(2,1)} %pad_maximum_fusion.5), channel_id=1, source_target_pairs={{3,2},{0,1},{7,6},{4,5},{11,10},{8,9},{15,14},{12,13},{19,18},{16,... | collective-permute-start | bytes 1823240 | tf_op jit(solution)/shard_map/ppermute | solution.py:63
  223.1 4.2 %all-to-all-start.2 = ((f32[8,1,320]{2,1,0:T(1,128)}), f32[8,1,320]{2,1,0:T(1,128)S(1)}, u32[]{:S(2)}, u32[]{:S(2)}) async-start(f32[8,1,320]{2,1,0:T(1,128)} %reshape.238), calls=%async_computation.2 | async-start | bytes 24576 | tf_op jit(solution)/shard_map/all_to_all | solution.py:149
  234.8 4.1 %collective-permute-start.36 = (bf16[16,9496]{1,0:T(8,128)(2,1)S(1)}, bf16[16,9496]{1,0:T(8,128)(2,1)S(1)}, u32[]{:S(2)}, u32[]{:S(2)}) collective-permute-start(bf16[16,9496]{1,0:T(8,128)(2,1)S(1)} %fusion.66), channel_id=1, source_target_pairs={{3,2},{0,1},{7,6},{4,5},{11,10},{8,9},{15,14},{12,13},{19,18},{16,... | collective-permute-start | bytes 911624 | tf_op jit(solution)/shard_map/ppermute | solution.py:63
  248.5 14.7 %collective-permute-done.31 = f32[1,1]{1,0:T(1,128)} collective-permute-done((f32[1,1]{1,0:T(1,128)}, f32[1,1]{1,0:T(1,128)}, u32[]{:S(2)}, u32[]{:S(2)}) %collective-permute-start.31) | collective-permute-done | bytes 36 | tf_op jit(solution)/shard_map/ppermute | solution.py:63
  269.3 12.8 %collective-permute-done.41 = bf16[32,9496]{1,0:T(8,128)(2,1)S(1)} collective-permute-done((bf16[32,9496]{1,0:T(8,128)(2,1)}, bf16[32,9496]{1,0:T(8,128)(2,1)S(1)}, u32[]{:S(2)}, u32[]{:S(2)}) %collective-permute-start.41) | collective-permute-done | bytes 607776 | tf_op jit(solution)/shard_map/ppermute | solution.py:63
  287.6 7.6 %collective-permute-done.42 = bf16[32,9496]{1,0:T(8,128)(2,1)S(1)} collective-permute-done((bf16[32,9496]{1,0:T(8,128)(2,1)S(1)}, bf16[32,9496]{1,0:T(8,128)(2,1)S(1)}, u32[]{:S(2)}, u32[]{:S(2)}) %collective-permute-start.42) | collective-permute-done | bytes 607776 | tf_op jit(solution)/shard_map/ppermute | solution.py:63
  300.0 17.6 %collective-permute-done.40 = f32[1,1]{1,0:T(1,128)} collective-permute-done((f32[1,1]{1,0:T(1,128)}, f32[1,1]{1,0:T(1,128)}, u32[]{:S(2)}, u32[]{:S(2)}) %collective-permute-start.40) | collective-permute-done | bytes 36 | tf_op jit(solution)/shard_map/ppermute | solution.py:63
  322.9 5.0 %all-to-all-start.3 = ((f32[8,64,320]{2,1,0:T(8,128)}), f32[8,64,320]{2,1,0:T(8,128)S(1)}, u32[]{:S(2)}, u32[]{:S(2)}) async-start(f32[8,64,320]{2,1,0:T(8,128)} %bitcast.97), calls=%async_computation.3 | async-start | bytes 1572864 | tf_op jit(solution)/shard_map/all_to_all | solution.py:312
  327.9 15.0 %fusion.74 = f32[640,9496]{0,1:T(8,128)} fusion(bf16[256,9496]{1,0:T(8,128)(2,1)} %copy-done.4, bf16[128,640]{1,0:T(8,128)(2,1)S(1)} %bitcast.212, bf16[128,640]{1,0:T(8,128)(2,1)S(1)} %bitcast.211), kind=kOutput, calls=%fused_computation.123 | convolution fusion | flops 3112304640 | bytes 29499392 | tf_op jit(solution)/shard_map/dot_general | solution.py:299
  344.9 9.9 %collective-permute-done.46 = f32[64,320]{1,0:T(8,128)S(1)} collective-permute-done((f32[64,320]{1,0:T(8,128)S(1)}, f32[64,320]{1,0:T(8,128)S(1)}, u32[]{:S(2)}, u32[]{:S(2)}) %collective-permute-start.46) | collective-permute-done | bytes 81952 | tf_op jit(solution)/shard_map/ppermute | solution.py:319
  (267 shorter events, 154.3 us)
Async XLA Ops:
  13.3 34.8 %collective-permute-start.6 = (bf16[8,75968]{1,0:T(8,128)(2,1)}, bf16[8,75968]{1,0:T(8,128)(2,1)S(1)}, u32[]{:S(2)}, u32[]{:S(2)}) collective-permute-start(bf16[8,75968]{1,0:T(8,128)(2,1)} %bitcast.1), channel_id=1, source_target_pairs={{1,0},{2,3},{5,4},{6,7},{9,8},{10,11},{13,12},{14,15},{17,16},{18,... | collective-permute-start | bytes 3646472 | tf_op jit(solution)/shard_map/ppermute | solution.py:85
  44.7 26.6 %collective-permute-start.9 = (f32[16,9496]{1,0:T(8,128)S(1)}, f32[16,9496]{1,0:T(8,128)S(1)}, u32[]{:S(2)}, u32[]{:S(2)}) collective-permute-start(f32[16,9496]{1,0:T(8,128)S(1)} %get-tuple-element.112), channel_id=1, source_target_pairs={{3,2},{0,1},{7,6},{4,5},{11,10},{8,9},{15,14},{12,13},{19,18},{16,... | collective-permute-start | bytes 1823240 | tf_op jit(solution)/shard_map/ppermute | solution.py:63
  60.3 22.4 %collective-permute-start.10 = (f32[16,9496]{1,0:T(8,128)S(1)}, f32[16,9496]{1,0:T(8,128)S(1)}, u32[]{:S(2)}, u32[]{:S(2)}) collective-permute-start(f32[16,9496]{1,0:T(8,128)S(1)} %get-tuple-element.118), channel_id=1, source_target_pairs={{3,2},{0,1},{7,6},{4,5},{11,10},{8,9},{15,14},{12,13},{19,18},{16,... | collective-permute-start | bytes 1823240 | tf_op jit(solution)/shard_map/ppermute | solution.py:63
  91.8 52.8 %all-to-all-start = ((bf16[8,16,9496]{2,1,0:T(8,128)(2,1)}), bf16[8,16,9496]{2,1,0:T(8,128)(2,1)}, u32[]{:S(2)}, u32[]{:S(2)}) async-start(bf16[8,16,9496]{2,1,0:T(8,128)(2,1)} %copy-done.12), calls=%async_computation | async-start | bytes 4915200 | tf_op jit(solution)/shard_map/all_to_all | solution.py:124
  100.1 28.2 %collective-permute-start.17 = (f32[16,9496]{1,0:T(8,128)}, f32[16,9496]{1,0:T(8,128)}, u32[]{:S(2)}, u32[]{:S(2)}) collective-permute-start(f32[16,9496]{1,0:T(8,128)} %copy-done.1), channel_id=1, source_target_pairs={{3,2},{0,1},{7,6},{4,5},{11,10},{8,9},{15,14},{12,13},{19,18},{16,... | collective-permute-start | bytes 1823240 | tf_op jit(solution)/shard_map/ppermute | solution.py:63
  121.2 28.8 %collective-permute-start.21 = (f32[16,9496]{1,0:T(8,128)}, f32[16,9496]{1,0:T(8,128)}, u32[]{:S(2)}, u32[]{:S(2)}) collective-permute-start(f32[16,9496]{1,0:T(8,128)} %get-tuple-element.140), channel_id=1, source_target_pairs={{3,2},{0,1},{7,6},{4,5},{11,10},{8,9},{15,14},{12,13},{19,18},{16,... | collective-permute-start | bytes 1823240 | tf_op jit(solution)/shard_map/ppermute | solution.py:63
  130.2 23.6 %collective-permute-start.20 = (f32[16,9496]{1,0:T(8,128)}, f32[16,9496]{1,0:T(8,128)}, u32[]{:S(2)}, u32[]{:S(2)}) collective-permute-start(f32[16,9496]{1,0:T(8,128)} %add.178), channel_id=1, source_target_pairs={{2,1},{1,2},{6,5},{5,6},{10,9},{9,10},{14,13},{13,14},{18,17},{17,... | collective-permute-start | bytes 1823240 | tf_op jit(solution)/shard_map/ppermute | solution.py:63
  133.7 23.4 %collective-permute-start.19 = (f32[16,9496]{1,0:T(8,128)}, f32[16,9496]{1,0:T(8,128)}, u32[]{:S(2)}, u32[]{:S(2)}) collective-permute-start(f32[16,9496]{1,0:T(8,128)} %add.179), channel_id=1, source_target_pairs={{1,0},{2,3},{5,4},{6,7},{9,8},{10,11},{13,12},{14,15},{17,16},{18,... | collective-permute-start | bytes 1823240 | tf_op jit(solution)/shard_map/ppermute | solution.py:63
  136.9 31.7 %collective-permute-start.24 = (f32[16,9496]{1,0:T(8,128)}, f32[16,9496]{1,0:T(8,128)}, u32[]{:S(2)}, u32[]{:S(2)}) collective-permute-start(f32[16,9496]{1,0:T(8,128)} %get-tuple-element.144), channel_id=1, source_target_pairs={{3,2},{0,1},{7,6},{4,5},{11,10},{8,9},{15,14},{12,13},{19,18},{16,... | collective-permute-start | bytes 1823240 | tf_op jit(solution)/shard_map/ppermute | solution.py:63
  152.3 21.2 %collective-permute-start.23 = (f32[16,9496]{1,0:T(8,128)}, f32[16,9496]{1,0:T(8,128)}, u32[]{:S(2)}, u32[]{:S(2)}) collective-permute-start(f32[16,9496]{1,0:T(8,128)} %add.181), channel_id=1, source_target_pairs={{2,1},{1,2},{6,5},{5,6},{10,9},{9,10},{14,13},{13,14},{18,17},{17,... | collective-permute-start | bytes 1823240 | tf_op jit(solution)/shard_map/ppermute | solution.py:63
  170.7 25.0 %collective-permute-start.26 = (f32[16,9496]{1,0:T(8,128)}, f32[16,9496]{1,0:T(8,128)}, u32[]{:S(2)}, u32[]{:S(2)}) collective-permute-start(f32[16,9496]{1,0:T(8,128)} %add.184), channel_id=1, source_target_pairs={{2,1},{1,2},{6,5},{5,6},{10,9},{9,10},{14,13},{13,14},{18,17},{17,... | collective-permute-start | bytes 1823240 | tf_op jit(solution)/shard_map/ppermute | solution.py:63
  183.4 21.5 %collective-permute-start.25 = (f32[16,9496]{1,0:T(8,128)}, f32[16,9496]{1,0:T(8,128)S(1)}, u32[]{:S(2)}, u32[]{:S(2)}) collective-permute-start(f32[16,9496]{1,0:T(8,128)} %add.185), channel_id=1, source_target_pairs={{1,0},{2,3},{5,4},{6,7},{9,8},{10,11},{13,12},{14,15},{17,16},{18,... | collective-permute-start | bytes 1823240 | tf_op jit(solution)/shard_map/ppermute | solution.py:63
  187.6 20.7 %collective-permute-start.28 = (bf16[32,9496]{1,0:T(8,128)(2,1)}, bf16[32,9496]{1,0:T(8,128)(2,1)}, u32[]{:S(2)}, u32[]{:S(2)}) collective-permute-start(bf16[32,9496]{1,0:T(8,128)(2,1)} %pad_maximum_fusion.4), channel_id=1, source_target_pairs={{3,2},{0,1},{7,6},{4,5},{11,10},{8,9},{15,14},{12,13},{19,18},{16,... | collective-permute-start | bytes 1823240 | tf_op jit(solution)/shard_map/ppermute | solution.py:63
  197.8 21.7 %collective-permute-start.27 = (f32[16,9496]{1,0:T(8,128)}, f32[16,9496]{1,0:T(8,128)}, u32[]{:S(2)}, u32[]{:S(2)}) collective-permute-start(f32[16,9496]{1,0:T(8,128)} %add.187), channel_id=1, source_target_pairs={{1,0},{2,3},{5,4},{6,7},{9,8},{10,11},{13,12},{14,15},{17,16},{18,... | collective-permute-start | bytes 1823240 | tf_op jit(solution)/shard_map/ppermute | solution.py:63
  208.4 22.9 %collective-permute-start.30 = (bf16[32,9496]{1,0:T(8,128)(2,1)}, bf16[32,9496]{1,0:T(8,128)(2,1)}, u32[]{:S(2)}, u32[]{:S(2)}) collective-permute-start(bf16[32,9496]{1,0:T(8,128)(2,1)} %collective-permute-done.28), channel_id=1, source_target_pairs={{2,1},{1,2},{6,5},{5,6},{10,9},{9,10},{14,13},{13,14},{18,17},{17,... | collective-permute-start | bytes 1823240 | tf_op jit(solution)/shard_map/ppermute | solution.py:63
  234.8 33.1 %collective-permute-start.36 = (bf16[16,9496]{1,0:T(8,128)(2,1)S(1)}, bf16[16,9496]{1,0:T(8,128)(2,1)S(1)}, u32[]{:S(2)}, u32[]{:S(2)}) collective-permute-start(bf16[16,9496]{1,0:T(8,128)(2,1)S(1)} %fusion.66), channel_id=1, source_target_pairs={{3,2},{0,1},{7,6},{4,5},{11,10},{8,9},{15,14},{12,13},{19,18},{16,... | collective-permute-start | bytes 911624 | tf_op jit(solution)/shard_map/ppermute | solution.py:63
  238.9 28.3 %collective-permute-start.32 = (bf16[32,9496]{1,0:T(8,128)(2,1)S(1)}, bf16[32,9496]{1,0:T(8,128)(2,1)S(1)}, u32[]{:S(2)}, u32[]{:S(2)}) collective-permute-start(bf16[32,9496]{1,0:T(8,128)(2,1)S(1)} %pad_maximum_fusion.6), channel_id=1, source_target_pairs={{3,2},{0,1},{7,6},{4,5},{11,10},{8,9},{15,14},{12,13},{19,18},{16,... | collective-permute-start | bytes 1823240 | tf_op jit(solution)/shard_map/ppermute | solution.py:63
  240.2 25.6 %collective-permute-start.33 = (bf16[32,9496]{1,0:T(8,128)(2,1)}, bf16[32,9496]{1,0:T(8,128)(2,1)S(1)}, u32[]{:S(2)}, u32[]{:S(2)}) collective-permute-start(bf16[32,9496]{1,0:T(8,128)(2,1)} %collective-permute-done.29), channel_id=1, source_target_pairs={{2,1},{1,2},{6,5},{5,6},{10,9},{9,10},{14,13},{13,14},{18,17},{17,... | collective-permute-start | bytes 1823240 | tf_op jit(solution)/shard_map/ppermute | solution.py:63
  242.2 26.4 %collective-permute-start.35 = (bf16[16,9496]{1,0:T(8,128)(2,1)S(1)}, bf16[16,9496]{1,0:T(8,128)(2,1)S(1)}, u32[]{:S(2)}, u32[]{:S(2)}) collective-permute-start(bf16[16,9496]{1,0:T(8,128)(2,1)S(1)} %fusion.65), channel_id=1, source_target_pairs={{3,2},{0,1},{7,6},{4,5},{11,10},{8,9},{15,14},{12,13},{19,18},{16,... | collective-permute-start | bytes 911624 | tf_op jit(solution)/shard_map/ppermute | solution.py:63
  265.9 29.4 %collective-permute-start.42 = (bf16[32,9496]{1,0:T(8,128)(2,1)S(1)}, bf16[32,9496]{1,0:T(8,128)(2,1)S(1)}, u32[]{:S(2)}, u32[]{:S(2)}) collective-permute-start(bf16[32,9496]{1,0:T(8,128)(2,1)S(1)} %collective-permute-done.33), channel_id=1, source_target_pairs={{1,0},{2,3},{5,4},{6,7},{9,8},{10,11},{13,12},{14,15},{17,16},{18,... | collective-permute-start | bytes 1823240 | tf_op jit(solution)/shard_map/ppermute | solution.py:63
  282.1 36.8 %collective-permute-start.43 = (bf16[32,9496]{1,0:T(8,128)(2,1)S(1)}, bf16[32,9496]{1,0:T(8,128)(2,1)S(1)}, u32[]{:S(2)}, u32[]{:S(2)}) collective-permute-start(bf16[32,9496]{1,0:T(8,128)(2,1)S(1)} %collective-permute-done.34), channel_id=1, source_target_pairs={{1,0},{2,3},{5,4},{6,7},{9,8},{10,11},{13,12},{14,15},{17,16},{18,... | collective-permute-start | bytes 1823240 | tf_op jit(solution)/shard_map/ppermute | solution.py:63
  285.0 33.9 %collective-permute-start.44 = (bf16[16,9496]{1,0:T(8,128)(2,1)S(1)}, bf16[16,9496]{1,0:T(8,128)(2,1)S(1)}, u32[]{:S(2)}, u32[]{:S(2)}) collective-permute-start(bf16[16,9496]{1,0:T(8,128)(2,1)S(1)} %collective-permute-done.39), channel_id=1, source_target_pairs={{1,0},{2,3},{5,4},{6,7},{9,8},{10,11},{13,12},{14,15},{17,16},{18,... | collective-permute-start | bytes 911624 | tf_op jit(solution)/shard_map/ppermute | solution.py:63
  286.3 32.7 %collective-permute-start.45 = (bf16[16,9496]{1,0:T(8,128)(2,1)S(1)}, bf16[16,9496]{1,0:T(8,128)(2,1)S(1)}, u32[]{:S(2)}, u32[]{:S(2)}) collective-permute-start(bf16[16,9496]{1,0:T(8,128)(2,1)S(1)} %collective-permute-done.38), channel_id=1, source_target_pairs={{1,0},{2,3},{5,4},{6,7},{9,8},{10,11},{13,12},{14,15},{17,16},{18,... | collective-permute-start | bytes 911624 | tf_op jit(solution)/shard_map/ppermute | solution.py:63
  295.5 22.1 %collective-permute-start.40 = (f32[1,1]{1,0:T(1,128)}, f32[1,1]{1,0:T(1,128)}, u32[]{:S(2)}, u32[]{:S(2)}) collective-permute-start(f32[1,1]{1,0:T(1,128)} %collective-permute-done.37), channel_id=1, source_target_pairs={{1,0},{2,3},{5,4},{6,7},{9,8},{10,11},{13,12},{14,15},{17,16},{18,... | collective-permute-start | bytes 20 | tf_op jit(solution)/shard_map/ppermute | solution.py:63
  (52 other events, 765.4 us)

commit v6 on v5

--- a/solution.py
+++ b/solution.py
@@ -1,3 +1,5 @@
+import functools
+
 import jax
 import jax.numpy as jnp
 from jax import lax
@@ -44,6 +46,39 @@
     )(hidden, head_rows)
 
 
+def stats_kernel(count, *refs):
+    student_refs, target_ref, out_ref = refs[:count], refs[count], refs[count + 1]
+    height = student_refs[0].shape[0]
+    for i, student_ref in enumerate(student_refs):
+        at = pl.ds(i * height, height)
+        student = student_ref[...]
+        target = target_ref[i].astype(jnp.float32)
+        student_top = jnp.max(student, axis=1, keepdims=True)
+        target_top = jnp.max(target, axis=1, keepdims=True)
+        target_exp = jnp.exp(target - target_top)
+        out_ref[at, 0:1] = student_top
+        out_ref[at, 1:2] = target_top
+        out_ref[at, 2:3] = jnp.sum(jnp.exp(student - student_top), axis=1, keepdims=True)
+        out_ref[at, 3:4] = jnp.sum(target_exp, axis=1, keepdims=True)
+        out_ref[at, 4:5] = jnp.sum(target_exp * (target - student), axis=1, keepdims=True)
+
+
+def row_stats(students, targets):
+    count = len(students)
+    height, cols = students[0].shape
+    stats = pl.pallas_call(
+        functools.partial(stats_kernel, count),
+        out_shape=jax.ShapeDtypeStruct((count * height, 5), jnp.float32),
+        compiler_params=pltpu.CompilerParams(
+            vmem_limit_bytes=(8 * count * height * cols + 16 * 1024 * 1024)),
+        cost_estimate=pl.CostEstimate(
+            flops=12 * count * height * cols,
+            bytes_accessed=6 * count * height * cols,
+            transcendentals=2 * count * height * cols),
+    )(*students, targets)
+    return stats.T
+
+
 def body(hidden_states, head_weight, teacher_logits):
     seq_count = lax.axis_size("seq")
     vocab_count = lax.axis_size("vocab")
@@ -85,16 +120,12 @@
         lax.ppermute(mine, "seq", [(j, 0), (last - j, last)]) for j in range(1, half)
     ]
 
-    middle = chunks // 2
-    groups = [list(range(middle)), list(range(middle, chunks))]
-    loads = [[[i, i + 1] for i in range(0, middle - 1, 2)] + [[middle - 1]] * (middle % 2),
-             [[middle, middle + 1]] + [[i] for i in range(middle + 2, chunks)]]
+    loads = [[i, i + 1] for i in range(0, chunks - 3, 2)] + [[chunks - 2], [chunks - 1]]
     moving = [None] * chunks
     students = [None] * chunks
     targets = []
-    pieces = []
-    locals_ = [None] * chunks
-    exchanged = {}
+    locals_ = []
+    exchanged = []
     travels = {}
     settled_loss = []
     tie = []
@@ -113,44 +144,29 @@
             tie[:] = [value]
         moving[i] = hop(value, j)
 
-    def cut_teacher():
+    def exchange_teacher():
         rows_held = tied(jnp.concatenate(held, axis=0))
-        pieces.append(jnp.stack(
-            [rows_held[:, v * cols:(v + 1) * cols] for v in range(vocab_count)]))
-        tie[:] = pieces
-
-    def exchange_teacher():
-        targets.extend(
-            lax.all_to_all(tied(pieces[0]), "vocab", split_axis=0, concat_axis=0, tiled=True))
+        pieces = jnp.stack([rows_held[:, v * cols:(v + 1) * cols] for v in range(vocab_count)])
+        tie[:] = [pieces]
+        targets.append(
+            lax.all_to_all(pieces, "vocab", split_axis=0, concat_axis=0, tiled=True))
 
     def hold_teacher():
         held[:] = lax.optimization_barrier((*held, *tie))[:half]
         tie[:] = [held[-1]]
 
-    def local_stats(i):
-        student = tied(students[i])
-        target = targets[i].astype(jnp.float32)
-        student_top = jnp.max(student, axis=1)
-        target_top = jnp.max(target, axis=1)
-        target_exp = jnp.exp(target - target_top[:, None])
-        locals_[i] = jnp.stack([
-            student_top,
-            target_top,
-            jnp.sum(jnp.exp(student - student_top[:, None]), axis=1),
-            jnp.sum(target_exp, axis=1),
-            jnp.sum(target_exp * (target - student), axis=1),
-        ])
-        tie[:] = [locals_[i]]
-
-    def exchange_stats(g):
-        stats = jnp.concatenate([locals_[i] for i in groups[g]], axis=1)
-        tie[:] = [stats]
+    def hold_targets():
+        targets[0] = tied(targets[0])
+
+    def local_stats(first, stop):
+        locals_.append(row_stats(
+            [tied(students[first]), *students[first + 1:stop]], targets[0][first:stop]))
+        tie[:] = [locals_[-1]]
+
+    def exchange_stats():
+        stats = jnp.concatenate(locals_, axis=1)
         stats = jnp.broadcast_to(stats, (vocab_count, *stats.shape))
         stats = lax.all_to_all(stats, "vocab", split_axis=0, concat_axis=0, tiled=True)
-        exchanged[g] = stats
-
-    def merge_stats(g):
-        stats = tied(exchanged[g])
         student_max = jnp.max(stats[:, 0], axis=0)
         teacher_max = jnp.max(stats[:, 1], axis=0)
         student_scale = jnp.exp(stats[:, 0] - student_max)
@@ -158,18 +174,17 @@
         student_sum = jnp.sum(stats[:, 2] * student_scale, axis=0)
         teacher_sum = jnp.sum(stats[:, 3] * teacher_scale, axis=0)
         cross = jnp.sum(stats[:, 4] * teacher_scale, axis=0)
-        exchanged[g] = lax.optimization_barrier(
-            (student_max, student_sum, teacher_max, teacher_sum, cross))
-        tie[:] = [exchanged[g][0]]
-
-    def form_grads(g, p):
-        student_max, student_sum, teacher_max, teacher_sum, _ = exchanged[g]
+        exchanged.extend(lax.optimization_barrier(
+            (student_max, student_sum, teacher_max, teacher_sum, cross)))
+        tie[:] = [exchanged[0]]
+
+    def form_grads(p):
+        student_max, student_sum, teacher_max, teacher_sum, _ = exchanged
         grads = []
-        for i in loads[g][p]:
-            first = (i - groups[g][0]) * chunk
-            at = slice(first, first + chunk)
+        for i in loads[p]:
+            at = slice(i * chunk, (i + 1) * chunk)
             student = tied(students[i])
-            target = targets[i].astype(jnp.float32)
+            target = targets[0][i].astype(jnp.float32)
             grads.append((
                 LOSS_SCALE * (
                     jnp.exp(student - student_max[at, None]) / student_sum[at, None]
@@ -178,19 +193,18 @@
             ).astype(jnp.bfloat16))
         grad = jnp.concatenate(grads, axis=0)
         tie[:] = [grad]
-        travels[g, p] = [grad]
-
-    def send_grad(g, p, j):
-        value = travels[g, p][j] if j == 0 else tied(travels[g, p][j])
-        travels[g, p].append(hop(value, j))
+        travels[p] = [grad]
+
+    def send_grad(p, j):
+        value = travels[p][j] if j == 0 else tied(travels[p][j])
+        travels[p].append(hop(value, j))
 
     def sum_up(i):
         students[i] = own_part[i] + tied(moving[i])
         tie[:] = [students[i]]
 
     def loss():
-        student_max, student_sum, teacher_max, teacher_sum, cross = (
-            jnp.concatenate(both) for both in zip(*exchanged.values()))
+        student_max, student_sum, teacher_max, teacher_sum, cross = exchanged
         divergence = jnp.sum(
             cross / teacher_sum
             - teacher_max
@@ -241,32 +255,25 @@
         plan(i + hops, 4, sum_up, i)
     end = chunks + hops - 1
     plan(2, 0, hold_teacher)
-    plan(3, 15, cut_teacher)
-    plan(4, 15, exchange_teacher)
-    stats_slot = middle + hops
-    for i in range(chunks):
-        wait = min(6 + i // 2, stats_slot) if i < middle else i + hops + (i == middle)
-        plan(max(i + hops, wait), 15, local_stats, i)
-    early_keys, late_keys = [], []
-    for g, slot in enumerate((stats_slot, end)):
-        plan(slot, 18, exchange_stats, g)
-        plan(slot + 1, 20, merge_stats, g)
-        for p in range(len(loads[g])):
-            (late_keys if g else early_keys).append((g, p))
-            first = slot + 1 + (0 if g else p)
-            plan(first, 40 + 2 * p, form_grads, g, p)
-            plan(first, 41 + 2 * p, send_grad, g, p, 0)
-            for j in range(1, hops):
-                if g == 0:
-                    plan(first + j, 30 - j if first + j <= end else 90 - j, send_grad, g, p, j)
-                else:
-                    plan(first + j + (p + 1) // 2, 120 + 10 * j + p, send_grad, g, p, j)
-    plan(end + 1, 60, loss)
+    plan(3, 15, exchange_teacher)
+    plan(6, 0, hold_targets)
+    plan(end - 1, 15, local_stats, 0, chunks - 2)
+    plan(end, 15, local_stats, chunks - 2, chunks)
+    plan(end, 16, exchange_stats)
+    count = len(loads)
+    early_keys, late_keys = list(range(count // 2)), list(range(count // 2, count))
+    for p in range(count):
+        step = min(p, count - 2)
+        plan(end + max(step, 1), 40 + 2 * p, form_grads, p)
+        plan(end + max(step, 1), 41 + 2 * p, send_grad, p, 0)
+        for j in range(1, hops):
+            plan(end + 1 + step + j, 30 - j, send_grad, p, j)
+    plan(end + 1, 35, loss)
     for j in range(hops):
-        plan(end + 1 + j + (j > 0), 1510, send_loss, j)
+        plan(end + 1, 36 if j == 0 else 41 + 2 * min(j - 1, 1), send_loss, j)
+    plan(end + 1, 50, settle_loss)
     final = max(slots)
-    plan(final, 1600, early_feature)
-    plan(final, 1700, settle_loss)
+    plan(final, 700, early_feature)
 
     first_part = jnp.dot(
         ordered[half_tokens:half_tokens + chunk], head_weight, preferred_element_type=jnp.float32)

time: 359 us -> 343 us (0.955)
  other arithmetic: 67.7 us -> 29.8 us
  waiting for transfers between devices: 110 us -> 134 us
  starting transfers between devices: 121 us -> 108 us
  local copies, waits for them, and re-layouts: 9.08 us -> 17.7 us
    ppermute x42, waiting for transfers between devices: 91.6 us -> 115 us  [hop(): return lax.ppermute(value, 'seq', [(last - j, last - j - 1), (j, j + 1)])]
    reduce_sum x10 -> x2, other arithmetic: 11.9 us -> 0.05 us  [the longest x1 0.02 us: exchange_stats(): student_sum = jnp.sum(stats[:, 2] * student_scale, axis=0)]
    add x16, other arithmetic: 19.4 us -> 11 us  [send(): value = part + tied(moving[i])]
    reduce_max x19 -> x2, other arithmetic: 8.13 us -> 0.03 us  [the longest x1 0.02 us: exchange_stats(): student_max = jnp.max(stats[:, 0], axis=0)]
    ppermute x42, starting transfers between devices: 95.1 us -> 87.6 us  [hop(): return lax.ppermute(value, 'seq', [(last - j, last - j - 1), (j, j + 1)])]
    add x8, other arithmetic: 11.1 us -> 5.62 us  [sum_up(): students[i] = own_part[i] + tied(moving[i])]
    unnamed x61 -> x79, local copies, waits for them, and re-layouts: 5.49 us -> 9.94 us
    all_to_all x2 -> x1, starting transfers between devices: 8.42 us -> 4.22 us  [exchange_stats(): lax.all_to_all(stats, 'vocab', split_axis=0, concat_axis=0, tiled=True)]
  transfers between devices with their start and end apart: 51 -> 50, of which waited for: 17 -> 26; matrix products, arithmetic and copies ran while one was open for 26% -> 16% of each run, Pallas kernels for 4% -> 5%
where the time goes in v6:
time: 343 us; the launch traced here: 341 us
  waiting for transfers between devices  134 us (39%)
  starting transfers between devices  108 us (31%)
  other arithmetic  29.8 us (9%)
  matrix products  27.6 us (8%)
  Pallas kernels  18.1 us (5%)
  local copies, waits for them, and re-layouts  17.7 us (5%)
  between operations  5.47 us (2%)
    ppermute x42, waiting for transfers between devices, hop(): return lax.ppermute(value, 'seq', [(last - j, last - j - 1), (j, j + 1)])  115 us
    ppermute x42, starting transfers between devices, hop(): return lax.ppermute(value, 'seq', [(last - j, last - j - 1), (j, j + 1)])  87.6 us
    pallas_call x1, Pallas kernels, partial_students(): pl.pallas_call(partial_kernel, grid=(pl.cdiv(cols, tile),), in_specs=[pl....  15.1 us
    dot_general x1, matrix products, body(): lax.dot_general(all_grads, matching, (((0,), (0,)), ((), ())), preferred_...  15 us
    add x16, other arithmetic, send(): value = part + tied(moving[i])  11 us
    unnamed x79, local copies, waits for them, and re-layouts  9.94 us
    ppermute x1, waiting for transfers between devices, body(): hidden_grad = lax.ppermute(feature, ('vocab', 'seq'), pairs)  9.93 us
    dot_general x1, matrix products, body(): jnp.dot(ordered[half_tokens:half_tokens + chunk], head_weight, preferred_...  8.45 us
  transfers between devices with their start and end apart: 50, of which 26 were waited for; matrix products, arithmetic and copies ran while one was open for 16% of the time, Pallas kernels for 5%

profile of v6, /device:TPU:2, one launch (start us, length us, event | category | flops | bytes accessed | tf_op | source)
XLA Modules:
  0.0 340.9 jit_solution(18161032095267658393)
XLA Ops:
  14.9 8.4 %fusion.58 = f32[16,9496]{1,0:T(8,128)S(1)} fusion(bf16[640,9496]{0,1:T(8,128)(2,1)} %param.4, bf16[256,640]{1,0:T(8,128)(2,1)S(1)} %bitcast.104), kind=kOutput, calls=%fused_computation.108 | convolution fusion | flops 194478080 | bytes 12783104 | tf_op jit(solution)/shard_map/dot_general | solution.py:278
  23.4 4.9 %collective-permute-start.3 = (f32[16,9496]{1,0:T(8,128)S(1)}, f32[16,9496]{1,0:T(8,128)S(1)}, u32[]{:S(2)}, u32[]{:S(2)}) collective-permute-start(f32[16,9496]{1,0:T(8,128)S(1)} %fusion.58), channel_id=1, source_target_pairs={{3,2},{0,1},{7,6},{4,5},{11,10},{8,9},{15,14},{12,13},{19,18},{16,... | collective-permute-start | bytes 1823240 | tf_op jit(solution)/shard_map/ppermute | solution.py:98
  28.4 15.1 %shard_map.58 = (f32[16,9496]{1,0:T(8,128)S(1)}, f32[16,9496]{1,0:T(8,128)S(1)}, f32[16,9496]{1,0:T(8,128)S(1)}, f32[16,9496]{1,0:T(8,128)S(1)}, f32[16,9496]{1,...) custom-call(bf16[240,640]{1,0:T(8,128)(2,1)S(1)} %pad_maximum_fusion, ...), custom_call_target="tpu_custom_call" | custom-call | flops 2917171200 | bytes 21271040 | tf_op jit(solution)/shard_map/pallas_call | solution.py:32
  50.9 10.0 %collective-permute-done.5 = f32[16,9496]{1,0:T(8,128)S(1)} collective-permute-done((f32[16,9496]{1,0:T(8,128)S(1)}, f32[16,9496]{1,0:T(8,128)S(1)}, u32[]{:S(2)}, u32[]{:S(2)}) %collective-permute-start.5) | collective-permute-done | bytes 607776 | tf_op jit(solution)/shard_map/ppermute | solution.py:98
  64.9 7.5 %collective-permute-done.9 = f32[16,9496]{1,0:T(8,128)S(1)} collective-permute-done((f32[16,9496]{1,0:T(8,128)S(1)}, f32[16,9496]{1,0:T(8,128)S(1)}, u32[]{:S(2)}, u32[]{:S(2)}) %collective-permute-start.9) | collective-permute-done | bytes 607776 | tf_op jit(solution)/shard_map/ppermute | solution.py:98
  74.2 4.9 %collective-permute-done.7 = f32[16,9496]{1,0:T(8,128)S(1)} collective-permute-done((f32[16,9496]{1,0:T(8,128)S(1)}, f32[16,9496]{1,0:T(8,128)S(1)}, u32[]{:S(2)}, u32[]{:S(2)}) %collective-permute-start.7) | collective-permute-done | bytes 607776 | tf_op jit(solution)/shard_map/ppermute | solution.py:98
  86.0 4.8 %all-to-all-start = ((bf16[8,16,9496]{2,1,0:T(8,128)(2,1)}), bf16[8,16,9496]{2,1,0:T(8,128)(2,1)}, u32[]{:S(2)}, u32[]{:S(2)}) async-start(bf16[8,16,9496]{2,1,0:T(8,128)(2,1)} %bitcast_dynamic-update-slice_fusion), calls=%async_computation | async-start | bytes 4915200 | tf_op jit(solution)/shard_map/all_to_all | solution.py:152
  95.1 4.6 %collective-permute-start.14 = (f32[16,9496]{1,0:T(8,128)}, f32[16,9496]{1,0:T(8,128)S(1)}, u32[]{:S(2)}, u32[]{:S(2)}) collective-permute-start(f32[16,9496]{1,0:T(8,128)} %copy-done.23), channel_id=1, source_target_pairs={{3,2},{0,1},{7,6},{4,5},{11,10},{8,9},{15,14},{12,13},{19,18},{16,... | collective-permute-start | bytes 1823240 | tf_op jit(solution)/shard_map/ppermute | solution.py:98
  99.7 7.8 %collective-permute-done.11 = f32[16,9496]{1,0:T(8,128)S(1)} collective-permute-done((f32[16,9496]{1,0:T(8,128)}, f32[16,9496]{1,0:T(8,128)S(1)}, u32[]{:S(2)}, u32[]{:S(2)}) %collective-permute-start.11) | collective-permute-done | bytes 607776 | tf_op jit(solution)/shard_map/ppermute | solution.py:98
  111.6 7.2 %collective-permute-start.19 = (f32[16,9496]{1,0:T(8,128)}, f32[16,9496]{1,0:T(8,128)}, u32[]{:S(2)}, u32[]{:S(2)}) collective-permute-start(f32[16,9496]{1,0:T(8,128)} %get-tuple-element.121), channel_id=1, source_target_pairs={{3,2},{0,1},{7,6},{4,5},{11,10},{8,9},{15,14},{12,13},{19,18},{16,... | collective-permute-start | bytes 1823240 | tf_op jit(solution)/shard_map/ppermute | solution.py:98
  128.3 5.1 %collective-permute-start.16 = (f32[16,9496]{1,0:T(8,128)}, f32[16,9496]{1,0:T(8,128)}, u32[]{:S(2)}, u32[]{:S(2)}) collective-permute-start(f32[16,9496]{1,0:T(8,128)} %get-tuple-element.125), channel_id=1, source_target_pairs={{3,2},{0,1},{7,6},{4,5},{11,10},{8,9},{15,14},{12,13},{19,18},{16,... | collective-permute-start | bytes 1823240 | tf_op jit(solution)/shard_map/ppermute | solution.py:98
  151.3 5.8 %collective-permute-done.22 = f32[16,9496]{1,0:T(8,128)S(1)} collective-permute-done((f32[16,9496]{1,0:T(8,128)S(1)}, f32[16,9496]{1,0:T(8,128)S(1)}, u32[]{:S(2)}, u32[]{:S(2)}) %collective-permute-start.22) | collective-permute-done | bytes 607776 | tf_op jit(solution)/shard_map/ppermute | solution.py:98
  162.3 7.3 %collective-permute-done.26 = f32[16,9496]{1,0:T(8,128)S(1)} collective-permute-done((f32[16,9496]{1,0:T(8,128)S(1)}, f32[16,9496]{1,0:T(8,128)S(1)}, u32[]{:S(2)}, u32[]{:S(2)}) %collective-permute-start.26) | collective-permute-done | bytes 607776 | tf_op jit(solution)/shard_map/ppermute | solution.py:98
  176.7 6.1 %collective-permute-done.24 = f32[16,9496]{1,0:T(8,128)} collective-permute-done((f32[16,9496]{1,0:T(8,128)}, f32[16,9496]{1,0:T(8,128)}, u32[]{:S(2)}, u32[]{:S(2)}) %collective-permute-start.24) | collective-permute-done | bytes 607776 | tf_op jit(solution)/shard_map/ppermute | solution.py:98
  186.3 9.2 %collective-permute-done.27 = f32[16,9496]{1,0:T(8,128)} collective-permute-done((f32[16,9496]{1,0:T(8,128)}, f32[16,9496]{1,0:T(8,128)}, u32[]{:S(2)}, u32[]{:S(2)}) %collective-permute-start.27) | collective-permute-done | bytes 607776 | tf_op jit(solution)/shard_map/ppermute | solution.py:98
  229.9 6.3 %collective-permute-start.39 = (bf16[32,9496]{1,0:T(8,128)(2,1)S(1)}, bf16[32,9496]{1,0:T(8,128)(2,1)S(1)}, u32[]{:S(2)}, u32[]{:S(2)}) collective-permute-start(bf16[32,9496]{1,0:T(8,128)(2,1)S(1)} %pad_maximum_fusion.6), channel_id=1, source_target_pairs={{3,2},{0,1},{7,6},{4,5},{11,10},{8,9},{15,14},{12,13},{19,18},{16,... | collective-permute-start | bytes 1823240 | tf_op jit(solution)/shard_map/ppermute | solution.py:98
  242.2 7.1 %collective-permute-start.38 = (bf16[16,9496]{1,0:T(8,128)(2,1)S(1)}, bf16[16,9496]{1,0:T(8,128)(2,1)S(1)}, u32[]{:S(2)}, u32[]{:S(2)}) collective-permute-start(bf16[16,9496]{1,0:T(8,128)(2,1)S(1)} %fusion.39), channel_id=1, source_target_pairs={{3,2},{0,1},{7,6},{4,5},{11,10},{8,9},{15,14},{12,13},{19,18},{16,... | collective-permute-start | bytes 911624 | tf_op jit(solution)/shard_map/ppermute | solution.py:98
  252.6 4.6 %collective-permute-start.37 = (bf16[16,9496]{1,0:T(8,128)(2,1)S(1)}, bf16[16,9496]{1,0:T(8,128)(2,1)S(1)}, u32[]{:S(2)}, u32[]{:S(2)}) collective-permute-start(bf16[16,9496]{1,0:T(8,128)(2,1)S(1)} %fusion.40), channel_id=1, source_target_pairs={{3,2},{0,1},{7,6},{4,5},{11,10},{8,9},{15,14},{12,13},{19,18},{16,... | collective-permute-start | bytes 911624 | tf_op jit(solution)/shard_map/ppermute | solution.py:98
  259.2 8.0 %collective-permute-done.34 = bf16[32,9496]{1,0:T(8,128)(2,1)S(1)} collective-permute-done((bf16[32,9496]{1,0:T(8,128)(2,1)S(1)}, bf16[32,9496]{1,0:T(8,128)(2,1)S(1)}, u32[]{:S(2)}, u32[]{:S(2)}) %collective-permute-start.34) | collective-permute-done | bytes 607776 | tf_op jit(solution)/shard_map/ppermute | solution.py:98
  270.3 8.5 %collective-permute-done.36 = bf16[32,9496]{1,0:T(8,128)(2,1)S(1)} collective-permute-done((bf16[32,9496]{1,0:T(8,128)(2,1)S(1)}, bf16[32,9496]{1,0:T(8,128)(2,1)S(1)}, u32[]{:S(2)}, u32[]{:S(2)}) %collective-permute-start.36) | collective-permute-done | bytes 607776 | tf_op jit(solution)/shard_map/ppermute | solution.py:98
  284.9 10.8 %collective-permute-done.43 = bf16[32,9496]{1,0:T(8,128)(2,1)S(1)} collective-permute-done((bf16[32,9496]{1,0:T(8,128)(2,1)S(1)}, bf16[32,9496]{1,0:T(8,128)(2,1)S(1)}, u32[]{:S(2)}, u32[]{:S(2)}) %collective-permute-start.43) | collective-permute-done | bytes 607776 | tf_op jit(solution)/shard_map/ppermute | solution.py:98
  295.7 5.6 %collective-permute-done.44 = bf16[16,9496]{1,0:T(8,128)(2,1)S(1)} collective-permute-done((bf16[16,9496]{1,0:T(8,128)(2,1)S(1)}, bf16[16,9496]{1,0:T(8,128)(2,1)S(1)}, u32[]{:S(2)}, u32[]{:S(2)}) %collective-permute-start.44) | collective-permute-done | bytes 303904 | tf_op jit(solution)/shard_map/ppermute | solution.py:98
  312.2 15.0 %fusion.42 = f32[640,9496]{0,1:T(8,128)} fusion(bf16[256,9496]{1,0:T(8,128)(2,1)} %copy-done.26, bf16[128,640]{1,0:T(8,128)(2,1)S(1)} %bitcast.115, bf16[128,640]{1,0:T(8,128)(2,1)S(1)} %bitcast.114), kind=kOutput, calls=%fused_computation.67 | convolution fusion | flops 3112304640 | bytes 29499392 | tf_op jit(solution)/shard_map/dot_general | solution.py:306
  329.2 9.9 %collective-permute-done.46 = f32[64,320]{1,0:T(8,128)S(1)} collective-permute-done((f32[64,320]{1,0:T(8,128)S(1)}, f32[64,320]{1,0:T(8,128)S(1)}, u32[]{:S(2)}, u32[]{:S(2)}) %collective-permute-start.46) | collective-permute-done | bytes 81952 | tf_op jit(solution)/shard_map/ppermute | solution.py:326
  (242 shorter events, 150.9 us)
Async XLA Ops:
  13.3 37.6 %collective-permute-start.6 = (bf16[8,75968]{1,0:T(8,128)(2,1)}, bf16[8,75968]{1,0:T(8,128)(2,1)}, u32[]{:S(2)}, u32[]{:S(2)}) collective-permute-start(bf16[8,75968]{1,0:T(8,128)(2,1)} %bitcast.1), channel_id=1, source_target_pairs={{1,0},{2,3},{5,4},{6,7},{9,8},{10,11},{13,12},{14,15},{17,16},{18,... | collective-permute-start | bytes 3646472 | tf_op jit(solution)/shard_map/ppermute | solution.py:120
  23.4 23.3 %collective-permute-start.3 = (f32[16,9496]{1,0:T(8,128)S(1)}, f32[16,9496]{1,0:T(8,128)S(1)}, u32[]{:S(2)}, u32[]{:S(2)}) collective-permute-start(f32[16,9496]{1,0:T(8,128)S(1)} %fusion.58), channel_id=1, source_target_pairs={{3,2},{0,1},{7,6},{4,5},{11,10},{8,9},{15,14},{12,13},{19,18},{16,... | collective-permute-start | bytes 1823240 | tf_op jit(solution)/shard_map/ppermute | solution.py:98
  47.4 24.9 %collective-permute-start.9 = (f32[16,9496]{1,0:T(8,128)S(1)}, f32[16,9496]{1,0:T(8,128)S(1)}, u32[]{:S(2)}, u32[]{:S(2)}) collective-permute-start(f32[16,9496]{1,0:T(8,128)S(1)} %get-tuple-element.99), channel_id=1, source_target_pairs={{3,2},{0,1},{7,6},{4,5},{11,10},{8,9},{15,14},{12,13},{19,18},{16,... | collective-permute-start | bytes 1823240 | tf_op jit(solution)/shard_map/ppermute | solution.py:98
  61.8 17.3 %collective-permute-start.7 = (f32[16,9496]{1,0:T(8,128)S(1)}, f32[16,9496]{1,0:T(8,128)S(1)}, u32[]{:S(2)}, u32[]{:S(2)}) collective-permute-start(f32[16,9496]{1,0:T(8,128)S(1)} %add.168), channel_id=1, source_target_pairs={{1,0},{2,3},{5,4},{6,7},{9,8},{10,11},{13,12},{14,15},{17,16},{18,... | collective-permute-start | bytes 1823240 | tf_op jit(solution)/shard_map/ppermute | solution.py:98
  86.0 47.3 %all-to-all-start = ((bf16[8,16,9496]{2,1,0:T(8,128)(2,1)}), bf16[8,16,9496]{2,1,0:T(8,128)(2,1)}, u32[]{:S(2)}, u32[]{:S(2)}) async-start(bf16[8,16,9496]{2,1,0:T(8,128)(2,1)} %bitcast_dynamic-update-slice_fusion), calls=%async_computation | async-start | bytes 4915200 | tf_op jit(solution)/shard_map/all_to_all | solution.py:152
  93.8 17.7 %collective-permute-start.15 = (f32[16,9496]{1,0:T(8,128)}, f32[16,9496]{1,0:T(8,128)S(1)}, u32[]{:S(2)}, u32[]{:S(2)}) collective-permute-start(f32[16,9496]{1,0:T(8,128)} %add.170), channel_id=1, source_target_pairs={{1,0},{2,3},{5,4},{6,7},{9,8},{10,11},{13,12},{14,15},{17,16},{18,... | collective-permute-start | bytes 1823240 | tf_op jit(solution)/shard_map/ppermute | solution.py:98
  95.1 25.6 %collective-permute-start.14 = (f32[16,9496]{1,0:T(8,128)}, f32[16,9496]{1,0:T(8,128)S(1)}, u32[]{:S(2)}, u32[]{:S(2)}) collective-permute-start(f32[16,9496]{1,0:T(8,128)} %copy-done.23), channel_id=1, source_target_pairs={{3,2},{0,1},{7,6},{4,5},{11,10},{8,9},{15,14},{12,13},{19,18},{16,... | collective-permute-start | bytes 1823240 | tf_op jit(solution)/shard_map/ppermute | solution.py:98
  109.5 18.7 %collective-permute-start.12 = (f32[16,9496]{1,0:T(8,128)S(1)}, f32[16,9496]{1,0:T(8,128)S(1)}, u32[]{:S(2)}, u32[]{:S(2)}) collective-permute-start(f32[16,9496]{1,0:T(8,128)S(1)} %add.173), channel_id=1, source_target_pairs={{1,0},{2,3},{5,4},{6,7},{9,8},{10,11},{13,12},{14,15},{17,16},{18,... | collective-permute-start | bytes 1823240 | tf_op jit(solution)/shard_map/ppermute | solution.py:98
  111.6 22.3 %collective-permute-start.19 = (f32[16,9496]{1,0:T(8,128)}, f32[16,9496]{1,0:T(8,128)}, u32[]{:S(2)}, u32[]{:S(2)}) collective-permute-start(f32[16,9496]{1,0:T(8,128)} %get-tuple-element.121), channel_id=1, source_target_pairs={{3,2},{0,1},{7,6},{4,5},{11,10},{8,9},{15,14},{12,13},{19,18},{16,... | collective-permute-start | bytes 1823240 | tf_op jit(solution)/shard_map/ppermute | solution.py:98
  124.0 18.0 %collective-permute-start.17 = (f32[16,9496]{1,0:T(8,128)}, f32[16,9496]{1,0:T(8,128)}, u32[]{:S(2)}, u32[]{:S(2)}) collective-permute-start(f32[16,9496]{1,0:T(8,128)} %add.176), channel_id=1, source_target_pairs={{1,0},{2,3},{5,4},{6,7},{9,8},{10,11},{13,12},{14,15},{17,16},{18,... | collective-permute-start | bytes 1823240 | tf_op jit(solution)/shard_map/ppermute | solution.py:98
  128.3 19.4 %collective-permute-start.16 = (f32[16,9496]{1,0:T(8,128)}, f32[16,9496]{1,0:T(8,128)}, u32[]{:S(2)}, u32[]{:S(2)}) collective-permute-start(f32[16,9496]{1,0:T(8,128)} %get-tuple-element.125), channel_id=1, source_target_pairs={{3,2},{0,1},{7,6},{4,5},{11,10},{8,9},{15,14},{12,13},{19,18},{16,... | collective-permute-start | bytes 1823240 | tf_op jit(solution)/shard_map/ppermute | solution.py:98
  137.2 19.9 %collective-permute-start.22 = (f32[16,9496]{1,0:T(8,128)S(1)}, f32[16,9496]{1,0:T(8,128)S(1)}, u32[]{:S(2)}, u32[]{:S(2)}) collective-permute-start(f32[16,9496]{1,0:T(8,128)S(1)} %add.179), channel_id=1, source_target_pairs={{1,0},{2,3},{5,4},{6,7},{9,8},{10,11},{13,12},{14,15},{17,16},{18,... | collective-permute-start | bytes 1823240 | tf_op jit(solution)/shard_map/ppermute | solution.py:98
  149.8 19.8 %collective-permute-start.26 = (f32[16,9496]{1,0:T(8,128)S(1)}, f32[16,9496]{1,0:T(8,128)S(1)}, u32[]{:S(2)}, u32[]{:S(2)}) collective-permute-start(f32[16,9496]{1,0:T(8,128)S(1)} %add.182), channel_id=1, source_target_pairs={{1,0},{2,3},{5,4},{6,7},{9,8},{10,11},{13,12},{14,15},{17,16},{18,... | collective-permute-start | bytes 1823240 | tf_op jit(solution)/shard_map/ppermute | solution.py:98
  161.0 21.8 %collective-permute-start.24 = (f32[16,9496]{1,0:T(8,128)}, f32[16,9496]{1,0:T(8,128)}, u32[]{:S(2)}, u32[]{:S(2)}) collective-permute-start(f32[16,9496]{1,0:T(8,128)} %add.185), channel_id=1, source_target_pairs={{1,0},{2,3},{5,4},{6,7},{9,8},{10,11},{13,12},{14,15},{17,16},{18,... | collective-permute-start | bytes 1823240 | tf_op jit(solution)/shard_map/ppermute | solution.py:98
  171.5 24.1 %collective-permute-start.27 = (f32[16,9496]{1,0:T(8,128)}, f32[16,9496]{1,0:T(8,128)}, u32[]{:S(2)}, u32[]{:S(2)}) collective-permute-start(f32[16,9496]{1,0:T(8,128)} %add.187), channel_id=1, source_target_pairs={{1,0},{2,3},{5,4},{6,7},{9,8},{10,11},{13,12},{14,15},{17,16},{18,... | collective-permute-start | bytes 1823240 | tf_op jit(solution)/shard_map/ppermute | solution.py:98
  216.2 24.5 %collective-permute-start.32 = (bf16[32,9496]{1,0:T(8,128)(2,1)S(1)}, bf16[32,9496]{1,0:T(8,128)(2,1)S(1)}, u32[]{:S(2)}, u32[]{:S(2)}) collective-permute-start(bf16[32,9496]{1,0:T(8,128)(2,1)S(1)} %pad_maximum_fusion.5), channel_id=1, source_target_pairs={{3,2},{0,1},{7,6},{4,5},{11,10},{8,9},{15,14},{12,13},{19,18},{16,... | collective-permute-start | bytes 1823240 | tf_op jit(solution)/shard_map/ppermute | solution.py:98
  229.9 28.7 %collective-permute-start.39 = (bf16[32,9496]{1,0:T(8,128)(2,1)S(1)}, bf16[32,9496]{1,0:T(8,128)(2,1)S(1)}, u32[]{:S(2)}, u32[]{:S(2)}) collective-permute-start(bf16[32,9496]{1,0:T(8,128)(2,1)S(1)} %pad_maximum_fusion.6), channel_id=1, source_target_pairs={{3,2},{0,1},{7,6},{4,5},{11,10},{8,9},{15,14},{12,13},{19,18},{16,... | collective-permute-start | bytes 1823240 | tf_op jit(solution)/shard_map/ppermute | solution.py:98
  242.2 26.6 %collective-permute-start.38 = (bf16[16,9496]{1,0:T(8,128)(2,1)S(1)}, bf16[16,9496]{1,0:T(8,128)(2,1)S(1)}, u32[]{:S(2)}, u32[]{:S(2)}) collective-permute-start(bf16[16,9496]{1,0:T(8,128)(2,1)S(1)} %fusion.39), channel_id=1, source_target_pairs={{3,2},{0,1},{7,6},{4,5},{11,10},{8,9},{15,14},{12,13},{19,18},{16,... | collective-permute-start | bytes 911624 | tf_op jit(solution)/shard_map/ppermute | solution.py:98
  250.0 17.2 %collective-permute-start.34 = (bf16[32,9496]{1,0:T(8,128)(2,1)S(1)}, bf16[32,9496]{1,0:T(8,128)(2,1)S(1)}, u32[]{:S(2)}, u32[]{:S(2)}) collective-permute-start(bf16[32,9496]{1,0:T(8,128)(2,1)S(1)} %collective-permute-done.33), channel_id=1, source_target_pairs={{1,0},{2,3},{5,4},{6,7},{9,8},{10,11},{13,12},{14,15},{17,16},{18,... | collective-permute-start | bytes 1823240 | tf_op jit(solution)/shard_map/ppermute | solution.py:98
  257.2 21.6 %collective-permute-start.36 = (bf16[32,9496]{1,0:T(8,128)(2,1)S(1)}, bf16[32,9496]{1,0:T(8,128)(2,1)S(1)}, u32[]{:S(2)}, u32[]{:S(2)}) collective-permute-start(bf16[32,9496]{1,0:T(8,128)(2,1)S(1)} %collective-permute-done.35), channel_id=1, source_target_pairs={{1,0},{2,3},{5,4},{6,7},{9,8},{10,11},{13,12},{14,15},{17,16},{18,... | collective-permute-start | bytes 1823240 | tf_op jit(solution)/shard_map/ppermute | solution.py:98
  267.3 28.4 %collective-permute-start.43 = (bf16[32,9496]{1,0:T(8,128)(2,1)S(1)}, bf16[32,9496]{1,0:T(8,128)(2,1)S(1)}, u32[]{:S(2)}, u32[]{:S(2)}) collective-permute-start(bf16[32,9496]{1,0:T(8,128)(2,1)S(1)} %collective-permute-done.40), channel_id=1, source_target_pairs={{1,0},{2,3},{5,4},{6,7},{9,8},{10,11},{13,12},{14,15},{17,16},{18,... | collective-permute-start | bytes 1823240 | tf_op jit(solution)/shard_map/ppermute | solution.py:98
  279.1 22.2 %collective-permute-start.44 = (bf16[16,9496]{1,0:T(8,128)(2,1)S(1)}, bf16[16,9496]{1,0:T(8,128)(2,1)S(1)}, u32[]{:S(2)}, u32[]{:S(2)}) collective-permute-start(bf16[16,9496]{1,0:T(8,128)(2,1)S(1)} %collective-permute-done.42), channel_id=1, source_target_pairs={{1,0},{2,3},{5,4},{6,7},{9,8},{10,11},{13,12},{14,15},{17,16},{18,... | collective-permute-start | bytes 911624 | tf_op jit(solution)/shard_map/ppermute | solution.py:98
  280.6 23.9 %collective-permute-start.45 = (bf16[16,9496]{1,0:T(8,128)(2,1)S(1)}, bf16[16,9496]{1,0:T(8,128)(2,1)S(1)}, u32[]{:S(2)}, u32[]{:S(2)}) collective-permute-start(bf16[16,9496]{1,0:T(8,128)(2,1)S(1)} %collective-permute-done.41), channel_id=1, source_target_pairs={{1,0},{2,3},{5,4},{6,7},{9,8},{10,11},{13,12},{14,15},{17,16},{18,... | collective-permute-start | bytes 911624 | tf_op jit(solution)/shard_map/ppermute | solution.py:98
  308.6 18.6 %all-to-all-start.2 = ((f32[8,64,320]{2,1,0:T(8,128)}), f32[8,64,320]{2,1,0:T(8,128)S(1)}, u32[]{:S(2)}, u32[]{:S(2)}) async-start(f32[8,64,320]{2,1,0:T(8,128)} %bitcast.46), calls=%async_computation.2 | async-start | bytes 1572864 | tf_op jit(solution)/shard_map/all_to_all | solution.py:319
  (61 other events, 1093.1 us)

commit v7 on v6

--- a/solution.py
+++ b/solution.py
@@ -79,6 +79,34 @@
     return stats.T
 
 
+def head_kernel(grad_ref, hidden_ref, *refs):
+    out_ref = refs[-1]
+    out_ref[...] = lax.dot_general(
+        grad_ref[...], hidden_ref[...], (((0,), (0,)), ((), ())),
+        preferred_element_type=jnp.float32)
+
+
+def head_product(grads, hidden, first, stop, tile, out=None):
+    tokens, cols = grads.shape
+    rows = hidden.shape[1]
+    return pl.pallas_call(
+        head_kernel,
+        grid=(stop - first,),
+        in_specs=[
+            pl.BlockSpec((tokens, tile), lambda i: (0, first + i)),
+            pl.BlockSpec((tokens, rows), lambda i: (0, 0)),
+        ] + ([] if out is None else [pl.BlockSpec(memory_space=pl.ANY)]),
+        out_specs=pl.BlockSpec((tile, rows), lambda i: (first + i, 0)),
+        out_shape=jax.ShapeDtypeStruct((cols, rows), jnp.float32),
+        input_output_aliases={} if out is None else {2: 0},
+        compiler_params=pltpu.CompilerParams(vmem_limit_bytes=24 * 1024 * 1024),
+        cost_estimate=pl.CostEstimate(
+            flops=2 * tokens * rows * tile * (stop - first),
+            bytes_accessed=(4 * rows + 2 * tokens) * tile * (stop - first),
+            transcendentals=0),
+    )(grads, hidden, *([] if out is None else [out]))
+
+
 def body(hidden_states, head_weight, teacher_logits):
     seq_count = lax.axis_size("seq")
     vocab_count = lax.axis_size("vocab")
@@ -264,14 +292,14 @@
     early_keys, late_keys = list(range(count // 2)), list(range(count // 2, count))
     for p in range(count):
         step = min(p, count - 2)
-        plan(end + max(step, 1), 40 + 2 * p, form_grads, p)
-        plan(end + max(step, 1), 41 + 2 * p, send_grad, p, 0)
+        plan(end + 1, 40 + 4 * p, form_grads, p)
+        plan(end + 1, 41 + 4 * p, send_grad, p, 0)
         for j in range(1, hops):
-            plan(end + 1 + step + j, 30 - j, send_grad, p, j)
+            plan(end + 1 + step + j, 30 + j, send_grad, p, j)
     plan(end + 1, 35, loss)
     for j in range(hops):
-        plan(end + 1, 36 if j == 0 else 41 + 2 * min(j - 1, 1), send_loss, j)
-    plan(end + 1, 50, settle_loss)
+        plan(end + 1, 36 if j == 0 else 42 + 4 * min(j - 1, 1), send_loss, j)
+    plan(end + 3, 90, settle_loss)
     final = max(slots)
     plan(final, 700, early_feature)
 
@@ -303,9 +331,9 @@
     matching = jnp.concatenate([
         both[:, :early_rows].reshape(-1, rows), both[:, early_rows:].reshape(-1, rows)])
     all_grads = jnp.concatenate([early_grads, late_grads])
-    head_part = lax.dot_general(
-        all_grads, matching, (((0,), (0,)), ((), ())), preferred_element_type=jnp.float32
-    ).T
+    tile = min(VOCAB_TILE, cols)
+    blocks_out = pl.cdiv(cols, tile)
+    beside = (blocks_out * 3 + 4) // 5
     feature = feature.reshape(2, vocab_count, half, per_dev, rows).transpose(0, 2, 1, 3, 4)
     feature = feature.reshape(2, half, own_tokens, rows)
     low = jnp.where(low_side, feature[0], feature[1])
@@ -317,17 +345,22 @@
         feature = feature.reshape(seq_count, own_tokens, share, out_cols).transpose(0, 2, 1, 3)
         feature = feature.reshape(vocab_count, own_tokens, out_cols)
         feature = lax.all_to_all(feature, "vocab", split_axis=0, concat_axis=0, tiled=True)
+        head_part = head_product(all_grads, matching, 0, beside, tile)
         feature, head_part = lax.optimization_barrier((feature, head_part))
         feature = jnp.sum(feature, axis=0)
+        feature, head_part = lax.optimization_barrier((feature, head_part))
         pairs = [
             ((dst * share + b) * seq_count + src, (src * share + b) * seq_count + dst)
             for src in range(seq_count) for dst in range(seq_count) for b in range(share)
         ]
         hidden_grad = lax.ppermute(feature, ("vocab", "seq"), pairs)
+        if beside < blocks_out:
+            head_part = head_product(all_grads, matching, beside, blocks_out, tile, head_part)
     else:
         feature = lax.all_to_all(feature, "seq", split_axis=0, concat_axis=2, tiled=True)
         hidden_grad = lax.psum_scatter(feature[0], "vocab", scatter_dimension=1, tiled=True)
-    return (mean_divergence, hidden_grad, head_part)
+        head_part = head_product(all_grads, matching, 0, blocks_out, tile)
+    return (mean_divergence, hidden_grad, head_part.T)
 
 
 def solution(mesh):

time: 343 us -> 346 us (level)
  waiting for transfers between devices: 134 us -> 153 us
  matrix products: 27.6 us -> 12.6 us
  starting transfers between devices: 108 us -> 95.2 us
  Pallas kernels: 18.1 us -> 30 us
  local copies, waits for them, and re-layouts: 17.7 us -> 22.1 us
  other arithmetic: 29.8 us -> 26 us
    ppermute x42, waiting for transfers between devices: 115 us -> 139 us  [hop(): return lax.ppermute(value, 'seq', [(last - j, last - j - 1), (j, j + 1)])]
    dot_general x1 -> x0, matrix products: 15 us -> none  [body(): lax.dot_general(all_grads, matching, (((0,), (0,)), ((), ())), preferred_...]
    ppermute x42, starting transfers between devices: 87.6 us -> 73.2 us  [hop(): return lax.ppermute(value, 'seq', [(last - j, last - j - 1), (j, j + 1)])]
    pallas_call x0 -> x2, Pallas kernels: none -> 11.9 us  [head_product(): pl.pallas_call(head_kernel, grid=(stop - first,), in_specs=[pl.BlockSpec(...]
    ppermute x1, waiting for transfers between devices: 9.93 us -> 2.1 us  [body(): hidden_grad = lax.ppermute(feature, ('vocab', 'seq'), pairs)]
    unnamed x79 -> x77, local copies, waits for them, and re-layouts: 9.94 us -> 15.3 us
  transfers between devices with their start and end apart: 50 -> 50, of which waited for: 26 -> 29; matrix products, arithmetic and copies ran while one was open for 16% -> 11% of each run, Pallas kernels for 5% -> 8%
where the time goes in v7:
time: 346 us; the launch traced here: 344 us
  waiting for transfers between devices  153 us (44%)
  starting transfers between devices  95.2 us (28%)
  Pallas kernels  30 us (9%)
  other arithmetic  26 us (8%)
  local copies, waits for them, and re-layouts  22.1 us (6%)
  matrix products  12.6 us (4%)
  between operations  5.44 us (2%)
    ppermute x42, waiting for transfers between devices, hop(): return lax.ppermute(value, 'seq', [(last - j, last - j - 1), (j, j + 1)])  139 us
    ppermute x42, starting transfers between devices, hop(): return lax.ppermute(value, 'seq', [(last - j, last - j - 1), (j, j + 1)])  73.2 us
    unnamed x77, local copies, waits for them, and re-layouts  15.3 us
    pallas_call x1, Pallas kernels, partial_students(): pl.pallas_call(partial_kernel, grid=(pl.cdiv(cols, tile),), in_specs=[pl....  15.1 us
    pallas_call x2, Pallas kernels, head_product(): pl.pallas_call(head_kernel, grid=(stop - first,), in_specs=[pl.BlockSpec(...  11.9 us
    add x16, other arithmetic, send(): value = part + tied(moving[i])  10.1 us
    dot_general x1, matrix products, body(): jnp.dot(ordered[half_tokens:half_tokens + chunk], head_weight, preferred_...  8.45 us
    convert_element_type x5, other arithmetic, form_grads(): grads.append((LOSS_SCALE * (jnp.exp(student - student_max[at, None]) / st...  7.33 us
  transfers between devices with their start and end apart: 50, of which 29 were waited for; matrix products, arithmetic and copies ran while one was open for 11% of the time, Pallas kernels for 8%

profile of v7, /device:TPU:2, one launch (start us, length us, event | category | flops | bytes accessed | tf_op | source)
XLA Modules:
  0.0 343.9 jit_solution(7725454474792647752)
XLA Ops:
  14.9 8.4 %fusion.54 = f32[16,9496]{1,0:T(8,128)S(1)} fusion(bf16[640,9496]{0,1:T(8,128)(2,1)} %param.4, bf16[256,640]{1,0:T(8,128)(2,1)S(1)} %bitcast.105), kind=kOutput, calls=%fused_computation.105 | convolution fusion | flops 194478080 | bytes 12783104 | tf_op jit(solution)/shard_map/dot_general | solution.py:306
  23.4 4.9 %collective-permute-start.3 = (f32[16,9496]{1,0:T(8,128)S(1)}, f32[16,9496]{1,0:T(8,128)S(1)}, u32[]{:S(2)}, u32[]{:S(2)}) collective-permute-start(f32[16,9496]{1,0:T(8,128)S(1)} %fusion.54), channel_id=1, source_target_pairs={{3,2},{0,1},{7,6},{4,5},{11,10},{8,9},{15,14},{12,13},{19,18},{16,... | collective-permute-start | bytes 1823240 | tf_op jit(solution)/shard_map/ppermute | solution.py:126
  28.4 15.1 %shard_map.58 = (f32[16,9496]{1,0:T(8,128)S(1)}, f32[16,9496]{1,0:T(8,128)S(1)}, f32[16,9496]{1,0:T(8,128)S(1)}, f32[16,9496]{1,0:T(8,128)S(1)}, f32[16,9496]{1,...) custom-call(bf16[240,640]{1,0:T(8,128)(2,1)S(1)} %pad_maximum_fusion, ...), custom_call_target="tpu_custom_call" | custom-call | flops 2917171200 | bytes 21271040 | tf_op jit(solution)/shard_map/pallas_call | solution.py:32
  50.0 10.0 %collective-permute-done.5 = f32[16,9496]{1,0:T(8,128)S(1)} collective-permute-done((f32[16,9496]{1,0:T(8,128)S(1)}, f32[16,9496]{1,0:T(8,128)S(1)}, u32[]{:S(2)}, u32[]{:S(2)}) %collective-permute-start.5) | collective-permute-done | bytes 607776 | tf_op jit(solution)/shard_map/ppermute | solution.py:126
  64.0 7.5 %collective-permute-done.9 = f32[16,9496]{1,0:T(8,128)S(1)} collective-permute-done((f32[16,9496]{1,0:T(8,128)S(1)}, f32[16,9496]{1,0:T(8,128)S(1)}, u32[]{:S(2)}, u32[]{:S(2)}) %collective-permute-start.9) | collective-permute-done | bytes 607776 | tf_op jit(solution)/shard_map/ppermute | solution.py:126
  73.2 5.0 %collective-permute-done.7 = f32[16,9496]{1,0:T(8,128)S(1)} collective-permute-done((f32[16,9496]{1,0:T(8,128)S(1)}, f32[16,9496]{1,0:T(8,128)S(1)}, u32[]{:S(2)}, u32[]{:S(2)}) %collective-permute-start.7) | collective-permute-done | bytes 607776 | tf_op jit(solution)/shard_map/ppermute | solution.py:126
  85.1 4.8 %all-to-all-start = ((bf16[8,16,9496]{2,1,0:T(8,128)(2,1)}), bf16[8,16,9496]{2,1,0:T(8,128)(2,1)}, u32[]{:S(2)}, u32[]{:S(2)}) async-start(bf16[8,16,9496]{2,1,0:T(8,128)(2,1)} %bitcast_dynamic-update-slice_fusion), calls=%async_computation | async-start | bytes 4915200 | tf_op jit(solution)/shard_map/all_to_all | solution.py:180
  94.1 4.6 %collective-permute-start.14 = (f32[16,9496]{1,0:T(8,128)}, f32[16,9496]{1,0:T(8,128)S(1)}, u32[]{:S(2)}, u32[]{:S(2)}) collective-permute-start(f32[16,9496]{1,0:T(8,128)} %copy-done.25), channel_id=1, source_target_pairs={{3,2},{0,1},{7,6},{4,5},{11,10},{8,9},{15,14},{12,13},{19,18},{16,... | collective-permute-start | bytes 1823240 | tf_op jit(solution)/shard_map/ppermute | solution.py:126
  98.7 7.8 %collective-permute-done.11 = f32[16,9496]{1,0:T(8,128)S(1)} collective-permute-done((f32[16,9496]{1,0:T(8,128)}, f32[16,9496]{1,0:T(8,128)S(1)}, u32[]{:S(2)}, u32[]{:S(2)}) %collective-permute-start.11) | collective-permute-done | bytes 607776 | tf_op jit(solution)/shard_map/ppermute | solution.py:126
  110.6 7.2 %collective-permute-start.19 = (f32[16,9496]{1,0:T(8,128)}, f32[16,9496]{1,0:T(8,128)}, u32[]{:S(2)}, u32[]{:S(2)}) collective-permute-start(f32[16,9496]{1,0:T(8,128)} %get-tuple-element.123), channel_id=1, source_target_pairs={{3,2},{0,1},{7,6},{4,5},{11,10},{8,9},{15,14},{12,13},{19,18},{16,... | collective-permute-start | bytes 1823240 | tf_op jit(solution)/shard_map/ppermute | solution.py:126
  127.3 5.1 %collective-permute-start.16 = (f32[16,9496]{1,0:T(8,128)}, f32[16,9496]{1,0:T(8,128)}, u32[]{:S(2)}, u32[]{:S(2)}) collective-permute-start(f32[16,9496]{1,0:T(8,128)} %get-tuple-element.127), channel_id=1, source_target_pairs={{3,2},{0,1},{7,6},{4,5},{11,10},{8,9},{15,14},{12,13},{19,18},{16,... | collective-permute-start | bytes 1823240 | tf_op jit(solution)/shard_map/ppermute | solution.py:126
  149.6 6.3 %collective-permute-done.22 = f32[16,9496]{1,0:T(8,128)S(1)} collective-permute-done((f32[16,9496]{1,0:T(8,128)S(1)}, f32[16,9496]{1,0:T(8,128)S(1)}, u32[]{:S(2)}, u32[]{:S(2)}) %collective-permute-start.22) | collective-permute-done | bytes 607776 | tf_op jit(solution)/shard_map/ppermute | solution.py:126
  160.5 8.9 %collective-permute-done.26 = f32[16,9496]{1,0:T(8,128)S(1)} collective-permute-done((f32[16,9496]{1,0:T(8,128)S(1)}, f32[16,9496]{1,0:T(8,128)S(1)}, u32[]{:S(2)}, u32[]{:S(2)}) %collective-permute-start.26) | collective-permute-done | bytes 607776 | tf_op jit(solution)/shard_map/ppermute | solution.py:126
  175.5 6.5 %collective-permute-done.24 = f32[16,9496]{1,0:T(8,128)S(1)} collective-permute-done((f32[16,9496]{1,0:T(8,128)S(1)}, f32[16,9496]{1,0:T(8,128)S(1)}, u32[]{:S(2)}, u32[]{:S(2)}) %collective-permute-start.24) | collective-permute-done | bytes 607776 | tf_op jit(solution)/shard_map/ppermute | solution.py:126
  184.5 10.0 %collective-permute-done.27 = f32[16,9496]{1,0:T(8,128)} collective-permute-done((f32[16,9496]{1,0:T(8,128)}, f32[16,9496]{1,0:T(8,128)}, u32[]{:S(2)}, u32[]{:S(2)}) %collective-permute-start.27) | collective-permute-done | bytes 607776 | tf_op jit(solution)/shard_map/ppermute | solution.py:126
  228.7 10.9 %collective-permute-done.33 = bf16[32,9496]{1,0:T(8,128)(2,1)S(1)} collective-permute-done((bf16[32,9496]{1,0:T(8,128)(2,1)S(1)}, bf16[32,9496]{1,0:T(8,128)(2,1)S(1)}, u32[]{:S(2)}, u32[]{:S(2)}) %collective-permute-start.33) | collective-permute-done | bytes 607776 | tf_op jit(solution)/shard_map/ppermute | solution.py:126
  242.1 6.4 %collective-permute-done.30 = f32[1,1]{1,0:T(1,128)} collective-permute-done((f32[1,1]{1,0:T(1,128)}, f32[1,1]{1,0:T(1,128)}, u32[]{:S(2)}, u32[]{:S(2)}) %collective-permute-start.30) | collective-permute-done | bytes 36 | tf_op jit(solution)/shard_map/ppermute | solution.py:126
  251.0 8.4 %collective-permute-done.36 = bf16[32,9496]{1,0:T(8,128)(2,1)S(1)} collective-permute-done((bf16[32,9496]{1,0:T(8,128)(2,1)S(1)}, bf16[32,9496]{1,0:T(8,128)(2,1)S(1)}, u32[]{:S(2)}, u32[]{:S(2)}) %collective-permute-start.36) | collective-permute-done | bytes 607776 | tf_op jit(solution)/shard_map/ppermute | solution.py:126
  271.6 15.1 %collective-permute-done.37 = bf16[32,9496]{1,0:T(8,128)(2,1)S(1)} collective-permute-done((bf16[32,9496]{1,0:T(8,128)(2,1)S(1)}, bf16[32,9496]{1,0:T(8,128)(2,1)S(1)}, u32[]{:S(2)}, u32[]{:S(2)}) %collective-permute-start.37) | collective-permute-done | bytes 607776 | tf_op jit(solution)/shard_map/ppermute | solution.py:126
  291.2 8.6 %collective-permute-done.43 = bf16[32,9496]{1,0:T(8,128)(2,1)S(1)} collective-permute-done((bf16[32,9496]{1,0:T(8,128)(2,1)S(1)}, bf16[32,9496]{1,0:T(8,128)(2,1)S(1)}, u32[]{:S(2)}, u32[]{:S(2)}) %collective-permute-start.43) | collective-permute-done | bytes 607776 | tf_op jit(solution)/shard_map/ppermute | solution.py:126
  299.8 6.6 %collective-permute-done.44 = bf16[16,9496]{1,0:T(8,128)(2,1)S(1)} collective-permute-done((bf16[16,9496]{1,0:T(8,128)(2,1)S(1)}, bf16[16,9496]{1,0:T(8,128)(2,1)S(1)}, u32[]{:S(2)}, u32[]{:S(2)}) %collective-permute-start.44) | collective-permute-done | bytes 303904 | tf_op jit(solution)/shard_map/ppermute | solution.py:126
  306.4 4.8 %collective-permute-done.45 = bf16[16,9496]{1,0:T(8,128)(2,1)S(1)} collective-permute-done((bf16[16,9496]{1,0:T(8,128)(2,1)S(1)}, bf16[16,9496]{1,0:T(8,128)(2,1)S(1)}, u32[]{:S(2)}, u32[]{:S(2)}) %collective-permute-start.45) | collective-permute-done | bytes 303904 | tf_op jit(solution)/shard_map/ppermute | solution.py:126
  321.9 7.4 %shard_map.61.refs_0_ = f32[9496,640]{1,0:T(8,128)} custom-call(bf16[256,9496]{1,0:T(8,128)(2,1)S(1)} %copy-done.1, bf16[256,640]{1,0:T(8,128)(2,1)S(1)} %pad_maximum_fusion.9.hidden_ref), custom_call_target="tpu_custom_call" | custom-call | flops 2013265920 | bytes 18874368 | tf_op jit(solution)/shard_map/pallas_call | solution.py:92
  335.5 4.6 %shard_map.62 = f32[9496,640]{1,0:T(8,128)} custom-call(bf16[256,9496]{1,0:T(8,128)(2,1)S(1)} %copy-done.2, bf16[256,640]{1,0:T(8,128)(2,1)S(1)} %pad_maximum_fusion.9.hidden_ref, f32[9496,640]{1,0:T(8,128)} %shard_map.61.refs_0_), custom_call_target="tpu_custom_call", output_to_operand_aliasing={{}: (2, {})} | custom-call | flops 1342177280 | bytes 12582912 | tf_op jit(solution)/shard_map/pallas_call | solution.py:92
  (242 shorter events, 153.7 us)
Async XLA Ops:
  13.3 36.6 %collective-permute-start.6 = (bf16[8,75968]{1,0:T(8,128)(2,1)}, bf16[8,75968]{1,0:T(8,128)(2,1)}, u32[]{:S(2)}, u32[]{:S(2)}) collective-permute-start(bf16[8,75968]{1,0:T(8,128)(2,1)} %bitcast.1), channel_id=1, source_target_pairs={{1,0},{2,3},{5,4},{6,7},{9,8},{10,11},{13,12},{14,15},{17,16},{18,... | collective-permute-start | bytes 3646472 | tf_op jit(solution)/shard_map/ppermute | solution.py:148
  23.4 22.3 %collective-permute-start.3 = (f32[16,9496]{1,0:T(8,128)S(1)}, f32[16,9496]{1,0:T(8,128)S(1)}, u32[]{:S(2)}, u32[]{:S(2)}) collective-permute-start(f32[16,9496]{1,0:T(8,128)S(1)} %fusion.54), channel_id=1, source_target_pairs={{3,2},{0,1},{7,6},{4,5},{11,10},{8,9},{15,14},{12,13},{19,18},{16,... | collective-permute-start | bytes 1823240 | tf_op jit(solution)/shard_map/ppermute | solution.py:126
  46.5 24.9 %collective-permute-start.9 = (f32[16,9496]{1,0:T(8,128)S(1)}, f32[16,9496]{1,0:T(8,128)S(1)}, u32[]{:S(2)}, u32[]{:S(2)}) collective-permute-start(f32[16,9496]{1,0:T(8,128)S(1)} %get-tuple-element.101), channel_id=1, source_target_pairs={{3,2},{0,1},{7,6},{4,5},{11,10},{8,9},{15,14},{12,13},{19,18},{16,... | collective-permute-start | bytes 1823240 | tf_op jit(solution)/shard_map/ppermute | solution.py:126
  85.1 47.3 %all-to-all-start = ((bf16[8,16,9496]{2,1,0:T(8,128)(2,1)}), bf16[8,16,9496]{2,1,0:T(8,128)(2,1)}, u32[]{:S(2)}, u32[]{:S(2)}) async-start(bf16[8,16,9496]{2,1,0:T(8,128)(2,1)} %bitcast_dynamic-update-slice_fusion), calls=%async_computation | async-start | bytes 4915200 | tf_op jit(solution)/shard_map/all_to_all | solution.py:180
  92.8 17.7 %collective-permute-start.15 = (f32[16,9496]{1,0:T(8,128)}, f32[16,9496]{1,0:T(8,128)S(1)}, u32[]{:S(2)}, u32[]{:S(2)}) collective-permute-start(f32[16,9496]{1,0:T(8,128)} %add.170), channel_id=1, source_target_pairs={{1,0},{2,3},{5,4},{6,7},{9,8},{10,11},{13,12},{14,15},{17,16},{18,... | collective-permute-start | bytes 1823240 | tf_op jit(solution)/shard_map/ppermute | solution.py:126
  94.1 25.6 %collective-permute-start.14 = (f32[16,9496]{1,0:T(8,128)}, f32[16,9496]{1,0:T(8,128)S(1)}, u32[]{:S(2)}, u32[]{:S(2)}) collective-permute-start(f32[16,9496]{1,0:T(8,128)} %copy-done.25), channel_id=1, source_target_pairs={{3,2},{0,1},{7,6},{4,5},{11,10},{8,9},{15,14},{12,13},{19,18},{16,... | collective-permute-start | bytes 1823240 | tf_op jit(solution)/shard_map/ppermute | solution.py:126
  108.5 18.7 %collective-permute-start.12 = (f32[16,9496]{1,0:T(8,128)S(1)}, f32[16,9496]{1,0:T(8,128)S(1)}, u32[]{:S(2)}, u32[]{:S(2)}) collective-permute-start(f32[16,9496]{1,0:T(8,128)S(1)} %add.173), channel_id=1, source_target_pairs={{1,0},{2,3},{5,4},{6,7},{9,8},{10,11},{13,12},{14,15},{17,16},{18,... | collective-permute-start | bytes 1823240 | tf_op jit(solution)/shard_map/ppermute | solution.py:126
  110.6 22.3 %collective-permute-start.19 = (f32[16,9496]{1,0:T(8,128)}, f32[16,9496]{1,0:T(8,128)}, u32[]{:S(2)}, u32[]{:S(2)}) collective-permute-start(f32[16,9496]{1,0:T(8,128)} %get-tuple-element.123), channel_id=1, source_target_pairs={{3,2},{0,1},{7,6},{4,5},{11,10},{8,9},{15,14},{12,13},{19,18},{16,... | collective-permute-start | bytes 1823240 | tf_op jit(solution)/shard_map/ppermute | solution.py:126
  123.1 18.0 %collective-permute-start.17 = (f32[16,9496]{1,0:T(8,128)}, f32[16,9496]{1,0:T(8,128)}, u32[]{:S(2)}, u32[]{:S(2)}) collective-permute-start(f32[16,9496]{1,0:T(8,128)} %add.176), channel_id=1, source_target_pairs={{1,0},{2,3},{5,4},{6,7},{9,8},{10,11},{13,12},{14,15},{17,16},{18,... | collective-permute-start | bytes 1823240 | tf_op jit(solution)/shard_map/ppermute | solution.py:126
  127.3 18.7 %collective-permute-start.16 = (f32[16,9496]{1,0:T(8,128)}, f32[16,9496]{1,0:T(8,128)}, u32[]{:S(2)}, u32[]{:S(2)}) collective-permute-start(f32[16,9496]{1,0:T(8,128)} %get-tuple-element.127), channel_id=1, source_target_pairs={{3,2},{0,1},{7,6},{4,5},{11,10},{8,9},{15,14},{12,13},{19,18},{16,... | collective-permute-start | bytes 1823240 | tf_op jit(solution)/shard_map/ppermute | solution.py:126
  136.2 19.8 %collective-permute-start.22 = (f32[16,9496]{1,0:T(8,128)S(1)}, f32[16,9496]{1,0:T(8,128)S(1)}, u32[]{:S(2)}, u32[]{:S(2)}) collective-permute-start(f32[16,9496]{1,0:T(8,128)S(1)} %add.179), channel_id=1, source_target_pairs={{1,0},{2,3},{5,4},{6,7},{9,8},{10,11},{13,12},{14,15},{17,16},{18,... | collective-permute-start | bytes 1823240 | tf_op jit(solution)/shard_map/ppermute | solution.py:126
  148.2 21.2 %collective-permute-start.26 = (f32[16,9496]{1,0:T(8,128)S(1)}, f32[16,9496]{1,0:T(8,128)S(1)}, u32[]{:S(2)}, u32[]{:S(2)}) collective-permute-start(f32[16,9496]{1,0:T(8,128)S(1)} %add.182), channel_id=1, source_target_pairs={{1,0},{2,3},{5,4},{6,7},{9,8},{10,11},{13,12},{14,15},{17,16},{18,... | collective-permute-start | bytes 1823240 | tf_op jit(solution)/shard_map/ppermute | solution.py:126
  159.2 22.9 %collective-permute-start.24 = (f32[16,9496]{1,0:T(8,128)S(1)}, f32[16,9496]{1,0:T(8,128)S(1)}, u32[]{:S(2)}, u32[]{:S(2)}) collective-permute-start(f32[16,9496]{1,0:T(8,128)S(1)} %add.185), channel_id=1, source_target_pairs={{1,0},{2,3},{5,4},{6,7},{9,8},{10,11},{13,12},{14,15},{17,16},{18,... | collective-permute-start | bytes 1823240 | tf_op jit(solution)/shard_map/ppermute | solution.py:126
  170.5 24.0 %collective-permute-start.27 = (f32[16,9496]{1,0:T(8,128)}, f32[16,9496]{1,0:T(8,128)}, u32[]{:S(2)}, u32[]{:S(2)}) collective-permute-start(f32[16,9496]{1,0:T(8,128)} %add.187), channel_id=1, source_target_pairs={{1,0},{2,3},{5,4},{6,7},{9,8},{10,11},{13,12},{14,15},{17,16},{18,... | collective-permute-start | bytes 1823240 | tf_op jit(solution)/shard_map/ppermute | solution.py:126
  215.2 24.5 %collective-permute-start.33 = (bf16[32,9496]{1,0:T(8,128)(2,1)S(1)}, bf16[32,9496]{1,0:T(8,128)(2,1)S(1)}, u32[]{:S(2)}, u32[]{:S(2)}) collective-permute-start(bf16[32,9496]{1,0:T(8,128)(2,1)S(1)} %pad_maximum_fusion.5), channel_id=1, source_target_pairs={{3,2},{0,1},{7,6},{4,5},{11,10},{8,9},{15,14},{12,13},{19,18},{16,... | collective-permute-start | bytes 1823240 | tf_op jit(solution)/shard_map/ppermute | solution.py:126
  222.8 37.3 %collective-permute-start.39 = (bf16[16,9496]{1,0:T(8,128)(2,1)S(1)}, bf16[16,9496]{1,0:T(8,128)(2,1)S(1)}, u32[]{:S(2)}, u32[]{:S(2)}) collective-permute-start(bf16[16,9496]{1,0:T(8,128)(2,1)S(1)} %fusion.39), channel_id=1, source_target_pairs={{3,2},{0,1},{7,6},{4,5},{11,10},{8,9},{15,14},{12,13},{19,18},{16,... | collective-permute-start | bytes 911624 | tf_op jit(solution)/shard_map/ppermute | solution.py:126
  224.1 35.3 %collective-permute-start.36 = (bf16[32,9496]{1,0:T(8,128)(2,1)S(1)}, bf16[32,9496]{1,0:T(8,128)(2,1)S(1)}, u32[]{:S(2)}, u32[]{:S(2)}) collective-permute-start(bf16[32,9496]{1,0:T(8,128)(2,1)S(1)} %pad_maximum_fusion.6), channel_id=1, source_target_pairs={{3,2},{0,1},{7,6},{4,5},{11,10},{8,9},{15,14},{12,13},{19,18},{16,... | collective-permute-start | bytes 1823240 | tf_op jit(solution)/shard_map/ppermute | solution.py:126
  226.7 38.5 %collective-permute-start.38 = (bf16[16,9496]{1,0:T(8,128)(2,1)S(1)}, bf16[16,9496]{1,0:T(8,128)(2,1)S(1)}, u32[]{:S(2)}, u32[]{:S(2)}) collective-permute-start(bf16[16,9496]{1,0:T(8,128)(2,1)S(1)} %fusion.40), channel_id=1, source_target_pairs={{3,2},{0,1},{7,6},{4,5},{11,10},{8,9},{15,14},{12,13},{19,18},{16,... | collective-permute-start | bytes 911624 | tf_op jit(solution)/shard_map/ppermute | solution.py:126
  239.6 20.4 %collective-permute-start.35 = (bf16[32,9496]{1,0:T(8,128)(2,1)S(1)}, bf16[32,9496]{1,0:T(8,128)(2,1)S(1)}, u32[]{:S(2)}, u32[]{:S(2)}) collective-permute-start(bf16[32,9496]{1,0:T(8,128)(2,1)S(1)} %collective-permute-done.33), channel_id=1, source_target_pairs={{2,1},{1,2},{6,5},{5,6},{10,9},{9,10},{14,13},{13,14},{18,17},{17,... | collective-permute-start | bytes 1823240 | tf_op jit(solution)/shard_map/ppermute | solution.py:126
  248.5 23.0 %collective-permute-start.34 = (bf16[32,9496]{1,0:T(8,128)(2,1)S(1)}, bf16[32,9496]{1,0:T(8,128)(2,1)S(1)}, u32[]{:S(2)}, u32[]{:S(2)}) collective-permute-start(bf16[32,9496]{1,0:T(8,128)(2,1)S(1)} %collective-permute-done.32), channel_id=1, source_target_pairs={{1,0},{2,3},{5,4},{6,7},{9,8},{10,11},{13,12},{14,15},{17,16},{18,... | collective-permute-start | bytes 1823240 | tf_op jit(solution)/shard_map/ppermute | solution.py:126
  266.0 20.6 %collective-permute-start.37 = (bf16[32,9496]{1,0:T(8,128)(2,1)S(1)}, bf16[32,9496]{1,0:T(8,128)(2,1)S(1)}, u32[]{:S(2)}, u32[]{:S(2)}) collective-permute-start(bf16[32,9496]{1,0:T(8,128)(2,1)S(1)} %collective-permute-done.35), channel_id=1, source_target_pairs={{1,0},{2,3},{5,4},{6,7},{9,8},{10,11},{13,12},{14,15},{17,16},{18,... | collective-permute-start | bytes 1823240 | tf_op jit(solution)/shard_map/ppermute | solution.py:126
  267.3 32.5 %collective-permute-start.43 = (bf16[32,9496]{1,0:T(8,128)(2,1)S(1)}, bf16[32,9496]{1,0:T(8,128)(2,1)S(1)}, u32[]{:S(2)}, u32[]{:S(2)}) collective-permute-start(bf16[32,9496]{1,0:T(8,128)(2,1)S(1)} %collective-permute-done.42), channel_id=1, source_target_pairs={{1,0},{2,3},{5,4},{6,7},{9,8},{10,11},{13,12},{14,15},{17,16},{18,... | collective-permute-start | bytes 1823240 | tf_op jit(solution)/shard_map/ppermute | solution.py:126
  268.6 37.8 %collective-permute-start.44 = (bf16[16,9496]{1,0:T(8,128)(2,1)S(1)}, bf16[16,9496]{1,0:T(8,128)(2,1)S(1)}, u32[]{:S(2)}, u32[]{:S(2)}) collective-permute-start(bf16[16,9496]{1,0:T(8,128)(2,1)S(1)} %collective-permute-done.41), channel_id=1, source_target_pairs={{1,0},{2,3},{5,4},{6,7},{9,8},{10,11},{13,12},{14,15},{17,16},{18,... | collective-permute-start | bytes 911624 | tf_op jit(solution)/shard_map/ppermute | solution.py:126
  270.0 41.2 %collective-permute-start.45 = (bf16[16,9496]{1,0:T(8,128)(2,1)S(1)}, bf16[16,9496]{1,0:T(8,128)(2,1)S(1)}, u32[]{:S(2)}, u32[]{:S(2)}) collective-permute-start(bf16[16,9496]{1,0:T(8,128)(2,1)S(1)} %collective-permute-done.40), channel_id=1, source_target_pairs={{1,0},{2,3},{5,4},{6,7},{9,8},{10,11},{13,12},{14,15},{17,16},{18,... | collective-permute-start | bytes 911624 | tf_op jit(solution)/shard_map/ppermute | solution.py:126
  (60 other events, 1108.0 us)

commit v8 on v7

--- a/solution.py
+++ b/solution.py
@@ -9,41 +9,48 @@
 
 LOSS_SCALE = 256.0
 VOCAB_TILE = 1024
+STREAMS = 4
 
 
 def after(value, *others):
     return lax.optimization_barrier((value, *others))[0]
 
 
-def partial_kernel(hidden_ref, head_ref, *out_refs):
-    product = lax.dot_general(
-        hidden_ref[...], head_ref[...], (((1,), (1,)), ((), ())),
-        preferred_element_type=jnp.float32)
+def partial_kernel(hidden_ref, *refs):
+    head_refs, out_refs = refs[:STREAMS], refs[STREAMS:]
     height = out_refs[0].shape[0]
-    for i, out_ref in enumerate(out_refs):
-        out_ref[...] = product[i * height:(i + 1) * height]
+    width = head_refs[0].shape[0]
+    for k, head_ref in enumerate(head_refs):
+        product = lax.dot_general(
+            hidden_ref[...], head_ref[...], (((1,), (1,)), ((), ())),
+            preferred_element_type=jnp.float32)
+        for i, out_ref in enumerate(out_refs):
+            out_ref[:, k * width:(k + 1) * width] = product[i * height:(i + 1) * height]
 
 
 def partial_students(hidden, head_rows, chunk):
     tokens, rows = hidden.shape
     cols = head_rows.shape[0]
-    tile = min(VOCAB_TILE, cols)
+    width = VOCAB_TILE // STREAMS
+    most = pl.cdiv(cols, width) - 1
     count = tokens // chunk
+
+    def stream(k):
+        return pl.BlockSpec((width, rows), lambda i: (jnp.minimum(i * STREAMS + k, most), 0))
+
     return pl.pallas_call(
         partial_kernel,
-        grid=(pl.cdiv(cols, tile),),
-        in_specs=[
-            pl.BlockSpec((tokens, rows), lambda i: (0, 0)),
-            pl.BlockSpec((tile, rows), lambda i: (i, 0)),
-        ],
-        out_specs=[pl.BlockSpec((chunk, tile), lambda i: (0, i))] * count,
+        grid=(pl.cdiv(cols, VOCAB_TILE),),
+        in_specs=[pl.BlockSpec((tokens, rows), lambda i: (0, 0))]
+        + [stream(k) for k in range(STREAMS)],
+        out_specs=[pl.BlockSpec((chunk, VOCAB_TILE), lambda i: (0, i))] * count,
         out_shape=[jax.ShapeDtypeStruct((chunk, cols), jnp.float32)] * count,
         compiler_params=pltpu.CompilerParams(vmem_limit_bytes=16 * 1024 * 1024),
         cost_estimate=pl.CostEstimate(
             flops=2 * tokens * rows * cols,
             bytes_accessed=2 * rows * cols + 4 * tokens * cols,
             transcendentals=0),
-    )(hidden, head_rows)
+    )(hidden, *[head_rows] * STREAMS)
 
 
 def stats_kernel(count, *refs):
@@ -99,7 +106,7 @@
         out_specs=pl.BlockSpec((tile, rows), lambda i: (first + i, 0)),
         out_shape=jax.ShapeDtypeStruct((cols, rows), jnp.float32),
         input_output_aliases={} if out is None else {2: 0},
-        compiler_params=pltpu.CompilerParams(vmem_limit_bytes=24 * 1024 * 1024),
+        compiler_params=pltpu.CompilerParams(vmem_limit_bytes=56 * 1024 * 1024),
         cost_estimate=pl.CostEstimate(
             flops=2 * tokens * rows * tile * (stop - first),
             bytes_accessed=(4 * rows + 2 * tokens) * tile * (stop - first),
@@ -260,14 +267,20 @@
         return jnp.concatenate([p[0] for p in pairs] + [p[1] for p in pairs], axis=0)
 
     features = []
+    early_settled = []
 
     def settle_loss():
         travels["loss"][hops] = tied(travels["loss"][hops])
         settled_loss.append(sum(settle("loss"))[0, 0] / total_tokens)
         tie[:] = [settled_loss[0]]
 
+    def settle_early(p):
+        travels[p][hops] = tied(travels[p][hops])
+        early_settled.append(settle(p))
+        tie[:] = [early_settled[-1][1]]
+
     def early_feature():
-        grads = tied(settled(early_keys))
+        grads = tied(jnp.concatenate([e[0] for e in early_settled] + [e[1] for e in early_settled]))
         features.append((grads, jnp.dot(grads, head_rows, preferred_element_type=jnp.float32)))
         tie[:] = [features[0][1]]
 
@@ -292,10 +305,12 @@
     early_keys, late_keys = list(range(count // 2)), list(range(count // 2, count))
     for p in range(count):
         step = min(p, count - 2)
-        plan(end + 1, 40 + 4 * p, form_grads, p)
-        plan(end + 1, 41 + 4 * p, send_grad, p, 0)
+        plan(end + max(step, 1), 40 + 4 * p, form_grads, p)
+        plan(end + max(step, 1), 41 + 4 * p, send_grad, p, 0)
         for j in range(1, hops):
-            plan(end + 1 + step + j, 30 + j, send_grad, p, j)
+            plan(end + 1 + step + j, 30 + 2 * j, send_grad, p, j)
+        if p in early_keys:
+            plan(end + 1 + step + hops, 33, settle_early, p)
     plan(end + 1, 35, loss)
     for j in range(hops):
         plan(end + 1, 36 if j == 0 else 42 + 4 * min(j - 1, 1), send_loss, j)
@@ -303,9 +318,8 @@
     final = max(slots)
     plan(final, 700, early_feature)
 
-    first_part = jnp.dot(
-        ordered[half_tokens:half_tokens + chunk], head_weight, preferred_element_type=jnp.float32)
-    other_part = [first_part]
+    other_part = list(partial_students(
+        ordered[half_tokens:half_tokens + chunk], head_rows, chunk))
     own_part = None
     for slot in sorted(slots):
         for _, _, call, args in sorted(slots[slot], key=lambda e: e[:2]):

time: 346 us -> 341 us (0.986)
  waiting for transfers between devices: 153 us -> 135 us
  starting transfers between devices: 95.2 us -> 108 us
  matrix products: 12.6 us -> 4.15 us
  Pallas kernels: 30 us -> 38 us
    ppermute x42, waiting for transfers between devices: 139 us -> 121 us  [hop(): return lax.ppermute(value, 'seq', [(last - j, last - j - 1), (j, j + 1)])]
    ppermute x42, starting transfers between devices: 73.2 us -> 86.8 us  [hop(): return lax.ppermute(value, 'seq', [(last - j, last - j - 1), (j, j + 1)])]
    dot_general x1 -> x0, matrix products: 8.45 us -> none  [body(): jnp.dot(ordered[half_tokens:half_tokens + chunk], head_weight, preferred_...]
    pallas_call x1 -> x2, Pallas kernels: 15.1 us -> 20.1 us  [partial_students(): pl.pallas_call(partial_kernel, grid=(pl.cdiv(cols, VOCAB_TILE),), in_spec...]
    unnamed x77 -> x71, local copies, waits for them, and re-layouts: 15.3 us -> 14.9 us
  transfers between devices with their start and end apart: 50 -> 50, of which waited for: 29 -> 28; matrix products, arithmetic and copies ran while one was open for 11% -> 8% of each run, Pallas kernels for 8% -> 11%
where the time goes in v8:
time: 341 us; the launch traced here: 339 us
  waiting for transfers between devices  135 us (40%)
  starting transfers between devices  108 us (32%)
  Pallas kernels  38 us (11%)
  other arithmetic  26.3 us (8%)
  local copies, waits for them, and re-layouts  21.7 us (6%)
  between operations  5.45 us (2%)
  matrix products  4.15 us (1%)
    ppermute x42, waiting for transfers between devices, hop(): return lax.ppermute(value, 'seq', [(last - j, last - j - 1), (j, j + 1)])  121 us
    ppermute x42, starting transfers between devices, hop(): return lax.ppermute(value, 'seq', [(last - j, last - j - 1), (j, j + 1)])  86.8 us
    pallas_call x2, Pallas kernels, partial_students(): pl.pallas_call(partial_kernel, grid=(pl.cdiv(cols, VOCAB_TILE),), in_spec...  20.1 us
    unnamed x71, local copies, waits for them, and re-layouts  14.9 us
    pallas_call x2, Pallas kernels, head_product(): pl.pallas_call(head_kernel, grid=(stop - first,), in_specs=[pl.BlockSpec(...  14.8 us
    add x16, other arithmetic, send(): value = part + tied(moving[i])  10.1 us
    convert_element_type x5, other arithmetic, form_grads(): grads.append((LOSS_SCALE * (jnp.exp(student - student_max[at, None]) / st...  7.32 us
  transfers between devices with their start and end apart: 50, of which 28 were waited for; matrix products, arithmetic and copies ran while one was open for 8% of the time, Pallas kernels for 11%

profile of v8, /device:TPU:2, one launch (start us, length us, event | category | flops | bytes accessed | tf_op | source)
XLA Modules:
  0.0 339.1 jit_solution(17518856727341509099)
XLA Ops:
  19.1 5.0 %shard_map.58 = f32[16,9496]{1,0:T(8,128)S(1)} custom-call(bf16[16,640]{1,0:T(8,128)(2,1)S(1)} %slice.200.hidden_ref, bf16[9496,640]{1,0:T(8,128)(2,1)S(1)} %bitcast.96, bf16[9496,640]{1,0:T(8,128)(2,1)S(1)} %bitcast.97, bf16[9496,640]{1,0:T(8,128)(2,1)S(1)} %bitcast.98, bf16[9496,640]{1,0:T(8,128)(2,1)S(1)} %bitcast.99), custom_call_target="tpu_custom_call" | custom-call | flops 194478080 | bytes 12762624 | tf_op jit(solution)/shard_map/pallas_call | solution.py:41
  24.1 4.7 %collective-permute-start.3 = (f32[16,9496]{1,0:T(8,128)S(1)}, f32[16,9496]{1,0:T(8,128)S(1)}, u32[]{:S(2)}, u32[]{:S(2)}) collective-permute-start(f32[16,9496]{1,0:T(8,128)S(1)} %shard_map.58), channel_id=1, source_target_pairs={{3,2},{0,1},{7,6},{4,5},{11,10},{8,9},{15,14},{12,13},{19,18},{16,... | collective-permute-start | bytes 1823240 | tf_op jit(solution)/shard_map/ppermute | solution.py:133
  28.8 15.1 %shard_map.59 = (f32[16,9496]{1,0:T(8,128)S(1)}, f32[16,9496]{1,0:T(8,128)S(1)}, f32[16,9496]{1,0:T(8,128)S(1)}, f32[16,9496]{1,0:T(8,128)S(1)}, f32[16,9496]{1,...) custom-call(bf16[240,640]{1,0:T(8,128)(2,1)S(1)} %pad_maximum_fusion, ...), custom_call_target="tpu_custom_call" | custom-call | flops 2917171200 | bytes 21271040 | tf_op jit(solution)/shard_map/pallas_call | solution.py:41
  50.5 10.0 %collective-permute-done.5 = f32[16,9496]{1,0:T(8,128)S(1)} collective-permute-done((f32[16,9496]{1,0:T(8,128)S(1)}, f32[16,9496]{1,0:T(8,128)S(1)}, u32[]{:S(2)}, u32[]{:S(2)}) %collective-permute-start.5) | collective-permute-done | bytes 607776 | tf_op jit(solution)/shard_map/ppermute | solution.py:133
  64.1 7.8 %collective-permute-done.9 = f32[16,9496]{1,0:T(8,128)S(1)} collective-permute-done((f32[16,9496]{1,0:T(8,128)S(1)}, f32[16,9496]{1,0:T(8,128)S(1)}, u32[]{:S(2)}, u32[]{:S(2)}) %collective-permute-start.9) | collective-permute-done | bytes 607776 | tf_op jit(solution)/shard_map/ppermute | solution.py:133
  73.7 5.0 %collective-permute-done.7 = f32[16,9496]{1,0:T(8,128)S(1)} collective-permute-done((f32[16,9496]{1,0:T(8,128)S(1)}, f32[16,9496]{1,0:T(8,128)S(1)}, u32[]{:S(2)}, u32[]{:S(2)}) %collective-permute-start.7) | collective-permute-done | bytes 607776 | tf_op jit(solution)/shard_map/ppermute | solution.py:133
  85.6 4.8 %all-to-all-start = ((bf16[8,16,9496]{2,1,0:T(8,128)(2,1)}), bf16[8,16,9496]{2,1,0:T(8,128)(2,1)}, u32[]{:S(2)}, u32[]{:S(2)}) async-start(bf16[8,16,9496]{2,1,0:T(8,128)(2,1)} %bitcast_dynamic-update-slice_fusion), calls=%async_computation | async-start | bytes 4915200 | tf_op jit(solution)/shard_map/all_to_all | solution.py:187
  94.6 4.6 %collective-permute-start.14 = (f32[16,9496]{1,0:T(8,128)}, f32[16,9496]{1,0:T(8,128)S(1)}, u32[]{:S(2)}, u32[]{:S(2)}) collective-permute-start(f32[16,9496]{1,0:T(8,128)} %copy-done.24), channel_id=1, source_target_pairs={{3,2},{0,1},{7,6},{4,5},{11,10},{8,9},{15,14},{12,13},{19,18},{16,... | collective-permute-start | bytes 1823240 | tf_op jit(solution)/shard_map/ppermute | solution.py:133
  99.2 7.8 %collective-permute-done.11 = f32[16,9496]{1,0:T(8,128)S(1)} collective-permute-done((f32[16,9496]{1,0:T(8,128)}, f32[16,9496]{1,0:T(8,128)S(1)}, u32[]{:S(2)}, u32[]{:S(2)}) %collective-permute-start.11) | collective-permute-done | bytes 607776 | tf_op jit(solution)/shard_map/ppermute | solution.py:133
  111.1 7.1 %collective-permute-start.19 = (f32[16,9496]{1,0:T(8,128)}, f32[16,9496]{1,0:T(8,128)}, u32[]{:S(2)}, u32[]{:S(2)}) collective-permute-start(f32[16,9496]{1,0:T(8,128)} %get-tuple-element.125), channel_id=1, source_target_pairs={{3,2},{0,1},{7,6},{4,5},{11,10},{8,9},{15,14},{12,13},{19,18},{16,... | collective-permute-start | bytes 1823240 | tf_op jit(solution)/shard_map/ppermute | solution.py:133
  127.8 5.1 %collective-permute-start.16 = (f32[16,9496]{1,0:T(8,128)}, f32[16,9496]{1,0:T(8,128)}, u32[]{:S(2)}, u32[]{:S(2)}) collective-permute-start(f32[16,9496]{1,0:T(8,128)} %get-tuple-element.129), channel_id=1, source_target_pairs={{3,2},{0,1},{7,6},{4,5},{11,10},{8,9},{15,14},{12,13},{19,18},{16,... | collective-permute-start | bytes 1823240 | tf_op jit(solution)/shard_map/ppermute | solution.py:133
  150.2 6.3 %collective-permute-done.22 = f32[16,9496]{1,0:T(8,128)S(1)} collective-permute-done((f32[16,9496]{1,0:T(8,128)S(1)}, f32[16,9496]{1,0:T(8,128)S(1)}, u32[]{:S(2)}, u32[]{:S(2)}) %collective-permute-start.22) | collective-permute-done | bytes 607776 | tf_op jit(solution)/shard_map/ppermute | solution.py:133
  161.0 8.9 %collective-permute-done.26 = f32[16,9496]{1,0:T(8,128)S(1)} collective-permute-done((f32[16,9496]{1,0:T(8,128)S(1)}, f32[16,9496]{1,0:T(8,128)S(1)}, u32[]{:S(2)}, u32[]{:S(2)}) %collective-permute-start.26) | collective-permute-done | bytes 607776 | tf_op jit(solution)/shard_map/ppermute | solution.py:133
  176.1 6.5 %collective-permute-done.24 = f32[16,9496]{1,0:T(8,128)S(1)} collective-permute-done((f32[16,9496]{1,0:T(8,128)S(1)}, f32[16,9496]{1,0:T(8,128)S(1)}, u32[]{:S(2)}, u32[]{:S(2)}) %collective-permute-start.24) | collective-permute-done | bytes 607776 | tf_op jit(solution)/shard_map/ppermute | solution.py:133
  185.0 10.1 %collective-permute-done.27 = f32[16,9496]{1,0:T(8,128)} collective-permute-done((f32[16,9496]{1,0:T(8,128)}, f32[16,9496]{1,0:T(8,128)}, u32[]{:S(2)}, u32[]{:S(2)}) %collective-permute-start.27) | collective-permute-done | bytes 607776 | tf_op jit(solution)/shard_map/ppermute | solution.py:133
  221.6 5.3 %collective-permute-done.31 = bf16[32,9496]{1,0:T(8,128)(2,1)S(1)} collective-permute-done((bf16[32,9496]{1,0:T(8,128)(2,1)S(1)}, bf16[32,9496]{1,0:T(8,128)(2,1)S(1)}, u32[]{:S(2)}, u32[]{:S(2)}) %collective-permute-start.31) | collective-permute-done | bytes 607776 | tf_op jit(solution)/shard_map/ppermute | solution.py:133
  229.3 6.4 %collective-permute-start.35 = (bf16[32,9496]{1,0:T(8,128)(2,1)S(1)}, bf16[32,9496]{1,0:T(8,128)(2,1)S(1)}, u32[]{:S(2)}, u32[]{:S(2)}) collective-permute-start(bf16[32,9496]{1,0:T(8,128)(2,1)S(1)} %pad_maximum_fusion.6), channel_id=1, source_target_pairs={{3,2},{0,1},{7,6},{4,5},{11,10},{8,9},{15,14},{12,13},{19,18},{16,... | collective-permute-start | bytes 1823240 | tf_op jit(solution)/shard_map/ppermute | solution.py:133
  242.1 6.7 %collective-permute-start.39 = (bf16[16,9496]{1,0:T(8,128)(2,1)S(1)}, bf16[16,9496]{1,0:T(8,128)(2,1)S(1)}, u32[]{:S(2)}, u32[]{:S(2)}) collective-permute-start(bf16[16,9496]{1,0:T(8,128)(2,1)S(1)} %fusion.39), channel_id=1, source_target_pairs={{3,2},{0,1},{7,6},{4,5},{11,10},{8,9},{15,14},{12,13},{19,18},{16,... | collective-permute-start | bytes 911624 | tf_op jit(solution)/shard_map/ppermute | solution.py:133
  251.4 4.6 %collective-permute-start.38 = (bf16[16,9496]{1,0:T(8,128)(2,1)S(1)}, bf16[16,9496]{1,0:T(8,128)(2,1)S(1)}, u32[]{:S(2)}, u32[]{:S(2)}) collective-permute-start(bf16[16,9496]{1,0:T(8,128)(2,1)S(1)} %fusion.40), channel_id=1, source_target_pairs={{3,2},{0,1},{7,6},{4,5},{11,10},{8,9},{15,14},{12,13},{19,18},{16,... | collective-permute-start | bytes 911624 | tf_op jit(solution)/shard_map/ppermute | solution.py:133
  257.3 6.8 %collective-permute-done.34 = bf16[32,9496]{1,0:T(8,128)(2,1)S(1)} collective-permute-done((bf16[32,9496]{1,0:T(8,128)(2,1)S(1)}, bf16[32,9496]{1,0:T(8,128)(2,1)S(1)}, u32[]{:S(2)}, u32[]{:S(2)}) %collective-permute-start.34) | collective-permute-done | bytes 607776 | tf_op jit(solution)/shard_map/ppermute | solution.py:133
  268.1 10.6 %collective-permute-done.37 = bf16[32,9496]{1,0:T(8,128)(2,1)S(1)} collective-permute-done((bf16[32,9496]{1,0:T(8,128)(2,1)S(1)}, bf16[32,9496]{1,0:T(8,128)(2,1)S(1)}, u32[]{:S(2)}, u32[]{:S(2)}) %collective-permute-start.37) | collective-permute-done | bytes 607776 | tf_op jit(solution)/shard_map/ppermute | solution.py:133
  287.3 12.8 %collective-permute-done.43 = bf16[32,9496]{1,0:T(8,128)(2,1)S(1)} collective-permute-done((bf16[32,9496]{1,0:T(8,128)(2,1)S(1)}, bf16[32,9496]{1,0:T(8,128)(2,1)S(1)}, u32[]{:S(2)}, u32[]{:S(2)}) %collective-permute-start.43) | collective-permute-done | bytes 607776 | tf_op jit(solution)/shard_map/ppermute | solution.py:133
  315.6 8.9 %shard_map.62.refs_0_ = f32[9496,640]{1,0:T(8,128)} custom-call(bf16[256,9496]{1,0:T(8,128)(2,1)} %copy-done.27, bf16[256,640]{1,0:T(8,128)(2,1)} %pad_maximum_fusion.9.hidden_ref), custom_call_target="tpu_custom_call" | custom-call | flops 2013265920 | bytes 18874368 | tf_op jit(solution)/shard_map/pallas_call | solution.py:99
  328.4 5.9 %shard_map.63 = f32[9496,640]{1,0:T(8,128)} custom-call(bf16[256,9496]{1,0:T(8,128)(2,1)} %copy-done.27, bf16[256,640]{1,0:T(8,128)(2,1)} %pad_maximum_fusion.9.hidden_ref, f32[9496,640]{1,0:T(8,128)} %shard_map.62.refs_0_), custom_call_target="tpu_custom_call", output_to_operand_aliasing={{}: (2, {})} | custom-call | flops 1342177280 | bytes 12582912 | tf_op jit(solution)/shard_map/pallas_call | solution.py:99
  (236 shorter events, 156.9 us)
Async XLA Ops:
  13.3 37.1 %collective-permute-start.6 = (bf16[8,75968]{1,0:T(8,128)(2,1)}, bf16[8,75968]{1,0:T(8,128)(2,1)S(1)}, u32[]{:S(2)}, u32[]{:S(2)}) collective-permute-start(bf16[8,75968]{1,0:T(8,128)(2,1)} %bitcast.1), channel_id=1, source_target_pairs={{1,0},{2,3},{5,4},{6,7},{9,8},{10,11},{13,12},{14,15},{17,16},{18,... | collective-permute-start | bytes 3646472 | tf_op jit(solution)/shard_map/ppermute | solution.py:155
  24.1 22.1 %collective-permute-start.3 = (f32[16,9496]{1,0:T(8,128)S(1)}, f32[16,9496]{1,0:T(8,128)S(1)}, u32[]{:S(2)}, u32[]{:S(2)}) collective-permute-start(f32[16,9496]{1,0:T(8,128)S(1)} %shard_map.58), channel_id=1, source_target_pairs={{3,2},{0,1},{7,6},{4,5},{11,10},{8,9},{15,14},{12,13},{19,18},{16,... | collective-permute-start | bytes 1823240 | tf_op jit(solution)/shard_map/ppermute | solution.py:133
  47.0 24.9 %collective-permute-start.9 = (f32[16,9496]{1,0:T(8,128)S(1)}, f32[16,9496]{1,0:T(8,128)S(1)}, u32[]{:S(2)}, u32[]{:S(2)}) collective-permute-start(f32[16,9496]{1,0:T(8,128)S(1)} %get-tuple-element.103), channel_id=1, source_target_pairs={{3,2},{0,1},{7,6},{4,5},{11,10},{8,9},{15,14},{12,13},{19,18},{16,... | collective-permute-start | bytes 1823240 | tf_op jit(solution)/shard_map/ppermute | solution.py:133
  61.4 17.3 %collective-permute-start.7 = (f32[16,9496]{1,0:T(8,128)S(1)}, f32[16,9496]{1,0:T(8,128)S(1)}, u32[]{:S(2)}, u32[]{:S(2)}) collective-permute-start(f32[16,9496]{1,0:T(8,128)S(1)} %add.168), channel_id=1, source_target_pairs={{1,0},{2,3},{5,4},{6,7},{9,8},{10,11},{13,12},{14,15},{17,16},{18,... | collective-permute-start | bytes 1823240 | tf_op jit(solution)/shard_map/ppermute | solution.py:133
  85.6 47.3 %all-to-all-start = ((bf16[8,16,9496]{2,1,0:T(8,128)(2,1)}), bf16[8,16,9496]{2,1,0:T(8,128)(2,1)}, u32[]{:S(2)}, u32[]{:S(2)}) async-start(bf16[8,16,9496]{2,1,0:T(8,128)(2,1)} %bitcast_dynamic-update-slice_fusion), calls=%async_computation | async-start | bytes 4915200 | tf_op jit(solution)/shard_map/all_to_all | solution.py:187
  90.4 16.7 %collective-permute-start.11 = (f32[16,9496]{1,0:T(8,128)}, f32[16,9496]{1,0:T(8,128)S(1)}, u32[]{:S(2)}, u32[]{:S(2)}) collective-permute-start(f32[16,9496]{1,0:T(8,128)} %copy-done.26), channel_id=1, source_target_pairs={{3,2},{0,1},{7,6},{4,5},{11,10},{8,9},{15,14},{12,13},{19,18},{16,... | collective-permute-start | bytes 1823240 | tf_op jit(solution)/shard_map/ppermute | solution.py:133
  93.3 17.7 %collective-permute-start.15 = (f32[16,9496]{1,0:T(8,128)}, f32[16,9496]{1,0:T(8,128)S(1)}, u32[]{:S(2)}, u32[]{:S(2)}) collective-permute-start(f32[16,9496]{1,0:T(8,128)} %add.170), channel_id=1, source_target_pairs={{1,0},{2,3},{5,4},{6,7},{9,8},{10,11},{13,12},{14,15},{17,16},{18,... | collective-permute-start | bytes 1823240 | tf_op jit(solution)/shard_map/ppermute | solution.py:133
  94.6 25.6 %collective-permute-start.14 = (f32[16,9496]{1,0:T(8,128)}, f32[16,9496]{1,0:T(8,128)S(1)}, u32[]{:S(2)}, u32[]{:S(2)}) collective-permute-start(f32[16,9496]{1,0:T(8,128)} %copy-done.24), channel_id=1, source_target_pairs={{3,2},{0,1},{7,6},{4,5},{11,10},{8,9},{15,14},{12,13},{19,18},{16,... | collective-permute-start | bytes 1823240 | tf_op jit(solution)/shard_map/ppermute | solution.py:133
  109.0 18.7 %collective-permute-start.12 = (f32[16,9496]{1,0:T(8,128)S(1)}, f32[16,9496]{1,0:T(8,128)S(1)}, u32[]{:S(2)}, u32[]{:S(2)}) collective-permute-start(f32[16,9496]{1,0:T(8,128)S(1)} %add.173), channel_id=1, source_target_pairs={{1,0},{2,3},{5,4},{6,7},{9,8},{10,11},{13,12},{14,15},{17,16},{18,... | collective-permute-start | bytes 1823240 | tf_op jit(solution)/shard_map/ppermute | solution.py:133
  111.1 22.3 %collective-permute-start.19 = (f32[16,9496]{1,0:T(8,128)}, f32[16,9496]{1,0:T(8,128)}, u32[]{:S(2)}, u32[]{:S(2)}) collective-permute-start(f32[16,9496]{1,0:T(8,128)} %get-tuple-element.125), channel_id=1, source_target_pairs={{3,2},{0,1},{7,6},{4,5},{11,10},{8,9},{15,14},{12,13},{19,18},{16,... | collective-permute-start | bytes 1823240 | tf_op jit(solution)/shard_map/ppermute | solution.py:133
  123.6 18.0 %collective-permute-start.17 = (f32[16,9496]{1,0:T(8,128)}, f32[16,9496]{1,0:T(8,128)}, u32[]{:S(2)}, u32[]{:S(2)}) collective-permute-start(f32[16,9496]{1,0:T(8,128)} %add.176), channel_id=1, source_target_pairs={{1,0},{2,3},{5,4},{6,7},{9,8},{10,11},{13,12},{14,15},{17,16},{18,... | collective-permute-start | bytes 1823240 | tf_op jit(solution)/shard_map/ppermute | solution.py:133
  127.8 18.8 %collective-permute-start.16 = (f32[16,9496]{1,0:T(8,128)}, f32[16,9496]{1,0:T(8,128)}, u32[]{:S(2)}, u32[]{:S(2)}) collective-permute-start(f32[16,9496]{1,0:T(8,128)} %get-tuple-element.129), channel_id=1, source_target_pairs={{3,2},{0,1},{7,6},{4,5},{11,10},{8,9},{15,14},{12,13},{19,18},{16,... | collective-permute-start | bytes 1823240 | tf_op jit(solution)/shard_map/ppermute | solution.py:133
  136.7 19.8 %collective-permute-start.22 = (f32[16,9496]{1,0:T(8,128)S(1)}, f32[16,9496]{1,0:T(8,128)S(1)}, u32[]{:S(2)}, u32[]{:S(2)}) collective-permute-start(f32[16,9496]{1,0:T(8,128)S(1)} %add.179), channel_id=1, source_target_pairs={{1,0},{2,3},{5,4},{6,7},{9,8},{10,11},{13,12},{14,15},{17,16},{18,... | collective-permute-start | bytes 1823240 | tf_op jit(solution)/shard_map/ppermute | solution.py:133
  148.7 21.2 %collective-permute-start.26 = (f32[16,9496]{1,0:T(8,128)S(1)}, f32[16,9496]{1,0:T(8,128)S(1)}, u32[]{:S(2)}, u32[]{:S(2)}) collective-permute-start(f32[16,9496]{1,0:T(8,128)S(1)} %add.182), channel_id=1, source_target_pairs={{1,0},{2,3},{5,4},{6,7},{9,8},{10,11},{13,12},{14,15},{17,16},{18,... | collective-permute-start | bytes 1823240 | tf_op jit(solution)/shard_map/ppermute | solution.py:133
  159.7 22.8 %collective-permute-start.24 = (f32[16,9496]{1,0:T(8,128)S(1)}, f32[16,9496]{1,0:T(8,128)S(1)}, u32[]{:S(2)}, u32[]{:S(2)}) collective-permute-start(f32[16,9496]{1,0:T(8,128)S(1)} %add.185), channel_id=1, source_target_pairs={{1,0},{2,3},{5,4},{6,7},{9,8},{10,11},{13,12},{14,15},{17,16},{18,... | collective-permute-start | bytes 1823240 | tf_op jit(solution)/shard_map/ppermute | solution.py:133
  171.0 24.0 %collective-permute-start.27 = (f32[16,9496]{1,0:T(8,128)}, f32[16,9496]{1,0:T(8,128)}, u32[]{:S(2)}, u32[]{:S(2)}) collective-permute-start(f32[16,9496]{1,0:T(8,128)} %add.187), channel_id=1, source_target_pairs={{1,0},{2,3},{5,4},{6,7},{9,8},{10,11},{13,12},{14,15},{17,16},{18,... | collective-permute-start | bytes 1823240 | tf_op jit(solution)/shard_map/ppermute | solution.py:133
  215.7 24.4 %collective-permute-start.33 = (bf16[32,9496]{1,0:T(8,128)(2,1)S(1)}, bf16[32,9496]{1,0:T(8,128)(2,1)S(1)}, u32[]{:S(2)}, u32[]{:S(2)}) collective-permute-start(bf16[32,9496]{1,0:T(8,128)(2,1)S(1)} %pad_maximum_fusion.5), channel_id=1, source_target_pairs={{3,2},{0,1},{7,6},{4,5},{11,10},{8,9},{15,14},{12,13},{19,18},{16,... | collective-permute-start | bytes 1823240 | tf_op jit(solution)/shard_map/ppermute | solution.py:133
  220.3 31.1 %collective-permute-start.30 = (f32[1,1]{1,0:T(1,128)}, f32[1,1]{1,0:T(1,128)}, u32[]{:S(2)}, u32[]{:S(2)}) collective-permute-start(f32[1,1]{1,0:T(1,128)} %collective-permute-done.29), channel_id=1, source_target_pairs={{1,0},{2,3},{5,4},{6,7},{9,8},{10,11},{13,12},{14,15},{17,16},{18,... | collective-permute-start | bytes 20 | tf_op jit(solution)/shard_map/ppermute | solution.py:133
  229.3 28.0 %collective-permute-start.35 = (bf16[32,9496]{1,0:T(8,128)(2,1)S(1)}, bf16[32,9496]{1,0:T(8,128)(2,1)S(1)}, u32[]{:S(2)}, u32[]{:S(2)}) collective-permute-start(bf16[32,9496]{1,0:T(8,128)(2,1)S(1)} %pad_maximum_fusion.6), channel_id=1, source_target_pairs={{3,2},{0,1},{7,6},{4,5},{11,10},{8,9},{15,14},{12,13},{19,18},{16,... | collective-permute-start | bytes 1823240 | tf_op jit(solution)/shard_map/ppermute | solution.py:133
  240.1 24.1 %collective-permute-start.36 = (bf16[32,9496]{1,0:T(8,128)(2,1)S(1)}, bf16[32,9496]{1,0:T(8,128)(2,1)S(1)}, u32[]{:S(2)}, u32[]{:S(2)}) collective-permute-start(bf16[32,9496]{1,0:T(8,128)(2,1)S(1)} %collective-permute-done.33), channel_id=1, source_target_pairs={{2,1},{1,2},{6,5},{5,6},{10,9},{9,10},{14,13},{13,14},{18,17},{17,... | collective-permute-start | bytes 1823240 | tf_op jit(solution)/shard_map/ppermute | solution.py:133
  242.1 24.4 %collective-permute-start.39 = (bf16[16,9496]{1,0:T(8,128)(2,1)S(1)}, bf16[16,9496]{1,0:T(8,128)(2,1)S(1)}, u32[]{:S(2)}, u32[]{:S(2)}) collective-permute-start(bf16[16,9496]{1,0:T(8,128)(2,1)S(1)} %fusion.39), channel_id=1, source_target_pairs={{3,2},{0,1},{7,6},{4,5},{11,10},{8,9},{15,14},{12,13},{19,18},{16,... | collective-permute-start | bytes 911624 | tf_op jit(solution)/shard_map/ppermute | solution.py:133
  278.7 21.4 %collective-permute-start.43 = (bf16[32,9496]{1,0:T(8,128)(2,1)S(1)}, bf16[32,9496]{1,0:T(8,128)(2,1)S(1)}, u32[]{:S(2)}, u32[]{:S(2)}) collective-permute-start(bf16[32,9496]{1,0:T(8,128)(2,1)S(1)} %collective-permute-done.42), channel_id=1, source_target_pairs={{1,0},{2,3},{5,4},{6,7},{9,8},{10,11},{13,12},{14,15},{17,16},{18,... | collective-permute-start | bytes 1823240 | tf_op jit(solution)/shard_map/ppermute | solution.py:133
  280.0 23.4 %collective-permute-start.44 = (bf16[16,9496]{1,0:T(8,128)(2,1)S(1)}, bf16[16,9496]{1,0:T(8,128)(2,1)S(1)}, u32[]{:S(2)}, u32[]{:S(2)}) collective-permute-start(bf16[16,9496]{1,0:T(8,128)(2,1)S(1)} %collective-permute-done.41), channel_id=1, source_target_pairs={{1,0},{2,3},{5,4},{6,7},{9,8},{10,11},{13,12},{14,15},{17,16},{18,... | collective-permute-start | bytes 911624 | tf_op jit(solution)/shard_map/ppermute | solution.py:133
  281.3 25.4 %collective-permute-start.45 = (bf16[16,9496]{1,0:T(8,128)(2,1)S(1)}, bf16[16,9496]{1,0:T(8,128)(2,1)S(1)}, u32[]{:S(2)}, u32[]{:S(2)}) collective-permute-start(bf16[16,9496]{1,0:T(8,128)(2,1)S(1)} %collective-permute-done.40), channel_id=1, source_target_pairs={{1,0},{2,3},{5,4},{6,7},{9,8},{10,11},{13,12},{14,15},{17,16},{18,... | collective-permute-start | bytes 911624 | tf_op jit(solution)/shard_map/ppermute | solution.py:133
  (57 other events, 1112.2 us)

commit v9 on v8

--- a/solution.py
+++ b/solution.py
@@ -28,7 +28,7 @@
             out_ref[:, k * width:(k + 1) * width] = product[i * height:(i + 1) * height]
 
 
-def partial_students(hidden, head_rows, chunk):
+def partial_students(hidden, head_rows, chunk, grant):
     tokens, rows = hidden.shape
     cols = head_rows.shape[0]
     width = VOCAB_TILE // STREAMS
@@ -45,7 +45,7 @@
         + [stream(k) for k in range(STREAMS)],
         out_specs=[pl.BlockSpec((chunk, VOCAB_TILE), lambda i: (0, i))] * count,
         out_shape=[jax.ShapeDtypeStruct((chunk, cols), jnp.float32)] * count,
-        compiler_params=pltpu.CompilerParams(vmem_limit_bytes=16 * 1024 * 1024),
+        compiler_params=pltpu.CompilerParams(vmem_limit_bytes=grant * 1024 * 1024),
         cost_estimate=pl.CostEstimate(
             flops=2 * tokens * rows * cols,
             bytes_accessed=2 * rows * cols + 4 * tokens * cols,
@@ -155,12 +155,17 @@
         lax.ppermute(mine, "seq", [(j, 0), (last - j, last)]) for j in range(1, half)
     ]
 
+    middle = chunks // 2
+    groups = [range(middle), range(middle, chunks)]
     loads = [[i, i + 1] for i in range(0, chunks - 3, 2)] + [[chunks - 2], [chunks - 1]]
+    early_keys = [p for p, members in enumerate(loads) if members[-1] < middle]
+    late_keys = [p for p in range(len(loads)) if p not in early_keys]
     moving = [None] * chunks
     students = [None] * chunks
     targets = []
-    locals_ = []
-    exchanged = []
+    pieces = []
+    locals_ = {0: [], 1: []}
+    exchanged = {}
     travels = {}
     settled_loss = []
     tie = []
@@ -179,12 +184,15 @@
             tie[:] = [value]
         moving[i] = hop(value, j)
 
+    def cut_teacher():
+        rows_held = tied(jnp.concatenate(held, axis=0))
+        pieces.append(jnp.stack(
+            [rows_held[:, v * cols:(v + 1) * cols] for v in range(vocab_count)]))
+        tie[:] = pieces
+
     def exchange_teacher():
-        rows_held = tied(jnp.concatenate(held, axis=0))
-        pieces = jnp.stack([rows_held[:, v * cols:(v + 1) * cols] for v in range(vocab_count)])
-        tie[:] = [pieces]
         targets.append(
-            lax.all_to_all(pieces, "vocab", split_axis=0, concat_axis=0, tiled=True))
+            lax.all_to_all(tied(pieces[0]), "vocab", split_axis=0, concat_axis=0, tiled=True))
 
     def hold_teacher():
         held[:] = lax.optimization_barrier((*held, *tie))[:half]
@@ -193,15 +201,18 @@
     def hold_targets():
         targets[0] = tied(targets[0])
 
-    def local_stats(first, stop):
-        locals_.append(row_stats(
+    def local_stats(g, first, stop):
+        locals_[g].append(row_stats(
             [tied(students[first]), *students[first + 1:stop]], targets[0][first:stop]))
-        tie[:] = [locals_[-1]]
-
-    def exchange_stats():
-        stats = jnp.concatenate(locals_, axis=1)
+        tie[:] = [locals_[g][-1]]
+
+    def exchange_stats(g):
+        stats = jnp.concatenate(locals_[g], axis=1)
         stats = jnp.broadcast_to(stats, (vocab_count, *stats.shape))
-        stats = lax.all_to_all(stats, "vocab", split_axis=0, concat_axis=0, tiled=True)
+        exchanged[g] = lax.all_to_all(stats, "vocab", split_axis=0, concat_axis=0, tiled=True)
+
+    def merge_stats(g):
+        stats = tied(exchanged[g])
         student_max = jnp.max(stats[:, 0], axis=0)
         teacher_max = jnp.max(stats[:, 1], axis=0)
         student_scale = jnp.exp(stats[:, 0] - student_max)
@@ -209,15 +220,16 @@
         student_sum = jnp.sum(stats[:, 2] * student_scale, axis=0)
         teacher_sum = jnp.sum(stats[:, 3] * teacher_scale, axis=0)
         cross = jnp.sum(stats[:, 4] * teacher_scale, axis=0)
-        exchanged.extend(lax.optimization_barrier(
-            (student_max, student_sum, teacher_max, teacher_sum, cross)))
-        tie[:] = [exchanged[0]]
+        exchanged[g] = lax.optimization_barrier(
+            (student_max, student_sum, teacher_max, teacher_sum, cross))
+        tie[:] = [exchanged[g][0]]
 
     def form_grads(p):
-        student_max, student_sum, teacher_max, teacher_sum, _ = exchanged
+        g = 0 if p in early_keys else 1
+        student_max, student_sum, teacher_max, teacher_sum, _ = exchanged[g]
         grads = []
         for i in loads[p]:
-            at = slice(i * chunk, (i + 1) * chunk)
+            at = slice((i - groups[g][0]) * chunk, (i - groups[g][0] + 1) * chunk)
             student = tied(students[i])
             target = targets[0][i].astype(jnp.float32)
             grads.append((
@@ -239,7 +251,8 @@
         tie[:] = [students[i]]
 
     def loss():
-        student_max, student_sum, teacher_max, teacher_sum, cross = exchanged
+        student_max, student_sum, teacher_max, teacher_sum, cross = (
+            jnp.concatenate(both) for both in zip(exchanged[0], exchanged[1]))
         divergence = jnp.sum(
             cross / teacher_sum
             - teacher_max
@@ -296,40 +309,53 @@
         plan(i + hops, 4, sum_up, i)
     end = chunks + hops - 1
     plan(2, 0, hold_teacher)
-    plan(3, 15, exchange_teacher)
+    plan(3, 15, cut_teacher)
+    plan(3, 16, exchange_teacher)
     plan(6, 0, hold_targets)
-    plan(end - 1, 15, local_stats, 0, chunks - 2)
-    plan(end, 15, local_stats, chunks - 2, chunks)
-    plan(end, 16, exchange_stats)
-    count = len(loads)
-    early_keys, late_keys = list(range(count // 2)), list(range(count // 2, count))
-    for p in range(count):
-        step = min(p, count - 2)
-        plan(end + max(step, 1), 40 + 4 * p, form_grads, p)
-        plan(end + max(step, 1), 41 + 4 * p, send_grad, p, 0)
+    early_slot = middle + hops
+    plan(early_slot, 15, local_stats, 0, 0, middle)
+    plan(early_slot, 16, exchange_stats, 0)
+    plan(early_slot + 1, 20, merge_stats, 0)
+    for p in early_keys:
+        plan(early_slot + 1 + p, 40, form_grads, p)
+        plan(early_slot + 1 + p, 41, send_grad, p, 0)
+        for j in range(1, hops):
+            at = early_slot + 1 + p + j
+            if at < end or p == 0:
+                plan(at, (45 if at < end else 90) + j, send_grad, p, j)
+            else:
+                plan(at + 1, 60 + j, send_grad, p, j)
+        plan(max(early_slot + 2 + p + hops, end + 2 + p) + (p > 0), 95, settle_early, p)
+    if middle < chunks - 2:
+        plan(end - 1, 15, local_stats, 1, middle, chunks - 2)
+    plan(end, 15, local_stats, 1, chunks - 2, chunks)
+    plan(end, 16, exchange_stats, 1)
+    plan(end + 1, 20, merge_stats, 1)
+    for p in late_keys:
+        step = min(p - late_keys[0], len(late_keys) - 2)
+        plan(end + 1, 40 + 2 * p, form_grads, p)
+        plan(end + 1, 41 + 2 * p, send_grad, p, 0)
         for j in range(1, hops):
             plan(end + 1 + step + j, 30 + 2 * j, send_grad, p, j)
-        if p in early_keys:
-            plan(end + 1 + step + hops, 33, settle_early, p)
-    plan(end + 1, 35, loss)
+    plan(end + 1, 70, loss)
     for j in range(hops):
-        plan(end + 1, 36 if j == 0 else 42 + 4 * min(j - 1, 1), send_loss, j)
-    plan(end + 3, 90, settle_loss)
+        plan(end + 1 + j + (j > 0), 98, send_loss, j)
+    plan(end + 2 + hops, 99, settle_loss)
     final = max(slots)
     plan(final, 700, early_feature)
 
     other_part = list(partial_students(
-        ordered[half_tokens:half_tokens + chunk], head_rows, chunk))
+        ordered[half_tokens:half_tokens + chunk], head_rows, chunk, 16))
     own_part = None
     for slot in sorted(slots):
         for _, _, call, args in sorted(slots[slot], key=lambda e: e[:2]):
             call(*args)
-        if own_part is None:
-            remaining = tied(jnp.concatenate(
-                [ordered[half_tokens + chunk:], ordered[:half_tokens]]))
-            parts = partial_students(remaining, head_rows, chunk)
-            other_part.extend(parts[:chunks - 1])
-            own_part = parts[chunks - 1:]
+        if slot == -1:
+            other_part.extend(partial_students(
+                tied(ordered[half_tokens + chunk:]), head_rows, chunk, 16))
+            tie[:] = [other_part[1]]
+        if slot == 1:
+            own_part = partial_students(tied(ordered[:half_tokens]), head_rows, chunk, 16)
             tie[:] = [own_part[0]]
 
     mean_divergence = settled_loss[0]

time: 341 us -> 334 us (0.979)
  waiting for transfers between devices: 135 us -> 91.7 us
  starting transfers between devices: 108 us -> 127 us
  other arithmetic: 26.3 us -> 37.8 us
  Pallas kernels: 38 us -> 42.9 us
    ppermute x42, waiting for transfers between devices: 121 us -> 79.6 us  [hop(): return lax.ppermute(value, 'seq', [(last - j, last - j - 1), (j, j + 1)])]
    ppermute x42, starting transfers between devices: 86.8 us -> 101 us  [hop(): return lax.ppermute(value, 'seq', [(last - j, last - j - 1), (j, j + 1)])]
    add x16, other arithmetic: 10.1 us -> 16.8 us  [send(): value = part + tied(moving[i])]
    pallas_call x2 -> x3, Pallas kernels: 20.1 us -> 25 us  [partial_students(): pl.pallas_call(partial_kernel, grid=(pl.cdiv(cols, VOCAB_TILE),), in_spec...]
    all_to_all x1 -> x2, starting transfers between devices: 4.22 us -> 8.42 us  [exchange_stats(): lax.all_to_all(stats, 'vocab', split_axis=0, concat_axis=0, tiled=True)]
    unnamed x71 -> x85, local copies, waits for them, and re-layouts: 14.9 us -> 15.1 us
  transfers between devices with their start and end apart: 50 -> 51, of which waited for: 28 -> 24; matrix products, arithmetic and copies ran while one was open for 8% -> 14% of each run, Pallas kernels for 11% -> 13%
where the time goes in v9:
time: 334 us; the launch traced here: 332 us
  starting transfers between devices  127 us (38%)
  waiting for transfers between devices  91.7 us (27%)
  Pallas kernels  42.9 us (13%)
  other arithmetic  37.8 us (11%)
  local copies, waits for them, and re-layouts  22.6 us (7%)
  between operations  5.54 us (2%)
  matrix products  4.15 us (1%)
    ppermute x42, starting transfers between devices, hop(): return lax.ppermute(value, 'seq', [(last - j, last - j - 1), (j, j + 1)])  101 us
    ppermute x42, waiting for transfers between devices, hop(): return lax.ppermute(value, 'seq', [(last - j, last - j - 1), (j, j + 1)])  79.6 us
    pallas_call x3, Pallas kernels, partial_students(): pl.pallas_call(partial_kernel, grid=(pl.cdiv(cols, VOCAB_TILE),), in_spec...  25 us
    add x16, other arithmetic, send(): value = part + tied(moving[i])  16.8 us
    unnamed x85, local copies, waits for them, and re-layouts  15.1 us
    pallas_call x2, Pallas kernels, head_product(): pl.pallas_call(head_kernel, grid=(stop - first,), in_specs=[pl.BlockSpec(...  14.8 us
    all_to_all x2, starting transfers between devices, exchange_stats(): lax.all_to_all(stats, 'vocab', split_axis=0, concat_axis=0, tiled=True)  8.42 us
    convert_element_type x5, other arithmetic, form_grads(): grads.append((LOSS_SCALE * (jnp.exp(student - student_max[at, None]) / st...  7.45 us
  transfers between devices with their start and end apart: 51, of which 24 were waited for; matrix products, arithmetic and copies ran while one was open for 14% of the time, Pallas kernels for 13%

profile of v9, /device:TPU:2, one launch (start us, length us, event | category | flops | bytes accessed | tf_op | source)
XLA Modules:
  0.0 331.9 jit_solution(5929037237360863804)
XLA Ops:
  14.6 4.4 %copy-done = bf16[640,9496]{0,1:T(8,128)(2,1)S(1)} copy-done((bf16[640,9496]{0,1:T(8,128)(2,1)S(1)}, bf16[640,9496]{0,1:T(8,128)(2,1)}, u32[]{:S(2)}) %copy-start) | copy-done | bytes 12154904
  19.1 5.0 %shard_map.58 = f32[16,9496]{1,0:T(8,128)S(1)} custom-call(bf16[16,640]{1,0:T(8,128)(2,1)S(1)} %slice.220.hidden_ref, bf16[9496,640]{1,0:T(8,128)(2,1)S(1)} %bitcast.134, bf16[9496,640]{1,0:T(8,128)(2,1)S(1)} %bitcast.135, bf16[9496,640]{1,0:T(8,128)(2,1)S(1)} %bitcast.136, bf16[9496,640]{1,0:T(8,128)(2,1)S(1)} %bitcast.137), custom_call_target="tpu_custom_call" | custom-call | flops 194478080 | bytes 12762624 | tf_op jit(solution)/shard_map/pallas_call | solution.py:41
  24.1 4.7 %collective-permute-start.3 = (f32[16,9496]{1,0:T(8,128)S(1)}, f32[16,9496]{1,0:T(8,128)S(1)}, u32[]{:S(2)}, u32[]{:S(2)}) collective-permute-start(f32[16,9496]{1,0:T(8,128)S(1)} %shard_map.58), channel_id=1, source_target_pairs={{3,2},{0,1},{7,6},{4,5},{11,10},{8,9},{15,14},{12,13},{19,18},{16,... | collective-permute-start | bytes 1823240 | tf_op jit(solution)/shard_map/ppermute | solution.py:133
  28.8 9.0 %shard_map.59 = (f32[16,9496]{1,0:T(8,128)S(1)}, f32[16,9496]{1,0:T(8,128)S(1)}, f32[16,9496]{1,0:T(8,128)S(1)}, f32[16,9496]{1,0:T(8,128)S(1)}, f32[16,9496]{1,...) custom-call(bf16[112,640]{1,0:T(8,128)(2,1)S(1)} %slice.219.hidden_ref, bf16[9496,640]{1,0:T(8,128)(2,1)S(1)} %bitcast.138, ...), custom_call_target="tpu_custom_call" | custom-call | flops 1361346560 | bytes 16409088 | tf_op jit(solution)/shard_map/pallas_call | solution.py:41
  43.8 6.6 %collective-permute-start.9 = (f32[16,9496]{1,0:T(8,128)S(1)}, f32[16,9496]{1,0:T(8,128)S(1)}, u32[]{:S(2)}, u32[]{:S(2)}) collective-permute-start(f32[16,9496]{1,0:T(8,128)S(1)} %get-tuple-element.110), channel_id=1, source_target_pairs={{3,2},{0,1},{7,6},{4,5},{11,10},{8,9},{15,14},{12,13},{19,18},{16,... | collective-permute-start | bytes 1823240 | tf_op jit(solution)/shard_map/ppermute | solution.py:133
  50.4 10.9 %shard_map.60 = (f32[16,9496]{1,0:T(8,128)S(1)}, f32[16,9496]{1,0:T(8,128)S(1)}, f32[16,9496]{1,0:T(8,128)S(1)}, f32[16,9496]{1,0:T(8,128)S(1)}, f32[16,9496]{1,...) custom-call(bf16[128,640]{1,0:T(8,128)(2,1)S(1)} %slice.218.hidden_ref, ...), custom_call_target="tpu_custom_call" | custom-call | flops 1555824640 | bytes 17016832 | tf_op jit(solution)/shard_map/pallas_call | solution.py:41
  69.5 7.7 %collective-permute-done.7 = f32[16,9496]{1,0:T(8,128)S(1)} collective-permute-done((f32[16,9496]{1,0:T(8,128)S(1)}, f32[16,9496]{1,0:T(8,128)S(1)}, u32[]{:S(2)}, u32[]{:S(2)}) %collective-permute-start.7) | collective-permute-done | bytes 607776 | tf_op jit(solution)/shard_map/ppermute | solution.py:133
  84.0 4.8 %all-to-all-start = ((bf16[8,16,9496]{2,1,0:T(8,128)(2,1)}), bf16[8,16,9496]{2,1,0:T(8,128)(2,1)}, u32[]{:S(2)}, u32[]{:S(2)}) async-start(bf16[8,16,9496]{2,1,0:T(8,128)(2,1)} %bitcast_dynamic-update-slice_fusion), calls=%async_computation | async-start | bytes 4915200 | tf_op jit(solution)/shard_map/all_to_all | solution.py:195
  92.6 4.6 %collective-permute-start.10 = (f32[16,9496]{1,0:T(8,128)}, f32[16,9496]{1,0:T(8,128)S(1)}, u32[]{:S(2)}, u32[]{:S(2)}) collective-permute-start(f32[16,9496]{1,0:T(8,128)} %copy-done.19), channel_id=1, source_target_pairs={{3,2},{0,1},{7,6},{4,5},{11,10},{8,9},{15,14},{12,13},{19,18},{16,... | collective-permute-start | bytes 1823240 | tf_op jit(solution)/shard_map/ppermute | solution.py:133
  97.3 7.8 %collective-permute-done.13 = f32[16,9496]{1,0:T(8,128)S(1)} collective-permute-done((f32[16,9496]{1,0:T(8,128)}, f32[16,9496]{1,0:T(8,128)S(1)}, u32[]{:S(2)}, u32[]{:S(2)}) %collective-permute-start.13) | collective-permute-done | bytes 607776 | tf_op jit(solution)/shard_map/ppermute | solution.py:133
  109.1 6.5 %collective-permute-start.15 = (f32[16,9496]{1,0:T(8,128)}, f32[16,9496]{1,0:T(8,128)}, u32[]{:S(2)}, u32[]{:S(2)}) collective-permute-start(f32[16,9496]{1,0:T(8,128)} %get-tuple-element.133), channel_id=1, source_target_pairs={{3,2},{0,1},{7,6},{4,5},{11,10},{8,9},{15,14},{12,13},{19,18},{16,... | collective-permute-start | bytes 1823240 | tf_op jit(solution)/shard_map/ppermute | solution.py:133
  125.2 5.7 %collective-permute-start.20 = (f32[16,9496]{1,0:T(8,128)}, f32[16,9496]{1,0:T(8,128)}, u32[]{:S(2)}, u32[]{:S(2)}) collective-permute-start(f32[16,9496]{1,0:T(8,128)} %get-tuple-element.139), channel_id=1, source_target_pairs={{3,2},{0,1},{7,6},{4,5},{11,10},{8,9},{15,14},{12,13},{19,18},{16,... | collective-permute-start | bytes 1823240 | tf_op jit(solution)/shard_map/ppermute | solution.py:133
  140.4 5.6 %collective-permute-start.24 = (f32[16,9496]{1,0:T(8,128)}, f32[16,9496]{1,0:T(8,128)}, u32[]{:S(2)}, u32[]{:S(2)}) collective-permute-start(f32[16,9496]{1,0:T(8,128)} %get-tuple-element.146), channel_id=1, source_target_pairs={{3,2},{0,1},{7,6},{4,5},{11,10},{8,9},{15,14},{12,13},{19,18},{16,... | collective-permute-start | bytes 1823240 | tf_op jit(solution)/shard_map/ppermute | solution.py:133
  155.0 4.2 %all-to-all-start.1 = ((f32[8,1,320]{2,1,0:T(1,128)}), f32[8,1,320]{2,1,0:T(1,128)S(1)}, u32[]{:S(2)}, u32[]{:S(2)}) async-start(f32[8,1,320]{2,1,0:T(1,128)} %reshape.124), calls=%async_computation.1 | async-start | bytes 24576 | tf_op jit(solution)/shard_map/all_to_all | solution.py:212
  173.6 7.9 %collective-permute-start.28 = (bf16[32,9496]{1,0:T(8,128)(2,1)S(1)}, bf16[32,9496]{1,0:T(8,128)(2,1)}, u32[]{:S(2)}, u32[]{:S(2)}) collective-permute-start(bf16[32,9496]{1,0:T(8,128)(2,1)S(1)} %pad_maximum_fusion.4), channel_id=1, source_target_pairs={{3,2},{0,1},{7,6},{4,5},{11,10},{8,9},{15,14},{12,13},{19,18},{16,... | collective-permute-start | bytes 1823240 | tf_op jit(solution)/shard_map/ppermute | solution.py:133
  195.3 6.4 %collective-permute-done.27 = f32[16,9496]{1,0:T(8,128)} collective-permute-done((f32[16,9496]{1,0:T(8,128)}, f32[16,9496]{1,0:T(8,128)}, u32[]{:S(2)}, u32[]{:S(2)}) %collective-permute-start.27) | collective-permute-done | bytes 607776 | tf_op jit(solution)/shard_map/ppermute | solution.py:133
  204.6 4.2 %all-to-all-start.2 = ((f32[8,1,320]{2,1,0:T(1,128)}), f32[8,1,320]{2,1,0:T(1,128)S(1)}, u32[]{:S(2)}, u32[]{:S(2)}) async-start(f32[8,1,320]{2,1,0:T(1,128)} %reshape.126), calls=%async_computation.2 | async-start | bytes 24576 | tf_op jit(solution)/shard_map/all_to_all | solution.py:212
  225.7 8.0 %collective-permute-start.34 = (bf16[16,9496]{1,0:T(8,128)(2,1)S(1)}, bf16[16,9496]{1,0:T(8,128)(2,1)S(1)}, u32[]{:S(2)}, u32[]{:S(2)}) collective-permute-start(bf16[16,9496]{1,0:T(8,128)(2,1)S(1)} %fusion.40), channel_id=1, source_target_pairs={{3,2},{0,1},{7,6},{4,5},{11,10},{8,9},{15,14},{12,13},{19,18},{16,... | collective-permute-start | bytes 911624 | tf_op jit(solution)/shard_map/ppermute | solution.py:133
  240.0 10.4 %collective-permute-done.35 = bf16[16,9496]{1,0:T(8,128)(2,1)S(1)} collective-permute-done((bf16[16,9496]{1,0:T(8,128)(2,1)S(1)}, bf16[16,9496]{1,0:T(8,128)(2,1)S(1)}, u32[]{:S(2)}, u32[]{:S(2)}) %collective-permute-start.35) | collective-permute-done | bytes 303904 | tf_op jit(solution)/shard_map/ppermute | solution.py:133
  251.9 10.5 %collective-permute-start.31 = (f32[1,1]{1,0:T(1,128)}, f32[1,1]{1,0:T(1,128)}, u32[]{:S(2)}, u32[]{:S(2)}) collective-permute-start(f32[1,1]{1,0:T(1,128)} %bitcast.39), channel_id=1, source_target_pairs={{3,2},{0,1},{7,6},{4,5},{11,10},{8,9},{15,14},{12,13},{19,18},{16,... | collective-permute-start | bytes 20 | tf_op jit(solution)/shard_map/ppermute | solution.py:133
  271.5 22.3 %collective-permute-done.42 = f32[1,1]{1,0:T(1,128)} collective-permute-done((f32[1,1]{1,0:T(1,128)}, f32[1,1]{1,0:T(1,128)}, u32[]{:S(2)}, u32[]{:S(2)}) %collective-permute-start.42) | collective-permute-done | bytes 36 | tf_op jit(solution)/shard_map/ppermute | solution.py:133
  303.4 4.2 %all-to-all-start.3 = ((f32[8,64,320]{2,1,0:T(8,128)}), f32[8,64,320]{2,1,0:T(8,128)S(1)}, u32[]{:S(2)}, u32[]{:S(2)}) async-start(f32[8,64,320]{2,1,0:T(8,128)} %bitcast.52), calls=%async_computation.3 | async-start | bytes 1572864 | tf_op jit(solution)/shard_map/all_to_all | solution.py:387
  308.4 8.9 %shard_map.64.refs_0_ = f32[9496,640]{1,0:T(8,128)} custom-call(bf16[256,9496]{1,0:T(8,128)(2,1)} %copy-done.22, bf16[256,640]{1,0:T(8,128)(2,1)} %pad_maximum_fusion.9.hidden_ref), custom_call_target="tpu_custom_call" | custom-call | flops 2013265920 | bytes 18874368 | tf_op jit(solution)/shard_map/pallas_call | solution.py:99
  321.2 5.9 %shard_map.65 = f32[9496,640]{1,0:T(8,128)} custom-call(bf16[256,9496]{1,0:T(8,128)(2,1)} %copy-done.22, bf16[256,640]{1,0:T(8,128)(2,1)} %pad_maximum_fusion.9.hidden_ref, f32[9496,640]{1,0:T(8,128)} %shard_map.64.refs_0_), custom_call_target="tpu_custom_call", output_to_operand_aliasing={{}: (2, {})} | custom-call | flops 1342177280 | bytes 12582912 | tf_op jit(solution)/shard_map/pallas_call | solution.py:99
  (268 shorter events, 150.1 us)
Async XLA Ops:
  13.3 48.1 %collective-permute-start.6 = (bf16[8,75968]{1,0:T(8,128)(2,1)}, bf16[8,75968]{1,0:T(8,128)(2,1)S(1)}, u32[]{:S(2)}, u32[]{:S(2)}) collective-permute-start(bf16[8,75968]{1,0:T(8,128)(2,1)} %bitcast.1), channel_id=1, source_target_pairs={{1,0},{2,3},{5,4},{6,7},{9,8},{10,11},{13,12},{14,15},{17,16},{18,... | collective-permute-start | bytes 3646472 | tf_op jit(solution)/shard_map/ppermute | solution.py:155
  24.1 18.9 %collective-permute-start.3 = (f32[16,9496]{1,0:T(8,128)S(1)}, f32[16,9496]{1,0:T(8,128)S(1)}, u32[]{:S(2)}, u32[]{:S(2)}) collective-permute-start(f32[16,9496]{1,0:T(8,128)S(1)} %shard_map.58), channel_id=1, source_target_pairs={{3,2},{0,1},{7,6},{4,5},{11,10},{8,9},{15,14},{12,13},{19,18},{16,... | collective-permute-start | bytes 1823240 | tf_op jit(solution)/shard_map/ppermute | solution.py:133
  37.9 23.6 %collective-permute-start.5 = (f32[16,9496]{1,0:T(8,128)S(1)}, f32[16,9496]{1,0:T(8,128)S(1)}, u32[]{:S(2)}, u32[]{:S(2)}) collective-permute-start(f32[16,9496]{1,0:T(8,128)S(1)} %get-tuple-element.108), channel_id=1, source_target_pairs={{3,2},{0,1},{7,6},{4,5},{11,10},{8,9},{15,14},{12,13},{19,18},{16,... | collective-permute-start | bytes 1823240 | tf_op jit(solution)/shard_map/ppermute | solution.py:133
  43.1 19.2 %collective-permute-start.4 = (f32[16,9496]{1,0:T(8,128)S(1)}, f32[16,9496]{1,0:T(8,128)S(1)}, u32[]{:S(2)}, u32[]{:S(2)}) collective-permute-start(f32[16,9496]{1,0:T(8,128)S(1)} %add.166), channel_id=1, source_target_pairs={{2,1},{1,2},{6,5},{5,6},{10,9},{9,10},{14,13},{13,14},{18,17},{17,... | collective-permute-start | bytes 1823240 | tf_op jit(solution)/shard_map/ppermute | solution.py:133
  43.8 23.8 %collective-permute-start.9 = (f32[16,9496]{1,0:T(8,128)S(1)}, f32[16,9496]{1,0:T(8,128)S(1)}, u32[]{:S(2)}, u32[]{:S(2)}) collective-permute-start(f32[16,9496]{1,0:T(8,128)S(1)} %get-tuple-element.110), channel_id=1, source_target_pairs={{3,2},{0,1},{7,6},{4,5},{11,10},{8,9},{15,14},{12,13},{19,18},{16,... | collective-permute-start | bytes 1823240 | tf_op jit(solution)/shard_map/ppermute | solution.py:133
  84.0 46.9 %all-to-all-start = ((bf16[8,16,9496]{2,1,0:T(8,128)(2,1)}), bf16[8,16,9496]{2,1,0:T(8,128)(2,1)}, u32[]{:S(2)}, u32[]{:S(2)}) async-start(bf16[8,16,9496]{2,1,0:T(8,128)(2,1)} %bitcast_dynamic-update-slice_fusion), calls=%async_computation | async-start | bytes 4915200 | tf_op jit(solution)/shard_map/all_to_all | solution.py:195
  92.6 25.6 %collective-permute-start.10 = (f32[16,9496]{1,0:T(8,128)}, f32[16,9496]{1,0:T(8,128)S(1)}, u32[]{:S(2)}, u32[]{:S(2)}) collective-permute-start(f32[16,9496]{1,0:T(8,128)} %copy-done.19), channel_id=1, source_target_pairs={{3,2},{0,1},{7,6},{4,5},{11,10},{8,9},{15,14},{12,13},{19,18},{16,... | collective-permute-start | bytes 1823240 | tf_op jit(solution)/shard_map/ppermute | solution.py:133
  109.1 22.3 %collective-permute-start.15 = (f32[16,9496]{1,0:T(8,128)}, f32[16,9496]{1,0:T(8,128)}, u32[]{:S(2)}, u32[]{:S(2)}) collective-permute-start(f32[16,9496]{1,0:T(8,128)} %get-tuple-element.133), channel_id=1, source_target_pairs={{3,2},{0,1},{7,6},{4,5},{11,10},{8,9},{15,14},{12,13},{19,18},{16,... | collective-permute-start | bytes 1823240 | tf_op jit(solution)/shard_map/ppermute | solution.py:133
  125.2 20.8 %collective-permute-start.20 = (f32[16,9496]{1,0:T(8,128)}, f32[16,9496]{1,0:T(8,128)}, u32[]{:S(2)}, u32[]{:S(2)}) collective-permute-start(f32[16,9496]{1,0:T(8,128)} %get-tuple-element.139), channel_id=1, source_target_pairs={{3,2},{0,1},{7,6},{4,5},{11,10},{8,9},{15,14},{12,13},{19,18},{16,... | collective-permute-start | bytes 1823240 | tf_op jit(solution)/shard_map/ppermute | solution.py:133
  140.4 21.3 %collective-permute-start.24 = (f32[16,9496]{1,0:T(8,128)}, f32[16,9496]{1,0:T(8,128)}, u32[]{:S(2)}, u32[]{:S(2)}) collective-permute-start(f32[16,9496]{1,0:T(8,128)} %get-tuple-element.146), channel_id=1, source_target_pairs={{3,2},{0,1},{7,6},{4,5},{11,10},{8,9},{15,14},{12,13},{19,18},{16,... | collective-permute-start | bytes 1823240 | tf_op jit(solution)/shard_map/ppermute | solution.py:133
  150.6 19.5 %collective-permute-start.22 = (f32[16,9496]{1,0:T(8,128)}, f32[16,9496]{1,0:T(8,128)}, u32[]{:S(2)}, u32[]{:S(2)}) collective-permute-start(f32[16,9496]{1,0:T(8,128)} %add.182), channel_id=1, source_target_pairs={{1,0},{2,3},{5,4},{6,7},{9,8},{10,11},{13,12},{14,15},{17,16},{18,... | collective-permute-start | bytes 1823240 | tf_op jit(solution)/shard_map/ppermute | solution.py:133
  167.5 19.6 %collective-permute-start.25 = (f32[16,9496]{1,0:T(8,128)}, f32[16,9496]{1,0:T(8,128)}, u32[]{:S(2)}, u32[]{:S(2)}) collective-permute-start(f32[16,9496]{1,0:T(8,128)} %add.185), channel_id=1, source_target_pairs={{1,0},{2,3},{5,4},{6,7},{9,8},{10,11},{13,12},{14,15},{17,16},{18,... | collective-permute-start | bytes 1823240 | tf_op jit(solution)/shard_map/ppermute | solution.py:133
  173.6 20.1 %collective-permute-start.28 = (bf16[32,9496]{1,0:T(8,128)(2,1)S(1)}, bf16[32,9496]{1,0:T(8,128)(2,1)}, u32[]{:S(2)}, u32[]{:S(2)}) collective-permute-start(bf16[32,9496]{1,0:T(8,128)(2,1)S(1)} %pad_maximum_fusion.4), channel_id=1, source_target_pairs={{3,2},{0,1},{7,6},{4,5},{11,10},{8,9},{15,14},{12,13},{19,18},{16,... | collective-permute-start | bytes 1823240 | tf_op jit(solution)/shard_map/ppermute | solution.py:133
  183.5 18.2 %collective-permute-start.27 = (f32[16,9496]{1,0:T(8,128)}, f32[16,9496]{1,0:T(8,128)}, u32[]{:S(2)}, u32[]{:S(2)}) collective-permute-start(f32[16,9496]{1,0:T(8,128)} %add.187), channel_id=1, source_target_pairs={{1,0},{2,3},{5,4},{6,7},{9,8},{10,11},{13,12},{14,15},{17,16},{18,... | collective-permute-start | bytes 1823240 | tf_op jit(solution)/shard_map/ppermute | solution.py:133
  193.7 19.2 %collective-permute-start.29 = (bf16[32,9496]{1,0:T(8,128)(2,1)}, bf16[32,9496]{1,0:T(8,128)(2,1)}, u32[]{:S(2)}, u32[]{:S(2)}) collective-permute-start(bf16[32,9496]{1,0:T(8,128)(2,1)} %collective-permute-done.28), channel_id=1, source_target_pairs={{2,1},{1,2},{6,5},{5,6},{10,9},{9,10},{14,13},{13,14},{18,17},{17,... | collective-permute-start | bytes 1823240 | tf_op jit(solution)/shard_map/ppermute | solution.py:133
  214.9 22.9 %collective-permute-start.32 = (bf16[32,9496]{1,0:T(8,128)(2,1)S(1)}, bf16[32,9496]{1,0:T(8,128)(2,1)S(1)}, u32[]{:S(2)}, u32[]{:S(2)}) collective-permute-start(bf16[32,9496]{1,0:T(8,128)(2,1)S(1)} %pad_maximum_fusion.6), channel_id=1, source_target_pairs={{3,2},{0,1},{7,6},{4,5},{11,10},{8,9},{15,14},{12,13},{19,18},{16,... | collective-permute-start | bytes 1823240 | tf_op jit(solution)/shard_map/ppermute | solution.py:133
  217.4 22.5 %collective-permute-start.36 = (bf16[32,9496]{1,0:T(8,128)(2,1)}, bf16[32,9496]{1,0:T(8,128)(2,1)S(1)}, u32[]{:S(2)}, u32[]{:S(2)}) collective-permute-start(bf16[32,9496]{1,0:T(8,128)(2,1)} %collective-permute-done.29), channel_id=1, source_target_pairs={{1,0},{2,3},{5,4},{6,7},{9,8},{10,11},{13,12},{14,15},{17,16},{18,... | collective-permute-start | bytes 1823240 | tf_op jit(solution)/shard_map/ppermute | solution.py:133
  225.7 25.3 %collective-permute-start.34 = (bf16[16,9496]{1,0:T(8,128)(2,1)S(1)}, bf16[16,9496]{1,0:T(8,128)(2,1)S(1)}, u32[]{:S(2)}, u32[]{:S(2)}) collective-permute-start(bf16[16,9496]{1,0:T(8,128)(2,1)S(1)} %fusion.40), channel_id=1, source_target_pairs={{3,2},{0,1},{7,6},{4,5},{11,10},{8,9},{15,14},{12,13},{19,18},{16,... | collective-permute-start | bytes 911624 | tf_op jit(solution)/shard_map/ppermute | solution.py:133
  237.9 26.7 %collective-permute-start.33 = (bf16[32,9496]{1,0:T(8,128)(2,1)S(1)}, bf16[32,9496]{1,0:T(8,128)(2,1)S(1)}, u32[]{:S(2)}, u32[]{:S(2)}) collective-permute-start(bf16[32,9496]{1,0:T(8,128)(2,1)S(1)} %collective-permute-done.32), channel_id=1, source_target_pairs={{2,1},{1,2},{6,5},{5,6},{10,9},{9,10},{14,13},{13,14},{18,17},{17,... | collective-permute-start | bytes 1823240 | tf_op jit(solution)/shard_map/ppermute | solution.py:133
  238.6 31.4 %collective-permute-start.39 = (bf16[32,9496]{1,0:T(8,128)(2,1)S(1)}, bf16[32,9496]{1,0:T(8,128)(2,1)S(1)}, u32[]{:S(2)}, u32[]{:S(2)}) collective-permute-start(bf16[32,9496]{1,0:T(8,128)(2,1)S(1)} %collective-permute-done.37), channel_id=1, source_target_pairs={{1,0},{2,3},{5,4},{6,7},{9,8},{10,11},{13,12},{14,15},{17,16},{18,... | collective-permute-start | bytes 1823240 | tf_op jit(solution)/shard_map/ppermute | solution.py:133
  264.6 34.8 %collective-permute-start.43 = (bf16[32,9496]{1,0:T(8,128)(2,1)S(1)}, bf16[32,9496]{1,0:T(8,128)(2,1)S(1)}, u32[]{:S(2)}, u32[]{:S(2)}) collective-permute-start(bf16[32,9496]{1,0:T(8,128)(2,1)S(1)} %collective-permute-done.33), channel_id=1, source_target_pairs={{1,0},{2,3},{5,4},{6,7},{9,8},{10,11},{13,12},{14,15},{17,16},{18,... | collective-permute-start | bytes 1823240 | tf_op jit(solution)/shard_map/ppermute | solution.py:133
  267.4 32.1 %collective-permute-start.44 = (bf16[16,9496]{1,0:T(8,128)(2,1)S(1)}, bf16[16,9496]{1,0:T(8,128)(2,1)S(1)}, u32[]{:S(2)}, u32[]{:S(2)}) collective-permute-start(bf16[16,9496]{1,0:T(8,128)(2,1)S(1)} %collective-permute-done.41), channel_id=1, source_target_pairs={{1,0},{2,3},{5,4},{6,7},{9,8},{10,11},{13,12},{14,15},{17,16},{18,... | collective-permute-start | bytes 911624 | tf_op jit(solution)/shard_map/ppermute | solution.py:133
  268.7 30.8 %collective-permute-start.45 = (bf16[16,9496]{1,0:T(8,128)(2,1)S(1)}, bf16[16,9496]{1,0:T(8,128)(2,1)S(1)}, u32[]{:S(2)}, u32[]{:S(2)}) collective-permute-start(bf16[16,9496]{1,0:T(8,128)(2,1)S(1)} %collective-permute-done.40), channel_id=1, source_target_pairs={{1,0},{2,3},{5,4},{6,7},{9,8},{10,11},{13,12},{14,15},{17,16},{18,... | collective-permute-start | bytes 911624 | tf_op jit(solution)/shard_map/ppermute | solution.py:133
  270.2 23.6 %collective-permute-start.42 = (f32[1,1]{1,0:T(1,128)}, f32[1,1]{1,0:T(1,128)}, u32[]{:S(2)}, u32[]{:S(2)}) collective-permute-start(f32[1,1]{1,0:T(1,128)} %collective-permute-done.38), channel_id=1, source_target_pairs={{1,0},{2,3},{5,4},{6,7},{9,8},{10,11},{13,12},{14,15},{17,16},{18,... | collective-permute-start | bytes 20 | tf_op jit(solution)/shard_map/ppermute | solution.py:133
  (64 other events, 1177.3 us)

commit v10 on v9

--- a/solution.py
+++ b/solution.py
@@ -337,12 +337,12 @@
         plan(end + 1, 41 + 2 * p, send_grad, p, 0)
         for j in range(1, hops):
             plan(end + 1 + step + j, 30 + 2 * j, send_grad, p, j)
-    plan(end + 1, 70, loss)
+    plan(end + 1, 35, loss)
     for j in range(hops):
-        plan(end + 1 + j + (j > 0), 98, send_loss, j)
-    plan(end + 2 + hops, 99, settle_loss)
+        plan(end + 1 + j, 36 if j == 0 else 98, send_loss, j)
     final = max(slots)
     plan(final, 700, early_feature)
+    plan(final, 710, settle_loss)
 
     other_part = list(partial_students(
         ordered[half_tokens:half_tokens + chunk], head_rows, chunk, 16))

time: 334 us -> 327 us (0.979)
  starting transfers between devices: 127 us -> 121 us
    ppermute x42, starting transfers between devices: 101 us -> 95.5 us  [hop(): return lax.ppermute(value, 'seq', [(last - j, last - j - 1), (j, j + 1)])]
  transfers between devices with their start and end apart: 51 -> 51, of which waited for: 24 -> 26; matrix products, arithmetic and copies ran while one was open for 14% -> 14% of each run, Pallas kernels for 13% -> 13%
where the time goes in v10:
time: 327 us; the launch traced here: 324 us
  starting transfers between devices  121 us (37%)
  waiting for transfers between devices  89.8 us (27%)
  Pallas kernels  42.9 us (13%)
  other arithmetic  37.9 us (12%)
  local copies, waits for them, and re-layouts  22.6 us (7%)
  between operations  5.52 us (2%)
  matrix products  4.15 us (1%)
    ppermute x42, starting transfers between devices, hop(): return lax.ppermute(value, 'seq', [(last - j, last - j - 1), (j, j + 1)])  95.5 us
    ppermute x42, waiting for transfers between devices, hop(): return lax.ppermute(value, 'seq', [(last - j, last - j - 1), (j, j + 1)])  77.6 us
    pallas_call x3, Pallas kernels, partial_students(): pl.pallas_call(partial_kernel, grid=(pl.cdiv(cols, VOCAB_TILE),), in_spec...  25 us
    add x16, other arithmetic, send(): value = part + tied(moving[i])  16.8 us
    unnamed x85, local copies, waits for them, and re-layouts  15.1 us
    pallas_call x2, Pallas kernels, head_product(): pl.pallas_call(head_kernel, grid=(stop - first,), in_specs=[pl.BlockSpec(...  14.8 us
    all_to_all x2, starting transfers between devices, exchange_stats(): lax.all_to_all(stats, 'vocab', split_axis=0, concat_axis=0, tiled=True)  8.42 us
    convert_element_type x5, other arithmetic, form_grads(): grads.append((LOSS_SCALE * (jnp.exp(student - student_max[at, None]) / st...  7.53 us
  transfers between devices with their start and end apart: 51, of which 26 were waited for; matrix products, arithmetic and copies ran while one was open for 14% of the time, Pallas kernels for 13%

profile of v10, /device:TPU:2, one launch (start us, length us, event | category | flops | bytes accessed | tf_op | source)
XLA Modules:
  0.0 324.1 jit_solution(2344807564391148421)
XLA Ops:
  14.6 4.4 %copy-done = bf16[640,9496]{0,1:T(8,128)(2,1)S(1)} copy-done((bf16[640,9496]{0,1:T(8,128)(2,1)S(1)}, bf16[640,9496]{0,1:T(8,128)(2,1)}, u32[]{:S(2)}) %copy-start) | copy-done | bytes 12154904
  19.1 5.0 %shard_map.58 = f32[16,9496]{1,0:T(8,128)S(1)} custom-call(bf16[16,640]{1,0:T(8,128)(2,1)S(1)} %slice.220.hidden_ref, bf16[9496,640]{1,0:T(8,128)(2,1)S(1)} %bitcast.134, bf16[9496,640]{1,0:T(8,128)(2,1)S(1)} %bitcast.135, bf16[9496,640]{1,0:T(8,128)(2,1)S(1)} %bitcast.136, bf16[9496,640]{1,0:T(8,128)(2,1)S(1)} %bitcast.137), custom_call_target="tpu_custom_call" | custom-call | flops 194478080 | bytes 12762624 | tf_op jit(solution)/shard_map/pallas_call | solution.py:41
  24.1 4.7 %collective-permute-start.3 = (f32[16,9496]{1,0:T(8,128)S(1)}, f32[16,9496]{1,0:T(8,128)S(1)}, u32[]{:S(2)}, u32[]{:S(2)}) collective-permute-start(f32[16,9496]{1,0:T(8,128)S(1)} %shard_map.58), channel_id=1, source_target_pairs={{3,2},{0,1},{7,6},{4,5},{11,10},{8,9},{15,14},{12,13},{19,18},{16,... | collective-permute-start | bytes 1823240 | tf_op jit(solution)/shard_map/ppermute | solution.py:133
  28.8 9.0 %shard_map.59 = (f32[16,9496]{1,0:T(8,128)S(1)}, f32[16,9496]{1,0:T(8,128)S(1)}, f32[16,9496]{1,0:T(8,128)S(1)}, f32[16,9496]{1,0:T(8,128)S(1)}, f32[16,9496]{1,...) custom-call(bf16[112,640]{1,0:T(8,128)(2,1)S(1)} %slice.219.hidden_ref, bf16[9496,640]{1,0:T(8,128)(2,1)S(1)} %bitcast.138, ...), custom_call_target="tpu_custom_call" | custom-call | flops 1361346560 | bytes 16409088 | tf_op jit(solution)/shard_map/pallas_call | solution.py:41
  43.8 6.6 %collective-permute-start.9 = (f32[16,9496]{1,0:T(8,128)S(1)}, f32[16,9496]{1,0:T(8,128)S(1)}, u32[]{:S(2)}, u32[]{:S(2)}) collective-permute-start(f32[16,9496]{1,0:T(8,128)S(1)} %get-tuple-element.110), channel_id=1, source_target_pairs={{3,2},{0,1},{7,6},{4,5},{11,10},{8,9},{15,14},{12,13},{19,18},{16,... | collective-permute-start | bytes 1823240 | tf_op jit(solution)/shard_map/ppermute | solution.py:133
  50.4 10.9 %shard_map.60 = (f32[16,9496]{1,0:T(8,128)S(1)}, f32[16,9496]{1,0:T(8,128)S(1)}, f32[16,9496]{1,0:T(8,128)S(1)}, f32[16,9496]{1,0:T(8,128)S(1)}, f32[16,9496]{1,...) custom-call(bf16[128,640]{1,0:T(8,128)(2,1)S(1)} %slice.218.hidden_ref, ...), custom_call_target="tpu_custom_call" | custom-call | flops 1555824640 | bytes 17016832 | tf_op jit(solution)/shard_map/pallas_call | solution.py:41
  69.5 7.7 %collective-permute-done.7 = f32[16,9496]{1,0:T(8,128)S(1)} collective-permute-done((f32[16,9496]{1,0:T(8,128)S(1)}, f32[16,9496]{1,0:T(8,128)S(1)}, u32[]{:S(2)}, u32[]{:S(2)}) %collective-permute-start.7) | collective-permute-done | bytes 607776 | tf_op jit(solution)/shard_map/ppermute | solution.py:133
  84.0 4.8 %all-to-all-start = ((bf16[8,16,9496]{2,1,0:T(8,128)(2,1)}), bf16[8,16,9496]{2,1,0:T(8,128)(2,1)}, u32[]{:S(2)}, u32[]{:S(2)}) async-start(bf16[8,16,9496]{2,1,0:T(8,128)(2,1)} %bitcast_dynamic-update-slice_fusion), calls=%async_computation | async-start | bytes 4915200 | tf_op jit(solution)/shard_map/all_to_all | solution.py:195
  92.6 4.6 %collective-permute-start.10 = (f32[16,9496]{1,0:T(8,128)}, f32[16,9496]{1,0:T(8,128)S(1)}, u32[]{:S(2)}, u32[]{:S(2)}) collective-permute-start(f32[16,9496]{1,0:T(8,128)} %copy-done.19), channel_id=1, source_target_pairs={{3,2},{0,1},{7,6},{4,5},{11,10},{8,9},{15,14},{12,13},{19,18},{16,... | collective-permute-start | bytes 1823240 | tf_op jit(solution)/shard_map/ppermute | solution.py:133
  97.3 7.8 %collective-permute-done.13 = f32[16,9496]{1,0:T(8,128)S(1)} collective-permute-done((f32[16,9496]{1,0:T(8,128)}, f32[16,9496]{1,0:T(8,128)S(1)}, u32[]{:S(2)}, u32[]{:S(2)}) %collective-permute-start.13) | collective-permute-done | bytes 607776 | tf_op jit(solution)/shard_map/ppermute | solution.py:133
  109.1 6.5 %collective-permute-start.15 = (f32[16,9496]{1,0:T(8,128)}, f32[16,9496]{1,0:T(8,128)}, u32[]{:S(2)}, u32[]{:S(2)}) collective-permute-start(f32[16,9496]{1,0:T(8,128)} %get-tuple-element.133), channel_id=1, source_target_pairs={{3,2},{0,1},{7,6},{4,5},{11,10},{8,9},{15,14},{12,13},{19,18},{16,... | collective-permute-start | bytes 1823240 | tf_op jit(solution)/shard_map/ppermute | solution.py:133
  125.2 5.7 %collective-permute-start.20 = (f32[16,9496]{1,0:T(8,128)}, f32[16,9496]{1,0:T(8,128)}, u32[]{:S(2)}, u32[]{:S(2)}) collective-permute-start(f32[16,9496]{1,0:T(8,128)} %get-tuple-element.139), channel_id=1, source_target_pairs={{3,2},{0,1},{7,6},{4,5},{11,10},{8,9},{15,14},{12,13},{19,18},{16,... | collective-permute-start | bytes 1823240 | tf_op jit(solution)/shard_map/ppermute | solution.py:133
  140.4 5.6 %collective-permute-start.24 = (f32[16,9496]{1,0:T(8,128)}, f32[16,9496]{1,0:T(8,128)}, u32[]{:S(2)}, u32[]{:S(2)}) collective-permute-start(f32[16,9496]{1,0:T(8,128)} %get-tuple-element.146), channel_id=1, source_target_pairs={{3,2},{0,1},{7,6},{4,5},{11,10},{8,9},{15,14},{12,13},{19,18},{16,... | collective-permute-start | bytes 1823240 | tf_op jit(solution)/shard_map/ppermute | solution.py:133
  155.0 4.2 %all-to-all-start.1 = ((f32[8,1,320]{2,1,0:T(1,128)}), f32[8,1,320]{2,1,0:T(1,128)S(1)}, u32[]{:S(2)}, u32[]{:S(2)}) async-start(f32[8,1,320]{2,1,0:T(1,128)} %reshape.124), calls=%async_computation.1 | async-start | bytes 24576 | tf_op jit(solution)/shard_map/all_to_all | solution.py:212
  173.6 7.9 %collective-permute-start.28 = (bf16[32,9496]{1,0:T(8,128)(2,1)S(1)}, bf16[32,9496]{1,0:T(8,128)(2,1)}, u32[]{:S(2)}, u32[]{:S(2)}) collective-permute-start(bf16[32,9496]{1,0:T(8,128)(2,1)S(1)} %pad_maximum_fusion.4), channel_id=1, source_target_pairs={{3,2},{0,1},{7,6},{4,5},{11,10},{8,9},{15,14},{12,13},{19,18},{16,... | collective-permute-start | bytes 1823240 | tf_op jit(solution)/shard_map/ppermute | solution.py:133
  195.3 6.4 %collective-permute-done.27 = f32[16,9496]{1,0:T(8,128)} collective-permute-done((f32[16,9496]{1,0:T(8,128)}, f32[16,9496]{1,0:T(8,128)}, u32[]{:S(2)}, u32[]{:S(2)}) %collective-permute-start.27) | collective-permute-done | bytes 607776 | tf_op jit(solution)/shard_map/ppermute | solution.py:133
  225.7 8.4 %collective-permute-start.30 = (f32[1,1]{1,0:T(1,128)}, f32[1,1]{1,0:T(1,128)}, u32[]{:S(2)}, u32[]{:S(2)}) collective-permute-start(f32[1,1]{1,0:T(1,128)} %bitcast.39), channel_id=1, source_target_pairs={{3,2},{0,1},{7,6},{4,5},{11,10},{8,9},{15,14},{12,13},{19,18},{16,... | collective-permute-start | bytes 20 | tf_op jit(solution)/shard_map/ppermute | solution.py:133
  237.9 4.4 %collective-permute-start.38 = (bf16[16,9496]{1,0:T(8,128)(2,1)S(1)}, bf16[16,9496]{1,0:T(8,128)(2,1)S(1)}, u32[]{:S(2)}, u32[]{:S(2)}) collective-permute-start(bf16[16,9496]{1,0:T(8,128)(2,1)S(1)} %fusion.39), channel_id=1, source_target_pairs={{3,2},{0,1},{7,6},{4,5},{11,10},{8,9},{15,14},{12,13},{19,18},{16,... | collective-permute-start | bytes 911624 | tf_op jit(solution)/shard_map/ppermute | solution.py:133
  244.4 6.0 %collective-permute-done.38 = bf16[16,9496]{1,0:T(8,128)(2,1)S(1)} collective-permute-done((bf16[16,9496]{1,0:T(8,128)(2,1)S(1)}, bf16[16,9496]{1,0:T(8,128)(2,1)S(1)}, u32[]{:S(2)}, u32[]{:S(2)}) %collective-permute-start.38) | collective-permute-done | bytes 303904 | tf_op jit(solution)/shard_map/ppermute | solution.py:133
  264.4 16.2 %collective-permute-done.39 = f32[1,1]{1,0:T(1,128)} collective-permute-done((f32[1,1]{1,0:T(1,128)}, f32[1,1]{1,0:T(1,128)}, u32[]{:S(2)}, u32[]{:S(2)}) %collective-permute-start.39) | collective-permute-done | bytes 36 | tf_op jit(solution)/shard_map/ppermute | solution.py:133
  282.0 5.3 %collective-permute-done.44 = bf16[16,9496]{1,0:T(8,128)(2,1)S(1)} collective-permute-done((bf16[16,9496]{1,0:T(8,128)(2,1)S(1)}, bf16[16,9496]{1,0:T(8,128)(2,1)S(1)}, u32[]{:S(2)}, u32[]{:S(2)}) %collective-permute-start.44) | collective-permute-done | bytes 303904 | tf_op jit(solution)/shard_map/ppermute | solution.py:133
  287.3 4.4 %collective-permute-done.45 = bf16[16,9496]{1,0:T(8,128)(2,1)S(1)} collective-permute-done((bf16[16,9496]{1,0:T(8,128)(2,1)S(1)}, bf16[16,9496]{1,0:T(8,128)(2,1)S(1)}, u32[]{:S(2)}, u32[]{:S(2)}) %collective-permute-start.45) | collective-permute-done | bytes 303904 | tf_op jit(solution)/shard_map/ppermute | solution.py:133
  300.7 8.9 %shard_map.64.refs_0_ = f32[9496,640]{1,0:T(8,128)} custom-call(bf16[256,9496]{1,0:T(8,128)(2,1)} %copy-done.22, bf16[256,640]{1,0:T(8,128)(2,1)} %pad_maximum_fusion.9.hidden_ref), custom_call_target="tpu_custom_call" | custom-call | flops 2013265920 | bytes 18874368 | tf_op jit(solution)/shard_map/pallas_call | solution.py:99
  313.4 5.9 %shard_map.65 = f32[9496,640]{1,0:T(8,128)} custom-call(bf16[256,9496]{1,0:T(8,128)(2,1)} %copy-done.22, bf16[256,640]{1,0:T(8,128)(2,1)} %pad_maximum_fusion.9.hidden_ref, f32[9496,640]{1,0:T(8,128)} %shard_map.64.refs_0_), custom_call_target="tpu_custom_call", output_to_operand_aliasing={{}: (2, {})} | custom-call | flops 1342177280 | bytes 12582912 | tf_op jit(solution)/shard_map/pallas_call | solution.py:99
  (268 shorter events, 157.3 us)
Async XLA Ops:
  13.3 48.1 %collective-permute-start.6 = (bf16[8,75968]{1,0:T(8,128)(2,1)}, bf16[8,75968]{1,0:T(8,128)(2,1)S(1)}, u32[]{:S(2)}, u32[]{:S(2)}) collective-permute-start(bf16[8,75968]{1,0:T(8,128)(2,1)} %bitcast.1), channel_id=1, source_target_pairs={{1,0},{2,3},{5,4},{6,7},{9,8},{10,11},{13,12},{14,15},{17,16},{18,... | collective-permute-start | bytes 3646472 | tf_op jit(solution)/shard_map/ppermute | solution.py:155
  24.1 18.9 %collective-permute-start.3 = (f32[16,9496]{1,0:T(8,128)S(1)}, f32[16,9496]{1,0:T(8,128)S(1)}, u32[]{:S(2)}, u32[]{:S(2)}) collective-permute-start(f32[16,9496]{1,0:T(8,128)S(1)} %shard_map.58), channel_id=1, source_target_pairs={{3,2},{0,1},{7,6},{4,5},{11,10},{8,9},{15,14},{12,13},{19,18},{16,... | collective-permute-start | bytes 1823240 | tf_op jit(solution)/shard_map/ppermute | solution.py:133
  37.9 23.6 %collective-permute-start.5 = (f32[16,9496]{1,0:T(8,128)S(1)}, f32[16,9496]{1,0:T(8,128)S(1)}, u32[]{:S(2)}, u32[]{:S(2)}) collective-permute-start(f32[16,9496]{1,0:T(8,128)S(1)} %get-tuple-element.108), channel_id=1, source_target_pairs={{3,2},{0,1},{7,6},{4,5},{11,10},{8,9},{15,14},{12,13},{19,18},{16,... | collective-permute-start | bytes 1823240 | tf_op jit(solution)/shard_map/ppermute | solution.py:133
  43.1 19.2 %collective-permute-start.4 = (f32[16,9496]{1,0:T(8,128)S(1)}, f32[16,9496]{1,0:T(8,128)S(1)}, u32[]{:S(2)}, u32[]{:S(2)}) collective-permute-start(f32[16,9496]{1,0:T(8,128)S(1)} %add.166), channel_id=1, source_target_pairs={{2,1},{1,2},{6,5},{5,6},{10,9},{9,10},{14,13},{13,14},{18,17},{17,... | collective-permute-start | bytes 1823240 | tf_op jit(solution)/shard_map/ppermute | solution.py:133
  43.8 23.8 %collective-permute-start.9 = (f32[16,9496]{1,0:T(8,128)S(1)}, f32[16,9496]{1,0:T(8,128)S(1)}, u32[]{:S(2)}, u32[]{:S(2)}) collective-permute-start(f32[16,9496]{1,0:T(8,128)S(1)} %get-tuple-element.110), channel_id=1, source_target_pairs={{3,2},{0,1},{7,6},{4,5},{11,10},{8,9},{15,14},{12,13},{19,18},{16,... | collective-permute-start | bytes 1823240 | tf_op jit(solution)/shard_map/ppermute | solution.py:133
  84.0 46.9 %all-to-all-start = ((bf16[8,16,9496]{2,1,0:T(8,128)(2,1)}), bf16[8,16,9496]{2,1,0:T(8,128)(2,1)}, u32[]{:S(2)}, u32[]{:S(2)}) async-start(bf16[8,16,9496]{2,1,0:T(8,128)(2,1)} %bitcast_dynamic-update-slice_fusion), calls=%async_computation | async-start | bytes 4915200 | tf_op jit(solution)/shard_map/all_to_all | solution.py:195
  92.6 25.6 %collective-permute-start.10 = (f32[16,9496]{1,0:T(8,128)}, f32[16,9496]{1,0:T(8,128)S(1)}, u32[]{:S(2)}, u32[]{:S(2)}) collective-permute-start(f32[16,9496]{1,0:T(8,128)} %copy-done.19), channel_id=1, source_target_pairs={{3,2},{0,1},{7,6},{4,5},{11,10},{8,9},{15,14},{12,13},{19,18},{16,... | collective-permute-start | bytes 1823240 | tf_op jit(solution)/shard_map/ppermute | solution.py:133
  107.1 18.0 %collective-permute-start.16 = (f32[16,9496]{1,0:T(8,128)S(1)}, f32[16,9496]{1,0:T(8,128)S(1)}, u32[]{:S(2)}, u32[]{:S(2)}) collective-permute-start(f32[16,9496]{1,0:T(8,128)S(1)} %add.173), channel_id=1, source_target_pairs={{1,0},{2,3},{5,4},{6,7},{9,8},{10,11},{13,12},{14,15},{17,16},{18,... | collective-permute-start | bytes 1823240 | tf_op jit(solution)/shard_map/ppermute | solution.py:133
  109.1 22.3 %collective-permute-start.15 = (f32[16,9496]{1,0:T(8,128)}, f32[16,9496]{1,0:T(8,128)}, u32[]{:S(2)}, u32[]{:S(2)}) collective-permute-start(f32[16,9496]{1,0:T(8,128)} %get-tuple-element.133), channel_id=1, source_target_pairs={{3,2},{0,1},{7,6},{4,5},{11,10},{8,9},{15,14},{12,13},{19,18},{16,... | collective-permute-start | bytes 1823240 | tf_op jit(solution)/shard_map/ppermute | solution.py:133
  125.2 20.8 %collective-permute-start.20 = (f32[16,9496]{1,0:T(8,128)}, f32[16,9496]{1,0:T(8,128)}, u32[]{:S(2)}, u32[]{:S(2)}) collective-permute-start(f32[16,9496]{1,0:T(8,128)} %get-tuple-element.139), channel_id=1, source_target_pairs={{3,2},{0,1},{7,6},{4,5},{11,10},{8,9},{15,14},{12,13},{19,18},{16,... | collective-permute-start | bytes 1823240 | tf_op jit(solution)/shard_map/ppermute | solution.py:133
  134.8 17.9 %collective-permute-start.18 = (f32[16,9496]{1,0:T(8,128)S(1)}, f32[16,9496]{1,0:T(8,128)S(1)}, u32[]{:S(2)}, u32[]{:S(2)}) collective-permute-start(f32[16,9496]{1,0:T(8,128)S(1)} %add.179), channel_id=1, source_target_pairs={{1,0},{2,3},{5,4},{6,7},{9,8},{10,11},{13,12},{14,15},{17,16},{18,... | collective-permute-start | bytes 1823240 | tf_op jit(solution)/shard_map/ppermute | solution.py:133
  140.4 21.3 %collective-permute-start.24 = (f32[16,9496]{1,0:T(8,128)}, f32[16,9496]{1,0:T(8,128)}, u32[]{:S(2)}, u32[]{:S(2)}) collective-permute-start(f32[16,9496]{1,0:T(8,128)} %get-tuple-element.146), channel_id=1, source_target_pairs={{3,2},{0,1},{7,6},{4,5},{11,10},{8,9},{15,14},{12,13},{19,18},{16,... | collective-permute-start | bytes 1823240 | tf_op jit(solution)/shard_map/ppermute | solution.py:133
  150.6 19.5 %collective-permute-start.22 = (f32[16,9496]{1,0:T(8,128)}, f32[16,9496]{1,0:T(8,128)}, u32[]{:S(2)}, u32[]{:S(2)}) collective-permute-start(f32[16,9496]{1,0:T(8,128)} %add.182), channel_id=1, source_target_pairs={{1,0},{2,3},{5,4},{6,7},{9,8},{10,11},{13,12},{14,15},{17,16},{18,... | collective-permute-start | bytes 1823240 | tf_op jit(solution)/shard_map/ppermute | solution.py:133
  167.5 19.6 %collective-permute-start.25 = (f32[16,9496]{1,0:T(8,128)}, f32[16,9496]{1,0:T(8,128)}, u32[]{:S(2)}, u32[]{:S(2)}) collective-permute-start(f32[16,9496]{1,0:T(8,128)} %add.185), channel_id=1, source_target_pairs={{1,0},{2,3},{5,4},{6,7},{9,8},{10,11},{13,12},{14,15},{17,16},{18,... | collective-permute-start | bytes 1823240 | tf_op jit(solution)/shard_map/ppermute | solution.py:133
  173.6 20.1 %collective-permute-start.28 = (bf16[32,9496]{1,0:T(8,128)(2,1)S(1)}, bf16[32,9496]{1,0:T(8,128)(2,1)}, u32[]{:S(2)}, u32[]{:S(2)}) collective-permute-start(bf16[32,9496]{1,0:T(8,128)(2,1)S(1)} %pad_maximum_fusion.4), channel_id=1, source_target_pairs={{3,2},{0,1},{7,6},{4,5},{11,10},{8,9},{15,14},{12,13},{19,18},{16,... | collective-permute-start | bytes 1823240 | tf_op jit(solution)/shard_map/ppermute | solution.py:133
  183.5 18.2 %collective-permute-start.27 = (f32[16,9496]{1,0:T(8,128)}, f32[16,9496]{1,0:T(8,128)}, u32[]{:S(2)}, u32[]{:S(2)}) collective-permute-start(f32[16,9496]{1,0:T(8,128)} %add.187), channel_id=1, source_target_pairs={{1,0},{2,3},{5,4},{6,7},{9,8},{10,11},{13,12},{14,15},{17,16},{18,... | collective-permute-start | bytes 1823240 | tf_op jit(solution)/shard_map/ppermute | solution.py:133
  193.7 19.2 %collective-permute-start.29 = (bf16[32,9496]{1,0:T(8,128)(2,1)}, bf16[32,9496]{1,0:T(8,128)(2,1)}, u32[]{:S(2)}, u32[]{:S(2)}) collective-permute-start(bf16[32,9496]{1,0:T(8,128)(2,1)} %collective-permute-done.28), channel_id=1, source_target_pairs={{2,1},{1,2},{6,5},{5,6},{10,9},{9,10},{14,13},{13,14},{18,17},{17,... | collective-permute-start | bytes 1823240 | tf_op jit(solution)/shard_map/ppermute | solution.py:133
  215.6 22.2 %collective-permute-start.34 = (bf16[32,9496]{1,0:T(8,128)(2,1)S(1)}, bf16[32,9496]{1,0:T(8,128)(2,1)S(1)}, u32[]{:S(2)}, u32[]{:S(2)}) collective-permute-start(bf16[32,9496]{1,0:T(8,128)(2,1)S(1)} %pad_maximum_fusion.6), channel_id=1, source_target_pairs={{3,2},{0,1},{7,6},{4,5},{11,10},{8,9},{15,14},{12,13},{19,18},{16,... | collective-permute-start | bytes 1823240 | tf_op jit(solution)/shard_map/ppermute | solution.py:133
  218.1 24.9 %collective-permute-start.31 = (bf16[32,9496]{1,0:T(8,128)(2,1)}, bf16[32,9496]{1,0:T(8,128)(2,1)S(1)}, u32[]{:S(2)}, u32[]{:S(2)}) collective-permute-start(bf16[32,9496]{1,0:T(8,128)(2,1)} %collective-permute-done.29), channel_id=1, source_target_pairs={{1,0},{2,3},{5,4},{6,7},{9,8},{10,11},{13,12},{14,15},{17,16},{18,... | collective-permute-start | bytes 1823240 | tf_op jit(solution)/shard_map/ppermute | solution.py:133
  225.7 18.7 %collective-permute-start.30 = (f32[1,1]{1,0:T(1,128)}, f32[1,1]{1,0:T(1,128)}, u32[]{:S(2)}, u32[]{:S(2)}) collective-permute-start(f32[1,1]{1,0:T(1,128)} %bitcast.39), channel_id=1, source_target_pairs={{3,2},{0,1},{7,6},{4,5},{11,10},{8,9},{15,14},{12,13},{19,18},{16,... | collective-permute-start | bytes 20 | tf_op jit(solution)/shard_map/ppermute | solution.py:133
  254.6 27.4 %collective-permute-start.43 = (bf16[32,9496]{1,0:T(8,128)(2,1)S(1)}, bf16[32,9496]{1,0:T(8,128)(2,1)S(1)}, u32[]{:S(2)}, u32[]{:S(2)}) collective-permute-start(bf16[32,9496]{1,0:T(8,128)(2,1)S(1)} %collective-permute-done.36), channel_id=1, source_target_pairs={{1,0},{2,3},{5,4},{6,7},{9,8},{10,11},{13,12},{14,15},{17,16},{18,... | collective-permute-start | bytes 1823240 | tf_op jit(solution)/shard_map/ppermute | solution.py:133
  255.9 24.8 %collective-permute-start.39 = (f32[1,1]{1,0:T(1,128)}, f32[1,1]{1,0:T(1,128)}, u32[]{:S(2)}, u32[]{:S(2)}) collective-permute-start(f32[1,1]{1,0:T(1,128)} %collective-permute-done.35), channel_id=1, source_target_pairs={{1,0},{2,3},{5,4},{6,7},{9,8},{10,11},{13,12},{14,15},{17,16},{18,... | collective-permute-start | bytes 20 | tf_op jit(solution)/shard_map/ppermute | solution.py:133
  257.2 30.1 %collective-permute-start.44 = (bf16[16,9496]{1,0:T(8,128)(2,1)S(1)}, bf16[16,9496]{1,0:T(8,128)(2,1)S(1)}, u32[]{:S(2)}, u32[]{:S(2)}) collective-permute-start(bf16[16,9496]{1,0:T(8,128)(2,1)S(1)} %collective-permute-done.42), channel_id=1, source_target_pairs={{1,0},{2,3},{5,4},{6,7},{9,8},{10,11},{13,12},{14,15},{17,16},{18,... | collective-permute-start | bytes 911624 | tf_op jit(solution)/shard_map/ppermute | solution.py:133
  258.5 33.2 %collective-permute-start.45 = (bf16[16,9496]{1,0:T(8,128)(2,1)S(1)}, bf16[16,9496]{1,0:T(8,128)(2,1)S(1)}, u32[]{:S(2)}, u32[]{:S(2)}) collective-permute-start(bf16[16,9496]{1,0:T(8,128)(2,1)S(1)} %collective-permute-done.41), channel_id=1, source_target_pairs={{1,0},{2,3},{5,4},{6,7},{9,8},{10,11},{13,12},{14,15},{17,16},{18,... | collective-permute-start | bytes 911624 | tf_op jit(solution)/shard_map/ppermute | solution.py:133
  (64 other events, 1098.2 us)
